TPU v7x, 32 devices: a whole 2x2x4 slice. The times are simulated.
32 devices in a mesh: row: 4 (over y, core), col: 8 (over z, x).
Axes of the slice: x: 2, y: 2, z: 4, core: 2. Of those that a mesh axis runs over, the one named last changes fastest.
Arguments:
- features: bfloat16 [32768, 128], P('col', 'row'), may hold values from -6 to 6
- block_codes: int32 [4, 3072], P('row', 'col'), may hold values from 0 to 8191
- block_count: int32 [4, 8], P('row', 'col'), may hold values from 1 to 384, as said below
- block_values: bfloat16 [4, 3072, 4096], P('row', 'col'), may hold values from -0.119628906 to 0.119628906
- weight: bfloat16 [128, 256], replicated, may hold values from -0.5 to 0.5
- bias: float32 [256], replicated, may hold values from -3 to 3
Outputs:
- activated: bfloat16 [32768, 256], P(('row', 'col'))
Inputs may be any that keep to these rules, and one draw needn't show every extreme that they name: `block_count`: every tile's count is at most 384; some tile holds exactly 384 in every draw; counts are skewed, the busiest tile about three times the mean. `block_codes`: A code c names local row block c // 64 and local column block c % 64.
All inputs are finite; a program needn't handle non-finite values.
Results may differ from a plain program's by a relative error of at most 0.0045.
Values may be sent and summed in bfloat16 or wider, within the bound.
No kernel may reach another device: no remote copies, remote signals or barrier semaphores. Data moves between devices by JAX's collectives and lax.ppermute only.
A program may use at most 128 MiB of HBM per device.

v0:
```python
import functools

import jax
import jax.numpy as jnp
from jax import lax
from jax.experimental import pallas as pl
from jax.experimental.pallas import tpu as pltpu
from jax.sharding import PartitionSpec as P

BLK = 64
PAIR = BLK // 2
LANES = 2 * BLK
GROUP = 16
STEPS = 4
UNROLL = 16
SLOT_AT, SOURCE_AT = 13, 7
MIB = 1024 * 1024
SMEM = pl.BlockSpec(memory_space=pltpu.SMEM)
VMEM = pl.BlockSpec(memory_space=pltpu.VMEM)


def log2(size):
    return size.bit_length() - 1


def list_width(slots):
    return -(-(slots + 2 * UNROLL + 8) // LANES) * LANES


def make_lists(orders, per, col_bits, count, codes, words_ref):
    slots, width = codes.shape[1], words_ref.shape[1]
    small = per // 2
    half = small << (len(orders[0][0]) - 1)
    row_block, col_block = codes >> col_bits, codes & ((1 << col_bits) - 1)
    owner = (row_block >> log2(per)) ^ lax.axis_index("col")
    sub = row_block & (per - 1)
    part_rows, rest = sub >> log2(small), sub & (small - 1)
    number = lax.broadcasted_iota(jnp.int32, (1, slots), 1)
    same = lax.broadcasted_iota(jnp.int32, (slots, slots), 0) == lax.broadcasted_iota(jnp.int32, (slots, slots), 1)
    column = lambda row: jnp.sum(jnp.where(same, row, 0.0), axis=1, keepdims=True)
    spot = lax.broadcasted_iota(jnp.int32, (slots, width), 1).astype(jnp.float32)
    lane = lax.broadcasted_iota(jnp.int32, (1, width), 1)
    for f, pair in enumerate(orders):
        places = []
        for order in pair:
            place = jnp.zeros_like(owner)
            for k, bit in enumerate(order):
                place = place | (((owner >> bit) & 1) << (len(order) - 1 - k))
            places.append(place)
        place = (jnp.where(part_rows == 0, places[0], places[1]) << log2(small)) + rest
        keep = place < half
        target = jnp.where(keep, part_rows * half + place, place - half)
        group = jnp.where(number < count, jnp.where(keep, 2, part_rows), 3)
        key = (group * slots + number).astype(jnp.float32)
        word = ((number << SLOT_AT) | (col_block << SOURCE_AT) | target).astype(jnp.float32)
        rank = jnp.sum(jnp.where(key < column(key), 1.0, 0.0), axis=1, keepdims=True)
        words = jnp.sum(jnp.where(rank == spot, column(word), 0.0), axis=0, keepdims=True).astype(jnp.int32)
        for k in range(4):
            before = jnp.sum(jnp.where(group < k, 1.0, 0.0), axis=1, keepdims=True).astype(jnp.int32)
            words = jnp.where(lane == width - 8 + k, before, words)
        words_ref[f : f + 1, :] = words


def relayout_kernel(orders, per, col_bits, count_ref, codes_hbm, values_hbm, out_ref, words_ref, codes, held, scratch, arrived, codes_arrived):
    codes_copy = pltpu.make_async_copy(codes_hbm, codes, codes_arrived)
    codes_copy.start()
    step = values_hbm.shape[0] // STEPS
    copies = []
    for k in range(STEPS):
        rows = pl.ds(k * step, step)
        copies.append(pltpu.make_async_copy(values_hbm.at[rows], held.at[rows], arrived.at[k]))
        copies[k].start()
    codes_copy.wait()
    make_lists(orders, per, col_bits, count_ref[0, 0], codes[...], words_ref)

    def one(g, carry):
        slots = pl.ds(pl.multiple_of(g * GROUP, GROUP), GROUP)
        base = pl.multiple_of(g * (GROUP * PAIR), GROUP * PAIR)
        for p in range(PAIR):
            scratch[pl.ds(base + p * GROUP, GROUP), :] = held[slots, p * LANES : (p + 1) * LANES].astype(jnp.float32)
        for s in range(GROUP):
            rows = scratch[pl.ds(base + s, PAIR, stride=GROUP), :]
            out_ref[pl.ds(base + s * PAIR, PAIR), :] = rows.astype(out_ref.dtype)
        return carry

    groups = step // GROUP
    for k in range(STEPS):
        copies[k].wait()
        lax.fori_loop(k * groups, (k + 1) * groups, one, 0, unroll=2)


def relayout(orders, per, col_bits, count, codes, values):
    slots = values.shape[0]
    return pl.pallas_call(
        functools.partial(relayout_kernel, orders, per, col_bits),
        in_specs=[SMEM] + [pl.BlockSpec(memory_space=pltpu.HBM)] * 2,
        out_specs=(VMEM, VMEM),
        out_shape=(
            jax.ShapeDtypeStruct((slots * PAIR, LANES), values.dtype),
            jax.ShapeDtypeStruct((2, list_width(slots)), jnp.int32),
        ),
        scratch_shapes=[
            pltpu.VMEM(codes.shape, codes.dtype),
            pltpu.VMEM(values.shape, values.dtype),
            pltpu.VMEM((slots * PAIR, LANES), jnp.float32),
            pltpu.SemaphoreType.DMA((STEPS,)),
            pltpu.SemaphoreType.DMA,
        ],
        cost_estimate=pl.CostEstimate(flops=0, bytes_accessed=4 * slots * BLK * BLK, transcendentals=0),
        compiler_params=pltpu.CompilerParams(vmem_limit_bytes=48 * MIB),
        name="relayout",
    )(count, codes, values)


def table_kernel(*refs):
    parts, table = refs[:-1], refs[-1]

    def build(q, carry):
        at = pl.ds(pl.multiple_of(q * LANES, LANES), LANES)
        x = [part[:, at].astype(jnp.float32) for part in parts]
        table[at, :] = jnp.concatenate(x + x, axis=0).T.astype(table.dtype)
        return carry

    lax.fori_loop(0, table.shape[0] // LANES, build, 0, unroll=4)


def make_table(parts):
    nodes = parts[0].shape[1]
    return pl.pallas_call(
        table_kernel,
        in_specs=[VMEM] * len(parts),
        out_specs=VMEM,
        out_shape=jax.ShapeDtypeStruct((nodes, LANES), jnp.bfloat16),
        compiler_params=pltpu.CompilerParams(vmem_limit_bytes=4 * MIB),
        cost_estimate=pl.CostEstimate(flops=0, bytes_accessed=nodes * LANES * 3, transcendentals=0),
        name="table",
    )(*parts)


def product_kernel(trash, feature_half, part, words_ref, blocks_ref, table_ref, *outs):
    pending, acc = outs[-1], outs[-2]
    bounds = words_ref.shape[1] - 8 + part
    start, end = words_ref[feature_half, bounds], words_ref[feature_half, bounds + 1]
    low = lax.broadcasted_iota(jnp.int32, (BLK, LANES), 1) < BLK
    acc[...] = jnp.zeros_like(acc)

    def step(g, carry):
        first = start + g * UNROLL
        products = []
        for u in range(UNROLL):
            word = words_ref[feature_half, first + u]
            block = blocks_ref[pl.ds(pl.multiple_of((word >> SLOT_AT) * PAIR, PAIR), PAIR), :]
            source = (word >> SOURCE_AT) & ((1 << (SLOT_AT - SOURCE_AT)) - 1)
            right = table_ref[pl.ds(pl.multiple_of(source * BLK, BLK), BLK), :]
            zero = jnp.zeros_like(right)
            right = jnp.concatenate([jnp.where(low, right, zero), jnp.where(low, zero, right)], axis=0)
            products.append(jnp.dot(block, right, preferred_element_type=jnp.float32))
        for u in range(UNROLL):
            i = first - UNROLL + u
            word = words_ref[feature_half, jnp.maximum(i, 0)]
            place = jnp.where((i >= start) & (i < end), word & ((1 << SOURCE_AT) - 1), trash)
            rows = pl.ds(pl.multiple_of(place * PAIR, PAIR), PAIR)
            acc[rows, :] = acc[rows, :] + pending[u * PAIR : (u + 1) * PAIR, :]
        for u in range(UNROLL):
            pending[u * PAIR : (u + 1) * PAIR, :] = products[u]
        return carry

    lax.fori_loop(0, (end - start + (UNROLL - 1)) // UNROLL + 1, step, 0)
    if len(outs) > 2:
        outs[0][...] = acc[: trash * PAIR, :].astype(outs[0].dtype)


def product(feature_half, part, words, blocks, table, trash, sent):
    full = jax.ShapeDtypeStruct(((trash + 1) * PAIR, LANES), jnp.float32)
    out = jax.ShapeDtypeStruct((trash * PAIR, LANES), jnp.bfloat16) if sent else full
    sums = [pltpu.VMEM(full.shape, full.dtype)] if sent else []
    return pl.pallas_call(
        functools.partial(product_kernel, trash, feature_half, part),
        in_specs=[SMEM, VMEM, VMEM],
        out_specs=VMEM,
        out_shape=out,
        scratch_shapes=sums + [pltpu.VMEM((UNROLL * PAIR, LANES), jnp.float32)],
        compiler_params=pltpu.CompilerParams(vmem_limit_bytes=8 * MIB),
        cost_estimate=pl.CostEstimate(flops=8 * trash * BLK * LANES * LANES, bytes_accessed=MIB, transcendentals=0),
        name="product_send" if sent else "product_keep",
    )(words, blocks, table)


def add_kernel(keep_ref, got_ref, next_ref, send_ref):
    half = next_ref.shape[0]
    next_ref[...] = keep_ref[:half, :] + got_ref[:half, :].astype(jnp.float32)
    send_ref[...] = (keep_ref[half:, :] + got_ref[half:, :].astype(jnp.float32)).astype(send_ref.dtype)


def add_halves(keep, which, got):
    rows, lanes = got.shape
    block = lambda n, i: pl.BlockSpec((n, lanes), lambda _: (i, 0))
    return pl.pallas_call(
        add_kernel,
        grid=(1,),
        in_specs=[block(rows, which), block(rows, 0)],
        out_specs=(block(rows // 2, 0), block(rows // 2, 0)),
        out_shape=(
            jax.ShapeDtypeStruct((rows // 2, lanes), jnp.float32),
            jax.ShapeDtypeStruct((rows // 2, lanes), jnp.bfloat16),
        ),
        compiler_params=pltpu.CompilerParams(vmem_limit_bytes=4 * MIB),
        cost_estimate=pl.CostEstimate(flops=rows * lanes, bytes_accessed=rows * lanes * 6, transcendentals=0),
        name="add",
    )(keep, got)


def layer_kernel(index, *refs):
    sums, (weight_ref, bias_ref, out_ref, wide, left, right) = refs[:8], refs[8:]
    r = lax.axis_index("row")
    wide[...] = weight_ref[...].astype(jnp.float32)
    size = wide.shape[0] // (2 * len(index[0]))
    halves = []
    for pieces in index:
        rows = [wide[pl.ds(pl.multiple_of((r ^ i) * size, size), size), :] for i in pieces]
        halves.append(jnp.concatenate(rows, axis=0).astype(jnp.bfloat16))
    zero = jnp.zeros_like(halves[0])
    even = jnp.concatenate([halves[0], zero, halves[1], zero], axis=0)
    odd = jnp.concatenate([zero, halves[0], zero, halves[1]], axis=0)
    rows = sums[0].shape[0]
    for k in range(2):
        aggregated = []
        for f in range(2):
            keep, got = sums[4 * f + 2 * k], sums[4 * f + 2 * k + 1]
            aggregated.append((keep[...] + got[...].astype(jnp.float32)).astype(jnp.bfloat16))
        both = jnp.concatenate(aggregated, axis=1)
        for h, w in enumerate((even, odd)):
            hidden = jnp.dot(both, w, preferred_element_type=jnp.float32) + bias_ref[...]
            hidden = jnp.maximum(hidden, 0.0)
            left[pl.ds(2 * rows * k + h, rows, stride=2), :] = hidden[:, :LANES]
            right[pl.ds(2 * rows * k + h, rows, stride=2), :] = hidden[:, LANES:]
    out_ref[:, :LANES] = left[...].astype(out_ref.dtype)
    out_ref[:, LANES:] = right[...].astype(out_ref.dtype)


def layer(index, sums, weight, bias):
    rows = 4 * sums[0].shape[0]
    return pl.pallas_call(
        functools.partial(layer_kernel, index),
        out_shape=jax.ShapeDtypeStruct((rows, weight.shape[1]), jnp.bfloat16),
        scratch_shapes=[pltpu.VMEM(weight.shape, jnp.float32)] + [pltpu.VMEM((rows, LANES), jnp.float32)] * 2,
        compiler_params=pltpu.CompilerParams(vmem_limit_bytes=8 * MIB),
        name="layer",
    )(*sums, weight, bias)


def exchange(x, axis, size, bit):
    return lax.ppermute(x, axis, [(i, i ^ (1 << bit)) for i in range(size)])


def shards(n_row, n_col, features, block_codes, block_count, block_values, weight, bias):
    top, col_axis_bits = log2(n_row) - 1, list(range(log2(n_col)))
    col_blocks = features.shape[0] // BLK
    row_total = col_blocks * n_col // n_row
    per = row_total // n_col
    half = row_total // 4

    z_first, x_first = col_axis_bits[1:] + col_axis_bits[:1], col_axis_bits
    orders = ((x_first, z_first), (x_first, z_first))

    def spread(pieces, index):
        for bit in range(top):
            pieces = pieces + [exchange(p, "row", n_row, bit) for p in pieces]
            index = index + [i ^ (1 << bit) for i in index]
        return pieces, index

    mine = features.T
    other = exchange(mine, "row", n_row, top)
    near, near_index = spread([mine], [0])
    blocks, words = relayout(orders, per, log2(col_blocks), block_count, block_codes, block_values[0])

    def products(f, table):
        sends = [product(f, k, words, blocks, table, half, True) for k in range(2)]
        kept = product(f, 2, words, blocks, table, 2 * half, False)
        return sends, [(kept, 0), (kept, 1)]

    table = make_table(near)
    first = product(0, 0, words, blocks, table, half, True)
    other, first = lax.optimization_barrier((other, first))
    far, far_index = spread([other], [1 << top])
    sends = [first, product(0, 1, words, blocks, table, half, True)]
    kept = product(0, 2, words, blocks, table, 2 * half, False)
    keeps = [(kept, 0), (kept, 1)]
    more_sends, more_keeps = products(1, make_table(far))
    sends, keeps = sends + more_sends, keeps + more_keeps

    chunk_orders = orders[0] + orders[1]
    for k in range(len(col_axis_bits)):
        for i in range(4):
            got = exchange(sends[i], "col", n_col, chunk_orders[i][k])
            if k < len(col_axis_bits) - 1:
                total, sends[i] = add_halves(*keeps[i], got)
                keeps[i] = (total, 0)
            else:
                keeps[i], sends[i] = keeps[i][0], got
    sums = [x for i in range(4) for x in (keeps[i], sends[i])]
    return layer((near_index, far_index), sums, weight, bias[None, :])


def solution(mesh):
    in_specs = (P("col", "row"), P("row", "col"), P("row", "col"), P("row", "col", None), P(), P())
    out_specs = P(("row", "col"), None)
    body = functools.partial(shards, mesh.shape["row"], mesh.shape["col"])
    return jax.shard_map(body, mesh=mesh, in_specs=in_specs, out_specs=out_specs, check_vma=False)
```

profile of v0, /device:TPU:0, one launch (start us, length us, event | category | flops | bytes accessed | tf_op | source)
XLA Modules:
  0.0 49.9 jit_solution(4816589781455575598)
XLA Ops:
  0.0 0.5 collective-permute-start
  0.5 2.6 %collective-permute-start.1 = (bf16[32,4096]{1,0:T(8,128)(2,1)}, bf16[32,4096]{1,0:T(8,128)(2,1)S(1)}, u32[]{:S(2)}, u32[]{:S(2)}) collective-permute-start(bf16[32,4096]{1,0:T(8,128)(2,1)} %bitcast.4), channel_id=1, source_target_pairs={{0,16},{8,24},{16,0},{24,8},{1,17},{9,25},{17,1},{25,9},{2,18},{10... | collective-permute-start | bytes 786440 | tf_op jit(solution)/shard_map/ppermute | solution.py:253
  3.7 0.7 %copy-done.2 = s32[1,384]{1,0:T(1,128)S(1)} copy-done((s32[1,384]{1,0:T(1,128)S(1)}, s32[1,384]{1,0:T(1,128)}, u32[]{:S(2)}) %copy-start.2) | copy-done | bytes 1560
  4.4 3.4 %relayout.1 = (bf16[12288,128]{1,0:T(8,128)(2,1)S(1)}, s32[2,512]{1,0:T(2,128)S(1)}) custom-call(s32[1,1]{1,0:T(1,128)S(6)} %copy.7.count_ref, s32[1,384]{1,0:T(1,128)S(1)} %copy-done.2, bf16[384,4096]{1,0:T(8,128)(2,1)} %bitcast.7), custom_call_target="tpu_custom_call" | custom-call | bytes 6291456 | tf_op jit(solution)/shard_map/relayout/pallas_call | solution.py:94
  7.8 0.9 %table.2.table_ref = bf16[4096,128]{1,0:T(8,128)(2,1)S(1)} custom-call(bf16[32,4096]{1,0:T(8,128)(2,1)S(1)} %bitcast.5, bf16[32,4096]{1,0:T(8,128)(2,1)S(1)} %collective-permute-done.refs_1_), custom_call_target="tpu_custom_call" | custom-call | bytes 1572864 | tf_op jit(solution)/shard_map/table/pallas_call | solution.py:129
  8.7 1.7 %product_send.4 = bf16[1024,128]{1,0:T(8,128)(2,1)S(1)} custom-call(s32[2,512]{1,0:T(2,128)S(1)} %get-tuple-element.25.words_ref, bf16[12288,128]{1,0:T(8,128)(2,1)S(1)} %get-tuple-element.26.blocks_ref, bf16[4096,128]{1,0:T(8,128)(2,1)S(1)} %table.2.table_ref), custom_call_target="tpu_custom_call" | custom-call | flops 268435456 | bytes 1048576 | tf_op jit(solution)/shard_map/product_send/pallas_call | solution.py:177
  10.4 0.1 collective-permute-start.8
  10.5 1.4 %collective-permute-start.2 = (bf16[1024,128]{1,0:T(8,128)(2,1)S(1)}, bf16[1024,128]{1,0:T(8,128)(2,1)S(1)}, u32[]{:S(2)}, u32[]{:S(2)}) collective-permute-start(bf16[1024,128]{1,0:T(8,128)(2,1)S(1)} %product_send.4), channel_id=1, source_target_pairs={{0,1},{1,0},{2,3},{3,2},{4,5},{5,4},{6,7},{7,6},{8,9},{9,8},{10,11... | collective-permute-start | bytes 786440 | tf_op jit(solution)/shard_map/ppermute | solution.py:253
  11.9 1.7 %product_send.5 = bf16[1024,128]{1,0:T(8,128)(2,1)S(1)} custom-call(s32[2,512]{1,0:T(2,128)S(1)} %get-tuple-element.25.words_ref, bf16[12288,128]{1,0:T(8,128)(2,1)S(1)} %get-tuple-element.26.blocks_ref, bf16[4096,128]{1,0:T(8,128)(2,1)S(1)} %table.2.table_ref), custom_call_target="tpu_custom_call" | custom-call | flops 268435456 | bytes 1048576 | tf_op jit(solution)/shard_map/product_send/pallas_call | solution.py:177
  13.6 1.2 %collective-permute-start.5 = (bf16[1024,128]{1,0:T(8,128)(2,1)S(1)}, bf16[1024,128]{1,0:T(8,128)(2,1)S(1)}, u32[]{:S(2)}, u32[]{:S(2)}) collective-permute-start(bf16[1024,128]{1,0:T(8,128)(2,1)S(1)} %product_send.5), channel_id=1, source_target_pairs={{0,2},{1,3},{2,0},{3,1},{4,6},{5,7},{6,4},{7,5},{8,10},{9,11},{10,... | collective-permute-start | bytes 786440 | tf_op jit(solution)/shard_map/ppermute | solution.py:253
  14.7 0.9 %table.3.table_ref = bf16[4096,128]{1,0:T(8,128)(2,1)S(1)} custom-call(bf16[32,4096]{1,0:T(8,128)(2,1)S(1)} %collective-permute-done.1.refs_0_, bf16[32,4096]{1,0:T(8,128)(2,1)S(1)} %collective-permute-done.8.refs_1_), custom_call_target="tpu_custom_call" | custom-call | bytes 1572864 | tf_op jit(solution)/shard_map/table/pallas_call | solution.py:129
  15.7 1.7 %product_send.6 = bf16[1024,128]{1,0:T(8,128)(2,1)S(1)} custom-call(s32[2,512]{1,0:T(2,128)S(1)} %get-tuple-element.25.words_ref, bf16[12288,128]{1,0:T(8,128)(2,1)S(1)} %get-tuple-element.26.blocks_ref, bf16[4096,128]{1,0:T(8,128)(2,1)S(1)} %table.3.table_ref), custom_call_target="tpu_custom_call" | custom-call | flops 268435456 | bytes 1048576 | tf_op jit(solution)/shard_map/product_send/pallas_call | solution.py:177
  17.4 0.6 %collective-permute-start.9 = (bf16[1024,128]{1,0:T(8,128)(2,1)S(1)}, bf16[1024,128]{1,0:T(8,128)(2,1)S(1)}, u32[]{:S(2)}, u32[]{:S(2)}) collective-permute-start(bf16[1024,128]{1,0:T(8,128)(2,1)S(1)} %product_send.6), channel_id=1, source_target_pairs={{0,1},{1,0},{2,3},{3,2},{4,5},{5,4},{6,7},{7,6},{8,9},{9,8},{10,11... | collective-permute-start | bytes 786440 | tf_op jit(solution)/shard_map/ppermute | solution.py:253
  18.0 1.7 %product_send.7 = bf16[1024,128]{1,0:T(8,128)(2,1)S(1)} custom-call(s32[2,512]{1,0:T(2,128)S(1)} %get-tuple-element.25.words_ref, bf16[12288,128]{1,0:T(8,128)(2,1)S(1)} %get-tuple-element.26.blocks_ref, bf16[4096,128]{1,0:T(8,128)(2,1)S(1)} %table.3.table_ref), custom_call_target="tpu_custom_call" | custom-call | flops 268435456 | bytes 1048576 | tf_op jit(solution)/shard_map/product_send/pallas_call | solution.py:177
  19.7 0.1 collective-permute-start.12
  19.8 2.5 %product_keep.2.keep_ref = f32[2080,128]{1,0:T(8,128)S(1)} custom-call(s32[2,512]{1,0:T(2,128)S(1)} %get-tuple-element.25.words_ref, bf16[12288,128]{1,0:T(8,128)(2,1)S(1)} %get-tuple-element.26.blocks_ref, bf16[4096,128]{1,0:T(8,128)(2,1)S(1)} %table.2.table_ref), custom_call_target="tpu_custom_call" | custom-call | flops 536870912 | bytes 1048576 | tf_op jit(solution)/shard_map/product_keep/pallas_call | solution.py:177
  22.3 0.8 %collective-permute-start.3 = (bf16[512,128]{1,0:T(8,128)(2,1)S(1)}, bf16[512,128]{1,0:T(8,128)(2,1)S(1)}, u32[]{:S(2)}, u32[]{:S(2)}) collective-permute-start(bf16[512,128]{1,0:T(8,128)(2,1)S(1)} %get-tuple-element.29), channel_id=1, source_target_pairs={{0,2},{1,3},{2,0},{3,1},{4,6},{5,7},{6,4},{7,5},{8,10},{9,11},{10,... | collective-permute-start | bytes 393224 | tf_op jit(solution)/shard_map/ppermute | solution.py:253
  23.2 2.9 %collective-permute-start.6 = (bf16[512,128]{1,0:T(8,128)(2,1)S(1)}, bf16[512,128]{1,0:T(8,128)(2,1)S(1)}, u32[]{:S(2)}, u32[]{:S(2)}) collective-permute-start(bf16[512,128]{1,0:T(8,128)(2,1)S(1)} %get-tuple-element.33), channel_id=1, source_target_pairs={{0,4},{1,5},{2,6},{3,7},{4,0},{5,1},{6,2},{7,3},{8,12},{9,13},{10,... | collective-permute-start | bytes 393224 | tf_op jit(solution)/shard_map/ppermute | solution.py:253
  26.1 2.5 %product_keep.3.keep_ref = f32[2080,128]{1,0:T(8,128)S(1)} custom-call(s32[2,512]{1,0:T(2,128)S(1)} %get-tuple-element.25.words_ref, bf16[12288,128]{1,0:T(8,128)(2,1)S(1)} %get-tuple-element.26.blocks_ref, bf16[4096,128]{1,0:T(8,128)(2,1)S(1)} %table.3.table_ref), custom_call_target="tpu_custom_call" | custom-call | flops 536870912 | bytes 1048576 | tf_op jit(solution)/shard_map/product_keep/pallas_call | solution.py:177
  28.7 0.7 %collective-permute-start.10 = (bf16[512,128]{1,0:T(8,128)(2,1)S(1)}, bf16[512,128]{1,0:T(8,128)(2,1)S(1)}, u32[]{:S(2)}, u32[]{:S(2)}) collective-permute-start(bf16[512,128]{1,0:T(8,128)(2,1)S(1)} %get-tuple-element.38), channel_id=1, source_target_pairs={{0,2},{1,3},{2,0},{3,1},{4,6},{5,7},{6,4},{7,5},{8,10},{9,11},{10,... | collective-permute-start | bytes 393224 | tf_op jit(solution)/shard_map/ppermute | solution.py:253
  29.3 2.3 %collective-permute-done.12.got_ref = bf16[1024,128]{1,0:T(8,128)(2,1)S(1)} collective-permute-done((bf16[1024,128]{1,0:T(8,128)(2,1)S(1)}, bf16[1024,128]{1,0:T(8,128)(2,1)S(1)}, u32[]{:S(2)}, u32[]{:S(2)}) %collective-permute-start.12) | collective-permute-done | bytes 262176 | tf_op jit(solution)/shard_map/ppermute | solution.py:253
  31.7 0.9 %collective-permute-start.13 = (bf16[512,128]{1,0:T(8,128)(2,1)S(1)}, bf16[512,128]{1,0:T(8,128)(2,1)S(1)}, u32[]{:S(2)}, u32[]{:S(2)}) collective-permute-start(bf16[512,128]{1,0:T(8,128)(2,1)S(1)} %get-tuple-element.42), channel_id=1, source_target_pairs={{0,4},{1,5},{2,6},{3,7},{4,0},{5,1},{6,2},{7,3},{8,12},{9,13},{10,... | collective-permute-start | bytes 393224 | tf_op jit(solution)/shard_map/ppermute | solution.py:253
  32.6 1.9 %collective-permute-done.3.got_ref = bf16[512,128]{1,0:T(8,128)(2,1)S(1)} collective-permute-done((bf16[512,128]{1,0:T(8,128)(2,1)S(1)}, bf16[512,128]{1,0:T(8,128)(2,1)S(1)}, u32[]{:S(2)}, u32[]{:S(2)}) %collective-permute-start.3) | collective-permute-done | bytes 131104 | tf_op jit(solution)/shard_map/ppermute | solution.py:253
  34.5 1.3 %collective-permute-start.4 = (bf16[256,128]{1,0:T(8,128)(2,1)S(1)}, bf16[256,128]{1,0:T(8,128)(2,1)S(1)}, u32[]{:S(2)}, u32[]{:S(2)}) collective-permute-start(bf16[256,128]{1,0:T(8,128)(2,1)S(1)} %get-tuple-element.31), channel_id=1, source_target_pairs={{0,4},{1,5},{2,6},{3,7},{4,0},{5,1},{6,2},{7,3},{8,12},{9,13},{10,... | collective-permute-start | bytes 196616 | tf_op jit(solution)/shard_map/ppermute | solution.py:253
  35.9 3.4 %collective-permute-start.7 = (bf16[256,128]{1,0:T(8,128)(2,1)S(1)}, bf16[256,128]{1,0:T(8,128)(2,1)S(1)}, u32[]{:S(2)}, u32[]{:S(2)}) collective-permute-start(bf16[256,128]{1,0:T(8,128)(2,1)S(1)} %get-tuple-element.35), channel_id=1, source_target_pairs={{0,1},{1,0},{2,3},{3,2},{4,5},{5,4},{6,7},{7,6},{8,9},{9,8},{10,11... | collective-permute-start | bytes 196616 | tf_op jit(solution)/shard_map/ppermute | solution.py:253
  39.3 0.6 %collective-permute-done.10.got_ref = bf16[512,128]{1,0:T(8,128)(2,1)S(1)} collective-permute-done((bf16[512,128]{1,0:T(8,128)(2,1)S(1)}, bf16[512,128]{1,0:T(8,128)(2,1)S(1)}, u32[]{:S(2)}, u32[]{:S(2)}) %collective-permute-start.10) | collective-permute-done | bytes 131104 | tf_op jit(solution)/shard_map/ppermute | solution.py:253
  39.9 0.4 collective-permute-start.11
  40.3 4.0 %collective-permute-done.13.got_ref = bf16[512,128]{1,0:T(8,128)(2,1)S(1)} collective-permute-done((bf16[512,128]{1,0:T(8,128)(2,1)S(1)}, bf16[512,128]{1,0:T(8,128)(2,1)S(1)}, u32[]{:S(2)}, u32[]{:S(2)}) %collective-permute-start.13) | collective-permute-done | bytes 131104 | tf_op jit(solution)/shard_map/ppermute | solution.py:253
  44.4 1.3 %collective-permute-start.14 = (bf16[256,128]{1,0:T(8,128)(2,1)S(1)}, bf16[256,128]{1,0:T(8,128)(2,1)S(1)}, u32[]{:S(2)}, u32[]{:S(2)}) collective-permute-start(bf16[256,128]{1,0:T(8,128)(2,1)S(1)} %get-tuple-element.44), channel_id=1, source_target_pairs={{0,1},{1,0},{2,3},{3,2},{4,5},{5,4},{6,7},{7,6},{8,9},{9,8},{10,11... | collective-permute-start | bytes 196616 | tf_op jit(solution)/shard_map/ppermute | solution.py:253
  45.7 1.3 %collective-permute-done.11.refs_5_ = bf16[256,128]{1,0:T(8,128)(2,1)S(1)} collective-permute-done((bf16[256,128]{1,0:T(8,128)(2,1)S(1)}, bf16[256,128]{1,0:T(8,128)(2,1)S(1)}, u32[]{:S(2)}, u32[]{:S(2)}) %collective-permute-start.11) | collective-permute-done | bytes 65568 | tf_op jit(solution)/shard_map/ppermute | solution.py:253
  47.0 1.7 %collective-permute-done.14.refs_7_ = bf16[256,128]{1,0:T(8,128)(2,1)S(1)} collective-permute-done((bf16[256,128]{1,0:T(8,128)(2,1)S(1)}, bf16[256,128]{1,0:T(8,128)(2,1)S(1)}, u32[]{:S(2)}, u32[]{:S(2)}) %collective-permute-start.14) | collective-permute-done | bytes 65568 | tf_op jit(solution)/shard_map/ppermute | solution.py:253
  48.7 1.2 %layer.1 = bf16[1024,256]{1,0:T(8,128)(2,1)} custom-call(f32[256,128]{1,0:T(8,128)S(1)} %get-tuple-element.30.refs_0_, bf16[256,128]{1,0:T(8,128)(2,1)S(1)} %collective-permute-done.4.refs_1_, f32[256,128]{1,0:T(8,128)S(1)} %get-tuple-element.34.refs_2_, bf16[256,128]{1,0:T(8,128)(2,1)S(1)} %collective-permute-done.7.refs_3_, ...), custom_call_target="tpu_custom_call" | custom-call | tf_op jit(solution)/shard_map/layer/pallas_call | solution.py:243
  (24 shorter events, 0.4 us)
Async XLA Ops:
  0.0 7.8 %copy-start = (bf16[4096,32]{0,1:T(8,128)(2,1)S(1)}, bf16[4096,32]{0,1:T(8,128)(2,1)}, u32[]{:S(2)}) copy-start(bf16[4096,32]{0,1:T(8,128)(2,1)} %param.6) | copy-start | bytes 786436
  0.0 7.7 %collective-permute-start = (bf16[32,4096]{1,0:T(8,128)(2,1)}, bf16[32,4096]{1,0:T(8,128)(2,1)S(1)}, u32[]{:S(2)}, u32[]{:S(2)}) collective-permute-start(bf16[32,4096]{1,0:T(8,128)(2,1)} %bitcast.3), channel_id=1, source_target_pairs={{0,8},{8,0},{16,24},{24,16},{1,9},{9,1},{17,25},{25,17},{2,10},{10... | collective-permute-start | bytes 786440 | tf_op jit(solution)/shard_map/ppermute | solution.py:253
  0.5 10.0 %collective-permute-start.1 = (bf16[32,4096]{1,0:T(8,128)(2,1)}, bf16[32,4096]{1,0:T(8,128)(2,1)S(1)}, u32[]{:S(2)}, u32[]{:S(2)}) collective-permute-start(bf16[32,4096]{1,0:T(8,128)(2,1)} %bitcast.4), channel_id=1, source_target_pairs={{0,16},{8,24},{16,0},{24,8},{1,17},{9,25},{17,1},{25,9},{2,18},{10... | collective-permute-start | bytes 786440 | tf_op jit(solution)/shard_map/ppermute | solution.py:253
  3.7 0.7 %copy-start.2 = (s32[1,384]{1,0:T(1,128)S(1)}, s32[1,384]{1,0:T(1,128)}, u32[]{:S(2)}) copy-start(s32[1,384]{1,0:T(1,128)} %codes_hbm.1) | copy-start | bytes 4612
  10.4 4.3 %collective-permute-start.8 = (bf16[32,4096]{1,0:T(8,128)(2,1)S(1)}, bf16[32,4096]{1,0:T(8,128)(2,1)S(1)}, u32[]{:S(2)}, u32[]{:S(2)}) collective-permute-start(bf16[32,4096]{1,0:T(8,128)(2,1)S(1)} %collective-permute-done.1.refs_0_), channel_id=1, source_target_pairs={{0,8},{8,0},{16,24},{24,16},{1,9},{9,1},{17,25},{25,17},{2,10},{10... | collective-permute-start | bytes 786440 | tf_op jit(solution)/shard_map/ppermute | solution.py:253
  10.5 11.8 %collective-permute-start.2 = (bf16[1024,128]{1,0:T(8,128)(2,1)S(1)}, bf16[1024,128]{1,0:T(8,128)(2,1)S(1)}, u32[]{:S(2)}, u32[]{:S(2)}) collective-permute-start(bf16[1024,128]{1,0:T(8,128)(2,1)S(1)} %product_send.4), channel_id=1, source_target_pairs={{0,1},{1,0},{2,3},{3,2},{4,5},{5,4},{6,7},{7,6},{8,9},{9,8},{10,11... | collective-permute-start | bytes 786440 | tf_op jit(solution)/shard_map/ppermute | solution.py:253
  13.6 9.5 %collective-permute-start.5 = (bf16[1024,128]{1,0:T(8,128)(2,1)S(1)}, bf16[1024,128]{1,0:T(8,128)(2,1)S(1)}, u32[]{:S(2)}, u32[]{:S(2)}) collective-permute-start(bf16[1024,128]{1,0:T(8,128)(2,1)S(1)} %product_send.5), channel_id=1, source_target_pairs={{0,2},{1,3},{2,0},{3,1},{4,6},{5,7},{6,4},{7,5},{8,10},{9,11},{10,... | collective-permute-start | bytes 786440 | tf_op jit(solution)/shard_map/ppermute | solution.py:253
  17.4 11.2 %collective-permute-start.9 = (bf16[1024,128]{1,0:T(8,128)(2,1)S(1)}, bf16[1024,128]{1,0:T(8,128)(2,1)S(1)}, u32[]{:S(2)}, u32[]{:S(2)}) collective-permute-start(bf16[1024,128]{1,0:T(8,128)(2,1)S(1)} %product_send.6), channel_id=1, source_target_pairs={{0,1},{1,0},{2,3},{3,2},{4,5},{5,4},{6,7},{7,6},{8,9},{9,8},{10,11... | collective-permute-start | bytes 786440 | tf_op jit(solution)/shard_map/ppermute | solution.py:253
  19.7 12.0 %collective-permute-start.12 = (bf16[1024,128]{1,0:T(8,128)(2,1)S(1)}, bf16[1024,128]{1,0:T(8,128)(2,1)S(1)}, u32[]{:S(2)}, u32[]{:S(2)}) collective-permute-start(bf16[1024,128]{1,0:T(8,128)(2,1)S(1)} %product_send.7), channel_id=1, source_target_pairs={{0,2},{1,3},{2,0},{3,1},{4,6},{5,7},{6,4},{7,5},{8,10},{9,11},{10,... | collective-permute-start | bytes 786440 | tf_op jit(solution)/shard_map/ppermute | solution.py:253
  22.3 12.2 %collective-permute-start.3 = (bf16[512,128]{1,0:T(8,128)(2,1)S(1)}, bf16[512,128]{1,0:T(8,128)(2,1)S(1)}, u32[]{:S(2)}, u32[]{:S(2)}) collective-permute-start(bf16[512,128]{1,0:T(8,128)(2,1)S(1)} %get-tuple-element.29), channel_id=1, source_target_pairs={{0,2},{1,3},{2,0},{3,1},{4,6},{5,7},{6,4},{7,5},{8,10},{9,11},{10,... | collective-permute-start | bytes 393224 | tf_op jit(solution)/shard_map/ppermute | solution.py:253
  23.2 12.7 %collective-permute-start.6 = (bf16[512,128]{1,0:T(8,128)(2,1)S(1)}, bf16[512,128]{1,0:T(8,128)(2,1)S(1)}, u32[]{:S(2)}, u32[]{:S(2)}) collective-permute-start(bf16[512,128]{1,0:T(8,128)(2,1)S(1)} %get-tuple-element.33), channel_id=1, source_target_pairs={{0,4},{1,5},{2,6},{3,7},{4,0},{5,1},{6,2},{7,3},{8,12},{9,13},{10,... | collective-permute-start | bytes 393224 | tf_op jit(solution)/shard_map/ppermute | solution.py:253
  28.6 20.1 %copy-start.1 = (bf16[128,256]{1,0:T(8,128)(2,1)S(1)}, bf16[128,256]{1,0:T(8,128)(2,1)}, u32[]{:S(2)}) copy-start(bf16[128,256]{1,0:T(8,128)(2,1)} %refs_8_.1) | copy-start | bytes 196612
  28.6 20.1 %copy-start.3 = (f32[256]{0:T(256)S(1)}, f32[256]{0:T(256)}, u32[]{:S(2)}) copy-start(f32[256]{0:T(256)} %param.11) | copy-start | bytes 3076
  28.7 11.2 %collective-permute-start.10 = (bf16[512,128]{1,0:T(8,128)(2,1)S(1)}, bf16[512,128]{1,0:T(8,128)(2,1)S(1)}, u32[]{:S(2)}, u32[]{:S(2)}) collective-permute-start(bf16[512,128]{1,0:T(8,128)(2,1)S(1)} %get-tuple-element.38), channel_id=1, source_target_pairs={{0,2},{1,3},{2,0},{3,1},{4,6},{5,7},{6,4},{7,5},{8,10},{9,11},{10,... | collective-permute-start | bytes 393224 | tf_op jit(solution)/shard_map/ppermute | solution.py:253
  31.7 12.6 %collective-permute-start.13 = (bf16[512,128]{1,0:T(8,128)(2,1)S(1)}, bf16[512,128]{1,0:T(8,128)(2,1)S(1)}, u32[]{:S(2)}, u32[]{:S(2)}) collective-permute-start(bf16[512,128]{1,0:T(8,128)(2,1)S(1)} %get-tuple-element.42), channel_id=1, source_target_pairs={{0,4},{1,5},{2,6},{3,7},{4,0},{5,1},{6,2},{7,3},{8,12},{9,13},{10,... | collective-permute-start | bytes 393224 | tf_op jit(solution)/shard_map/ppermute | solution.py:253
  34.5 11.2 %collective-permute-start.4 = (bf16[256,128]{1,0:T(8,128)(2,1)S(1)}, bf16[256,128]{1,0:T(8,128)(2,1)S(1)}, u32[]{:S(2)}, u32[]{:S(2)}) collective-permute-start(bf16[256,128]{1,0:T(8,128)(2,1)S(1)} %get-tuple-element.31), channel_id=1, source_target_pairs={{0,4},{1,5},{2,6},{3,7},{4,0},{5,1},{6,2},{7,3},{8,12},{9,13},{10,... | collective-permute-start | bytes 196616 | tf_op jit(solution)/shard_map/ppermute | solution.py:253
  35.9 9.8 %collective-permute-start.7 = (bf16[256,128]{1,0:T(8,128)(2,1)S(1)}, bf16[256,128]{1,0:T(8,128)(2,1)S(1)}, u32[]{:S(2)}, u32[]{:S(2)}) collective-permute-start(bf16[256,128]{1,0:T(8,128)(2,1)S(1)} %get-tuple-element.35), channel_id=1, source_target_pairs={{0,1},{1,0},{2,3},{3,2},{4,5},{5,4},{6,7},{7,6},{8,9},{9,8},{10,11... | collective-permute-start | bytes 196616 | tf_op jit(solution)/shard_map/ppermute | solution.py:253
  39.9 7.1 %collective-permute-start.11 = (bf16[256,128]{1,0:T(8,128)(2,1)S(1)}, bf16[256,128]{1,0:T(8,128)(2,1)S(1)}, u32[]{:S(2)}, u32[]{:S(2)}) collective-permute-start(bf16[256,128]{1,0:T(8,128)(2,1)S(1)} %get-tuple-element.40), channel_id=1, source_target_pairs={{0,4},{1,5},{2,6},{3,7},{4,0},{5,1},{6,2},{7,3},{8,12},{9,13},{10,... | collective-permute-start | bytes 196616 | tf_op jit(solution)/shard_map/ppermute | solution.py:253
  44.4 4.3 %collective-permute-start.14 = (bf16[256,128]{1,0:T(8,128)(2,1)S(1)}, bf16[256,128]{1,0:T(8,128)(2,1)S(1)}, u32[]{:S(2)}, u32[]{:S(2)}) collective-permute-start(bf16[256,128]{1,0:T(8,128)(2,1)S(1)} %get-tuple-element.44), channel_id=1, source_target_pairs={{0,1},{1,0},{2,3},{3,2},{4,5},{5,4},{6,7},{7,6},{8,9},{9,8},{10,11... | collective-permute-start | bytes 196616 | tf_op jit(solution)/shard_map/ppermute | solution.py:253
where the time goes:
time: 49.8 us; the launch traced here: 49.9 us
  Pallas kernels  18.5 us (37%)
  starting transfers between devices  18 us (36%)
  waiting for transfers between devices  11.8 us (24%)
  between operations  0.81 us (2%)
  local copies, waits for them, and re-layouts  0.69 us (1%)
    ppermute x15, starting transfers between devices, exchange(): return lax.ppermute(x, axis, [(i, i ^ 1 << bit) for i in range(size)])  18 us
    ppermute x15, waiting for transfers between devices, exchange(): return lax.ppermute(x, axis, [(i, i ^ 1 << bit) for i in range(size)])  11.8 us
    pallas_call x6, Pallas kernels, product(): pl.pallas_call(functools.partial(product_kernel, trash, feature_half, par...  11.8 us
    pallas_call x1, Pallas kernels, relayout(): pl.pallas_call(functools.partial(relayout_kernel, orders, per, col_bits),...  3.37 us
    pallas_call x2, Pallas kernels, make_table(): pl.pallas_call(table_kernel, in_specs=[VMEM] * len(parts), out_specs=VMEM...  1.85 us
    pallas_call x1, Pallas kernels, layer(): pl.pallas_call(functools.partial(layer_kernel, index), out_shape=jax.Shap...  1.18 us
  transfers between devices with their start and end apart: 15, of which 6 were waited for; matrix products, arithmetic and copies ran while one was open for 0% of the time, Pallas kernels for 35%

commit v1 on v0

--- a/solution.py
+++ b/solution.py
@@ -144,6 +144,14 @@
     low = lax.broadcasted_iota(jnp.int32, (BLK, LANES), 1) < BLK
     acc[...] = jnp.zeros_like(acc)
 
+    def add(first):
+        for u in range(UNROLL):
+            i = first + u
+            word = words_ref[feature_half, jnp.maximum(i, 0)]
+            place = jnp.where((i >= start) & (i < end), word & ((1 << SOURCE_AT) - 1), trash)
+            rows = pl.ds(pl.multiple_of(place * PAIR, PAIR), PAIR)
+            acc[rows, :] = acc[rows, :] + pending[u * PAIR : (u + 1) * PAIR, :]
+
     def step(g, carry):
         first = start + g * UNROLL
         products = []
@@ -155,17 +163,14 @@
             zero = jnp.zeros_like(right)
             right = jnp.concatenate([jnp.where(low, right, zero), jnp.where(low, zero, right)], axis=0)
             products.append(jnp.dot(block, right, preferred_element_type=jnp.float32))
-        for u in range(UNROLL):
-            i = first - UNROLL + u
-            word = words_ref[feature_half, jnp.maximum(i, 0)]
-            place = jnp.where((i >= start) & (i < end), word & ((1 << SOURCE_AT) - 1), trash)
-            rows = pl.ds(pl.multiple_of(place * PAIR, PAIR), PAIR)
-            acc[rows, :] = acc[rows, :] + pending[u * PAIR : (u + 1) * PAIR, :]
+        add(first - UNROLL)
         for u in range(UNROLL):
             pending[u * PAIR : (u + 1) * PAIR, :] = products[u]
         return carry
 
-    lax.fori_loop(0, (end - start + (UNROLL - 1)) // UNROLL + 1, step, 0)
+    groups = (end - start + (UNROLL - 1)) // UNROLL
+    lax.fori_loop(0, groups, step, 0)
+    add(start + (groups - 1) * UNROLL)
     if len(outs) > 2:
         outs[0][...] = acc[: trash * PAIR, :].astype(outs[0].dtype)
 
@@ -261,7 +266,7 @@
     half = row_total // 4
 
     z_first, x_first = col_axis_bits[1:] + col_axis_bits[:1], col_axis_bits
-    orders = ((x_first, z_first), (x_first, z_first))
+    orders = ((x_first, z_first), (x_first, x_first))
 
     def spread(pieces, index):
         for bit in range(top):
@@ -274,20 +279,18 @@
     near, near_index = spread([mine], [0])
     blocks, words = relayout(orders, per, log2(col_blocks), block_count, block_codes, block_values[0])
 
-    def products(f, table):
-        sends = [product(f, k, words, blocks, table, half, True) for k in range(2)]
-        kept = product(f, 2, words, blocks, table, 2 * half, False)
-        return sends, [(kept, 0), (kept, 1)]
-
     table = make_table(near)
     first = product(0, 0, words, blocks, table, half, True)
     other, first = lax.optimization_barrier((other, first))
     far, far_index = spread([other], [1 << top])
-    sends = [first, product(0, 1, words, blocks, table, half, True)]
-    kept = product(0, 2, words, blocks, table, 2 * half, False)
-    keeps = [(kept, 0), (kept, 1)]
-    more_sends, more_keeps = products(1, make_table(far))
-    sends, keeps = sends + more_sends, keeps + more_keeps
+    sends, keeps = [first, product(0, 1, words, blocks, table, half, True)], []
+    for f in range(2):
+        if f > 0:
+            table = make_table(far)
+            sends += [product(f, k, words, blocks, table, half, True) for k in range(2)]
+        kept = product(f, 2, words, blocks, table, 2 * half, False)
+        keeps += [(kept, 0), (kept, 1)]
+        far[0], _ = lax.optimization_barrier((far[0], kept))
 
     chunk_orders = orders[0] + orders[1]
     for k in range(len(col_axis_bits)):

time: 49.8 us -> 49.4 us (level)
  Pallas kernels: 18.5 us -> 22 us
  waiting for transfers between devices: 11.8 us -> 8.92 us
  starting transfers between devices: 18 us -> 17.2 us
    pallas_call x6, Pallas kernels: 11.8 us -> 15.3 us  [product(): pl.pallas_call(functools.partial(product_kernel, trash, feature_half, par...]
    ppermute x15, waiting for transfers between devices: 11.8 us -> 8.92 us  [exchange(): return lax.ppermute(x, axis, [(i, i ^ 1 << bit) for i in range(size)])]
    ppermute x15, starting transfers between devices: 18 us -> 17.2 us  [exchange(): return lax.ppermute(x, axis, [(i, i ^ 1 << bit) for i in range(size)])]
  transfers between devices with their start and end apart: 15 -> 15, of which waited for: 6 -> 4; matrix products, arithmetic and copies ran while one was open for 0% -> 0% of each run, Pallas kernels for 35% -> 42%
where the time goes in v1:
time: 49.4 us; the launch traced here: 49.7 us
  Pallas kernels  22 us (45%)
  starting transfers between devices  17.2 us (35%)
  waiting for transfers between devices  8.92 us (18%)
  between operations  0.82 us (2%)
  local copies, waits for them, and re-layouts  0.69 us (1%)
    ppermute x15, starting transfers between devices, exchange(): return lax.ppermute(x, axis, [(i, i ^ 1 << bit) for i in range(size)])  17.2 us
    pallas_call x6, Pallas kernels, product(): pl.pallas_call(functools.partial(product_kernel, trash, feature_half, par...  15.3 us
    ppermute x15, waiting for transfers between devices, exchange(): return lax.ppermute(x, axis, [(i, i ^ 1 << bit) for i in range(size)])  8.92 us
    pallas_call x1, Pallas kernels, relayout(): pl.pallas_call(functools.partial(relayout_kernel, orders, per, col_bits),...  3.37 us
    pallas_call x2, Pallas kernels, make_table(): pl.pallas_call(table_kernel, in_specs=[VMEM] * len(parts), out_specs=VMEM...  1.85 us
    pallas_call x1, Pallas kernels, layer(): pl.pallas_call(functools.partial(layer_kernel, index), out_shape=jax.Shap...  1.18 us
  transfers between devices with their start and end apart: 15, of which 4 were waited for; matrix products, arithmetic and copies ran while one was open for 0% of the time, Pallas kernels for 42%

profile of v1, /device:TPU:0, one launch (start us, length us, event | category | flops | bytes accessed | tf_op | source)
XLA Modules:
  0.0 49.7 jit_solution(3766551414689841130)
XLA Ops:
  0.0 0.5 collective-permute-start
  0.5 2.6 %collective-permute-start.1 = (bf16[32,4096]{1,0:T(8,128)(2,1)}, bf16[32,4096]{1,0:T(8,128)(2,1)S(1)}, u32[]{:S(2)}, u32[]{:S(2)}) collective-permute-start(bf16[32,4096]{1,0:T(8,128)(2,1)} %bitcast.4), channel_id=1, source_target_pairs={{0,16},{8,24},{16,0},{24,8},{1,17},{9,25},{17,1},{25,9},{2,18},{10... | collective-permute-start | bytes 786440 | tf_op jit(solution)/shard_map/ppermute | solution.py:258
  3.7 0.7 %copy-done.2 = s32[1,384]{1,0:T(1,128)S(1)} copy-done((s32[1,384]{1,0:T(1,128)S(1)}, s32[1,384]{1,0:T(1,128)}, u32[]{:S(2)}) %copy-start.2) | copy-done | bytes 1560
  4.4 3.4 %relayout.1 = (bf16[12288,128]{1,0:T(8,128)(2,1)S(1)}, s32[2,512]{1,0:T(2,128)S(1)}) custom-call(s32[1,1]{1,0:T(1,128)S(6)} %copy.7.count_ref, s32[1,384]{1,0:T(1,128)S(1)} %copy-done.2, bf16[384,4096]{1,0:T(8,128)(2,1)} %bitcast.7), custom_call_target="tpu_custom_call" | custom-call | bytes 6291456 | tf_op jit(solution)/shard_map/relayout/pallas_call | solution.py:94
  7.8 0.9 %table.2.table_ref = bf16[4096,128]{1,0:T(8,128)(2,1)S(1)} custom-call(bf16[32,4096]{1,0:T(8,128)(2,1)S(1)} %bitcast.5, bf16[32,4096]{1,0:T(8,128)(2,1)S(1)} %collective-permute-done.refs_1_), custom_call_target="tpu_custom_call" | custom-call | bytes 1572864 | tf_op jit(solution)/shard_map/table/pallas_call | solution.py:129
  8.7 2.1 %product_send.4 = bf16[1024,128]{1,0:T(8,128)(2,1)S(1)} custom-call(s32[2,512]{1,0:T(2,128)S(1)} %get-tuple-element.26.words_ref, bf16[12288,128]{1,0:T(8,128)(2,1)S(1)} %get-tuple-element.27.blocks_ref, bf16[4096,128]{1,0:T(8,128)(2,1)S(1)} %table.2.table_ref), custom_call_target="tpu_custom_call" | custom-call | flops 268435456 | bytes 1048576 | tf_op jit(solution)/shard_map/product_send/pallas_call | solution.py:182
  10.8 0.1 collective-permute-start.8
  10.9 1.0 %collective-permute-start.2 = (bf16[1024,128]{1,0:T(8,128)(2,1)S(1)}, bf16[1024,128]{1,0:T(8,128)(2,1)S(1)}, u32[]{:S(2)}, u32[]{:S(2)}) collective-permute-start(bf16[1024,128]{1,0:T(8,128)(2,1)S(1)} %product_send.4), channel_id=1, source_target_pairs={{0,1},{1,0},{2,3},{3,2},{4,5},{5,4},{6,7},{7,6},{8,9},{9,8},{10,11... | collective-permute-start | bytes 786440 | tf_op jit(solution)/shard_map/ppermute | solution.py:258
  11.9 2.1 %product_send.5 = bf16[1024,128]{1,0:T(8,128)(2,1)S(1)} custom-call(s32[2,512]{1,0:T(2,128)S(1)} %get-tuple-element.26.words_ref, bf16[12288,128]{1,0:T(8,128)(2,1)S(1)} %get-tuple-element.27.blocks_ref, bf16[4096,128]{1,0:T(8,128)(2,1)S(1)} %table.2.table_ref), custom_call_target="tpu_custom_call" | custom-call | flops 268435456 | bytes 1048576 | tf_op jit(solution)/shard_map/product_send/pallas_call | solution.py:182
  13.9 1.2 %collective-permute-start.5 = (bf16[1024,128]{1,0:T(8,128)(2,1)S(1)}, bf16[1024,128]{1,0:T(8,128)(2,1)S(1)}, u32[]{:S(2)}, u32[]{:S(2)}) collective-permute-start(bf16[1024,128]{1,0:T(8,128)(2,1)S(1)} %product_send.5), channel_id=1, source_target_pairs={{0,2},{1,3},{2,0},{3,1},{4,6},{5,7},{6,4},{7,5},{8,10},{9,11},{10,... | collective-permute-start | bytes 786440 | tf_op jit(solution)/shard_map/ppermute | solution.py:258
  15.2 3.4 %product_keep.2.keep_ref = f32[2080,128]{1,0:T(8,128)S(1)} custom-call(s32[2,512]{1,0:T(2,128)S(1)} %get-tuple-element.26.words_ref, bf16[12288,128]{1,0:T(8,128)(2,1)S(1)} %get-tuple-element.27.blocks_ref, bf16[4096,128]{1,0:T(8,128)(2,1)S(1)} %table.2.table_ref), custom_call_target="tpu_custom_call" | custom-call | flops 536870912 | bytes 1048576 | tf_op jit(solution)/shard_map/product_keep/pallas_call | solution.py:182
  18.6 0.9 %table.3.table_ref = bf16[4096,128]{1,0:T(8,128)(2,1)S(1)} custom-call(bf16[32,4096]{1,0:T(8,128)(2,1)S(1)} %collective-permute-done.1.refs_0_, bf16[32,4096]{1,0:T(8,128)(2,1)S(1)} %collective-permute-done.8.refs_1_), custom_call_target="tpu_custom_call" | custom-call | bytes 1572864 | tf_op jit(solution)/shard_map/table/pallas_call | solution.py:129
  19.5 2.1 %product_send.6 = bf16[1024,128]{1,0:T(8,128)(2,1)S(1)} custom-call(s32[2,512]{1,0:T(2,128)S(1)} %get-tuple-element.26.words_ref, bf16[12288,128]{1,0:T(8,128)(2,1)S(1)} %get-tuple-element.27.blocks_ref, bf16[4096,128]{1,0:T(8,128)(2,1)S(1)} %table.3.table_ref), custom_call_target="tpu_custom_call" | custom-call | flops 268435456 | bytes 1048576 | tf_op jit(solution)/shard_map/product_send/pallas_call | solution.py:182
  21.6 0.1 collective-permute-start.9
  21.6 2.3 %product_send.7 = bf16[1024,128]{1,0:T(8,128)(2,1)S(1)} custom-call(s32[2,512]{1,0:T(2,128)S(1)} %get-tuple-element.26.words_ref, bf16[12288,128]{1,0:T(8,128)(2,1)S(1)} %get-tuple-element.27.blocks_ref, bf16[4096,128]{1,0:T(8,128)(2,1)S(1)} %table.3.table_ref), custom_call_target="tpu_custom_call" | custom-call | flops 268435456 | bytes 1048576 | tf_op jit(solution)/shard_map/product_send/pallas_call | solution.py:182
  24.0 0.8 %collective-permute-start.12 = (bf16[1024,128]{1,0:T(8,128)(2,1)S(1)}, bf16[1024,128]{1,0:T(8,128)(2,1)S(1)}, u32[]{:S(2)}, u32[]{:S(2)}) collective-permute-start(bf16[1024,128]{1,0:T(8,128)(2,1)S(1)} %product_send.7), channel_id=1, source_target_pairs={{0,1},{1,0},{2,3},{3,2},{4,5},{5,4},{6,7},{7,6},{8,9},{9,8},{10,11... | collective-permute-start | bytes 786440 | tf_op jit(solution)/shard_map/ppermute | solution.py:258
  24.8 0.1 collective-permute-start.3
  24.9 0.1 add.10
  25.0 2.2 %collective-permute-start.6 = (bf16[512,128]{1,0:T(8,128)(2,1)S(1)}, bf16[512,128]{1,0:T(8,128)(2,1)S(1)}, u32[]{:S(2)}, u32[]{:S(2)}) collective-permute-start(bf16[512,128]{1,0:T(8,128)(2,1)S(1)} %get-tuple-element.34), channel_id=1, source_target_pairs={{0,4},{1,5},{2,6},{3,7},{4,0},{5,1},{6,2},{7,3},{8,12},{9,13},{10,... | collective-permute-start | bytes 393224 | tf_op jit(solution)/shard_map/ppermute | solution.py:258
  27.1 3.4 %product_keep.3.keep_ref = f32[2080,128]{1,0:T(8,128)S(1)} custom-call(s32[2,512]{1,0:T(2,128)S(1)} %get-tuple-element.26.words_ref, bf16[12288,128]{1,0:T(8,128)(2,1)S(1)} %get-tuple-element.27.blocks_ref, bf16[4096,128]{1,0:T(8,128)(2,1)S(1)} %table.3.table_ref), custom_call_target="tpu_custom_call" | custom-call | flops 536870912 | bytes 1048576 | tf_op jit(solution)/shard_map/product_keep/pallas_call | solution.py:182
  30.5 0.1 add.12
  30.6 0.1 collective-permute-start.10
  30.7 2.0 %collective-permute-done.12.got_ref = bf16[1024,128]{1,0:T(8,128)(2,1)S(1)} collective-permute-done((bf16[1024,128]{1,0:T(8,128)(2,1)S(1)}, bf16[1024,128]{1,0:T(8,128)(2,1)S(1)}, u32[]{:S(2)}, u32[]{:S(2)}) %collective-permute-start.12) | collective-permute-done | bytes 262176 | tf_op jit(solution)/shard_map/ppermute | solution.py:258
  32.7 0.7 %collective-permute-start.13 = (bf16[512,128]{1,0:T(8,128)(2,1)S(1)}, bf16[512,128]{1,0:T(8,128)(2,1)S(1)}, u32[]{:S(2)}, u32[]{:S(2)}) collective-permute-start(bf16[512,128]{1,0:T(8,128)(2,1)S(1)} %get-tuple-element.44), channel_id=1, source_target_pairs={{0,2},{1,3},{2,0},{3,1},{4,6},{5,7},{6,4},{7,5},{8,10},{9,11},{10,... | collective-permute-start | bytes 393224 | tf_op jit(solution)/shard_map/ppermute | solution.py:258
  33.4 4.0 %collective-permute-start.4 = (bf16[256,128]{1,0:T(8,128)(2,1)S(1)}, bf16[256,128]{1,0:T(8,128)(2,1)S(1)}, u32[]{:S(2)}, u32[]{:S(2)}) collective-permute-start(bf16[256,128]{1,0:T(8,128)(2,1)S(1)} %get-tuple-element.32), channel_id=1, source_target_pairs={{0,4},{1,5},{2,6},{3,7},{4,0},{5,1},{6,2},{7,3},{8,12},{9,13},{10,... | collective-permute-start | bytes 196616 | tf_op jit(solution)/shard_map/ppermute | solution.py:258
  37.5 1.6 %collective-permute-start.7 = (bf16[256,128]{1,0:T(8,128)(2,1)S(1)}, bf16[256,128]{1,0:T(8,128)(2,1)S(1)}, u32[]{:S(2)}, u32[]{:S(2)}) collective-permute-start(bf16[256,128]{1,0:T(8,128)(2,1)S(1)} %get-tuple-element.36), channel_id=1, source_target_pairs={{0,1},{1,0},{2,3},{3,2},{4,5},{5,4},{6,7},{7,6},{8,9},{9,8},{10,11... | collective-permute-start | bytes 196616 | tf_op jit(solution)/shard_map/ppermute | solution.py:258
  39.1 0.1 collective-permute-start.11
  39.1 1.3 %collective-permute-done.13.got_ref = bf16[512,128]{1,0:T(8,128)(2,1)S(1)} collective-permute-done((bf16[512,128]{1,0:T(8,128)(2,1)S(1)}, bf16[512,128]{1,0:T(8,128)(2,1)S(1)}, u32[]{:S(2)}, u32[]{:S(2)}) %collective-permute-start.13) | collective-permute-done | bytes 131104 | tf_op jit(solution)/shard_map/ppermute | solution.py:258
  40.4 2.4 %collective-permute-start.14 = (bf16[256,128]{1,0:T(8,128)(2,1)S(1)}, bf16[256,128]{1,0:T(8,128)(2,1)S(1)}, u32[]{:S(2)}, u32[]{:S(2)}) collective-permute-start(bf16[256,128]{1,0:T(8,128)(2,1)S(1)} %get-tuple-element.46), channel_id=1, source_target_pairs={{0,4},{1,5},{2,6},{3,7},{4,0},{5,1},{6,2},{7,3},{8,12},{9,13},{10,... | collective-permute-start | bytes 196616 | tf_op jit(solution)/shard_map/ppermute | solution.py:258
  42.8 5.0 %collective-permute-done.11.refs_5_ = bf16[256,128]{1,0:T(8,128)(2,1)S(1)} collective-permute-done((bf16[256,128]{1,0:T(8,128)(2,1)S(1)}, bf16[256,128]{1,0:T(8,128)(2,1)S(1)}, u32[]{:S(2)}, u32[]{:S(2)}) %collective-permute-start.11) | collective-permute-done | bytes 65568 | tf_op jit(solution)/shard_map/ppermute | solution.py:258
  47.8 0.7 %collective-permute-done.14.refs_7_ = bf16[256,128]{1,0:T(8,128)(2,1)S(1)} collective-permute-done((bf16[256,128]{1,0:T(8,128)(2,1)S(1)}, bf16[256,128]{1,0:T(8,128)(2,1)S(1)}, u32[]{:S(2)}, u32[]{:S(2)}) %collective-permute-start.14) | collective-permute-done | bytes 65568 | tf_op jit(solution)/shard_map/ppermute | solution.py:258
  48.5 1.2 %layer.1 = bf16[1024,256]{1,0:T(8,128)(2,1)} custom-call(f32[256,128]{1,0:T(8,128)S(1)} %get-tuple-element.31.refs_0_, bf16[256,128]{1,0:T(8,128)(2,1)S(1)} %collective-permute-done.4.refs_1_, f32[256,128]{1,0:T(8,128)S(1)} %get-tuple-element.35.refs_2_, bf16[256,128]{1,0:T(8,128)(2,1)S(1)} %collective-permute-done.7.refs_3_, ...), custom_call_target="tpu_custom_call" | custom-call | tf_op jit(solution)/shard_map/layer/pallas_call | solution.py:248
  (24 shorter events, 0.3 us)
Async XLA Ops:
  0.0 7.8 %copy-start = (bf16[4096,32]{0,1:T(8,128)(2,1)S(1)}, bf16[4096,32]{0,1:T(8,128)(2,1)}, u32[]{:S(2)}) copy-start(bf16[4096,32]{0,1:T(8,128)(2,1)} %param.6) | copy-start | bytes 786436
  0.0 7.7 %collective-permute-start = (bf16[32,4096]{1,0:T(8,128)(2,1)}, bf16[32,4096]{1,0:T(8,128)(2,1)S(1)}, u32[]{:S(2)}, u32[]{:S(2)}) collective-permute-start(bf16[32,4096]{1,0:T(8,128)(2,1)} %bitcast.3), channel_id=1, source_target_pairs={{0,8},{8,0},{16,24},{24,16},{1,9},{9,1},{17,25},{25,17},{2,10},{10... | collective-permute-start | bytes 786440 | tf_op jit(solution)/shard_map/ppermute | solution.py:258
  0.5 10.3 %collective-permute-start.1 = (bf16[32,4096]{1,0:T(8,128)(2,1)}, bf16[32,4096]{1,0:T(8,128)(2,1)S(1)}, u32[]{:S(2)}, u32[]{:S(2)}) collective-permute-start(bf16[32,4096]{1,0:T(8,128)(2,1)} %bitcast.4), channel_id=1, source_target_pairs={{0,16},{8,24},{16,0},{24,8},{1,17},{9,25},{17,1},{25,9},{2,18},{10... | collective-permute-start | bytes 786440 | tf_op jit(solution)/shard_map/ppermute | solution.py:258
  3.7 0.7 %copy-start.2 = (s32[1,384]{1,0:T(1,128)S(1)}, s32[1,384]{1,0:T(1,128)}, u32[]{:S(2)}) copy-start(s32[1,384]{1,0:T(1,128)} %codes_hbm.1) | copy-start | bytes 4612
  10.8 7.8 %collective-permute-start.8 = (bf16[32,4096]{1,0:T(8,128)(2,1)S(1)}, bf16[32,4096]{1,0:T(8,128)(2,1)S(1)}, u32[]{:S(2)}, u32[]{:S(2)}) collective-permute-start(bf16[32,4096]{1,0:T(8,128)(2,1)S(1)} %collective-permute-done.1.refs_0_), channel_id=1, source_target_pairs={{0,8},{8,0},{16,24},{24,16},{1,9},{9,1},{17,25},{25,17},{2,10},{10... | collective-permute-start | bytes 786440 | tf_op jit(solution)/shard_map/ppermute | solution.py:258
  10.9 13.9 %collective-permute-start.2 = (bf16[1024,128]{1,0:T(8,128)(2,1)S(1)}, bf16[1024,128]{1,0:T(8,128)(2,1)S(1)}, u32[]{:S(2)}, u32[]{:S(2)}) collective-permute-start(bf16[1024,128]{1,0:T(8,128)(2,1)S(1)} %product_send.4), channel_id=1, source_target_pairs={{0,1},{1,0},{2,3},{3,2},{4,5},{5,4},{6,7},{7,6},{8,9},{9,8},{10,11... | collective-permute-start | bytes 786440 | tf_op jit(solution)/shard_map/ppermute | solution.py:258
  13.9 11.0 %collective-permute-start.5 = (bf16[1024,128]{1,0:T(8,128)(2,1)S(1)}, bf16[1024,128]{1,0:T(8,128)(2,1)S(1)}, u32[]{:S(2)}, u32[]{:S(2)}) collective-permute-start(bf16[1024,128]{1,0:T(8,128)(2,1)S(1)} %product_send.5), channel_id=1, source_target_pairs={{0,2},{1,3},{2,0},{3,1},{4,6},{5,7},{6,4},{7,5},{8,10},{9,11},{10,... | collective-permute-start | bytes 786440 | tf_op jit(solution)/shard_map/ppermute | solution.py:258
  21.6 9.0 %collective-permute-start.9 = (bf16[1024,128]{1,0:T(8,128)(2,1)S(1)}, bf16[1024,128]{1,0:T(8,128)(2,1)S(1)}, u32[]{:S(2)}, u32[]{:S(2)}) collective-permute-start(bf16[1024,128]{1,0:T(8,128)(2,1)S(1)} %product_send.6), channel_id=1, source_target_pairs={{0,1},{1,0},{2,3},{3,2},{4,5},{5,4},{6,7},{7,6},{8,9},{9,8},{10,11... | collective-permute-start | bytes 786440 | tf_op jit(solution)/shard_map/ppermute | solution.py:258
  24.0 8.7 %collective-permute-start.12 = (bf16[1024,128]{1,0:T(8,128)(2,1)S(1)}, bf16[1024,128]{1,0:T(8,128)(2,1)S(1)}, u32[]{:S(2)}, u32[]{:S(2)}) collective-permute-start(bf16[1024,128]{1,0:T(8,128)(2,1)S(1)} %product_send.7), channel_id=1, source_target_pairs={{0,1},{1,0},{2,3},{3,2},{4,5},{5,4},{6,7},{7,6},{8,9},{9,8},{10,11... | collective-permute-start | bytes 786440 | tf_op jit(solution)/shard_map/ppermute | solution.py:258
  24.8 8.6 %collective-permute-start.3 = (bf16[512,128]{1,0:T(8,128)(2,1)S(1)}, bf16[512,128]{1,0:T(8,128)(2,1)S(1)}, u32[]{:S(2)}, u32[]{:S(2)}) collective-permute-start(bf16[512,128]{1,0:T(8,128)(2,1)S(1)} %get-tuple-element.30), channel_id=1, source_target_pairs={{0,2},{1,3},{2,0},{3,1},{4,6},{5,7},{6,4},{7,5},{8,10},{9,11},{10,... | collective-permute-start | bytes 393224 | tf_op jit(solution)/shard_map/ppermute | solution.py:258
  25.0 12.5 %collective-permute-start.6 = (bf16[512,128]{1,0:T(8,128)(2,1)S(1)}, bf16[512,128]{1,0:T(8,128)(2,1)S(1)}, u32[]{:S(2)}, u32[]{:S(2)}) collective-permute-start(bf16[512,128]{1,0:T(8,128)(2,1)S(1)} %get-tuple-element.34), channel_id=1, source_target_pairs={{0,4},{1,5},{2,6},{3,7},{4,0},{5,1},{6,2},{7,3},{8,12},{9,13},{10,... | collective-permute-start | bytes 393224 | tf_op jit(solution)/shard_map/ppermute | solution.py:258
  30.5 18.0 %copy-start.1 = (bf16[128,256]{1,0:T(8,128)(2,1)S(1)}, bf16[128,256]{1,0:T(8,128)(2,1)}, u32[]{:S(2)}) copy-start(bf16[128,256]{1,0:T(8,128)(2,1)} %refs_8_.1) | copy-start | bytes 196612
  30.5 18.0 %copy-start.3 = (f32[256]{0:T(256)S(1)}, f32[256]{0:T(256)}, u32[]{:S(2)}) copy-start(f32[256]{0:T(256)} %param.11) | copy-start | bytes 3076
  30.6 8.4 %collective-permute-start.10 = (bf16[512,128]{1,0:T(8,128)(2,1)S(1)}, bf16[512,128]{1,0:T(8,128)(2,1)S(1)}, u32[]{:S(2)}, u32[]{:S(2)}) collective-permute-start(bf16[512,128]{1,0:T(8,128)(2,1)S(1)} %get-tuple-element.40), channel_id=1, source_target_pairs={{0,2},{1,3},{2,0},{3,1},{4,6},{5,7},{6,4},{7,5},{8,10},{9,11},{10,... | collective-permute-start | bytes 393224 | tf_op jit(solution)/shard_map/ppermute | solution.py:258
  32.7 7.7 %collective-permute-start.13 = (bf16[512,128]{1,0:T(8,128)(2,1)S(1)}, bf16[512,128]{1,0:T(8,128)(2,1)S(1)}, u32[]{:S(2)}, u32[]{:S(2)}) collective-permute-start(bf16[512,128]{1,0:T(8,128)(2,1)S(1)} %get-tuple-element.44), channel_id=1, source_target_pairs={{0,2},{1,3},{2,0},{3,1},{4,6},{5,7},{6,4},{7,5},{8,10},{9,11},{10,... | collective-permute-start | bytes 393224 | tf_op jit(solution)/shard_map/ppermute | solution.py:258
  33.4 9.4 %collective-permute-start.4 = (bf16[256,128]{1,0:T(8,128)(2,1)S(1)}, bf16[256,128]{1,0:T(8,128)(2,1)S(1)}, u32[]{:S(2)}, u32[]{:S(2)}) collective-permute-start(bf16[256,128]{1,0:T(8,128)(2,1)S(1)} %get-tuple-element.32), channel_id=1, source_target_pairs={{0,4},{1,5},{2,6},{3,7},{4,0},{5,1},{6,2},{7,3},{8,12},{9,13},{10,... | collective-permute-start | bytes 196616 | tf_op jit(solution)/shard_map/ppermute | solution.py:258
  37.5 5.4 %collective-permute-start.7 = (bf16[256,128]{1,0:T(8,128)(2,1)S(1)}, bf16[256,128]{1,0:T(8,128)(2,1)S(1)}, u32[]{:S(2)}, u32[]{:S(2)}) collective-permute-start(bf16[256,128]{1,0:T(8,128)(2,1)S(1)} %get-tuple-element.36), channel_id=1, source_target_pairs={{0,1},{1,0},{2,3},{3,2},{4,5},{5,4},{6,7},{7,6},{8,9},{9,8},{10,11... | collective-permute-start | bytes 196616 | tf_op jit(solution)/shard_map/ppermute | solution.py:258
  39.1 8.7 %collective-permute-start.11 = (bf16[256,128]{1,0:T(8,128)(2,1)S(1)}, bf16[256,128]{1,0:T(8,128)(2,1)S(1)}, u32[]{:S(2)}, u32[]{:S(2)}) collective-permute-start(bf16[256,128]{1,0:T(8,128)(2,1)S(1)} %get-tuple-element.42), channel_id=1, source_target_pairs={{0,4},{1,5},{2,6},{3,7},{4,0},{5,1},{6,2},{7,3},{8,12},{9,13},{10,... | collective-permute-start | bytes 196616 | tf_op jit(solution)/shard_map/ppermute | solution.py:258
  40.4 8.1 %collective-permute-start.14 = (bf16[256,128]{1,0:T(8,128)(2,1)S(1)}, bf16[256,128]{1,0:T(8,128)(2,1)S(1)}, u32[]{:S(2)}, u32[]{:S(2)}) collective-permute-start(bf16[256,128]{1,0:T(8,128)(2,1)S(1)} %get-tuple-element.46), channel_id=1, source_target_pairs={{0,4},{1,5},{2,6},{3,7},{4,0},{5,1},{6,2},{7,3},{8,12},{9,13},{10,... | collective-permute-start | bytes 196616 | tf_op jit(solution)/shard_map/ppermute | solution.py:258

commit v2 on v1

v2 whole, which is shorter than its diff:
```python
import functools

import jax
import jax.numpy as jnp
from jax import lax
from jax.experimental import pallas as pl
from jax.experimental.pallas import tpu as pltpu
from jax.sharding import PartitionSpec as P

BLK = 64
PAIR = BLK // 2
LANES = 2 * BLK
GROUP = 16
STEPS = 4
UNROLL = 16
SLOT_AT, SOURCE_AT = 13, 7
MIB = 1024 * 1024
SMEM = pl.BlockSpec(memory_space=pltpu.SMEM)
VMEM = pl.BlockSpec(memory_space=pltpu.VMEM)


def log2(size):
    return size.bit_length() - 1


def list_width(slots):
    return -(-(slots + 2 * UNROLL + 8) // LANES) * LANES


def make_lists(orders, per, col_bits, count, codes, words_ref):
    slots, width = codes.shape[1], words_ref.shape[1]
    chunks = len(orders)
    small = per // chunks
    half = small << (len(orders[0]) - 1)
    row_block, col_block = codes >> col_bits, codes & ((1 << col_bits) - 1)
    owner = (row_block >> log2(per)) ^ lax.axis_index("col")
    sub = row_block & (per - 1)
    chunk, rest = sub >> log2(small), sub & (small - 1)
    number = lax.broadcasted_iota(jnp.int32, (1, slots), 1)
    same = lax.broadcasted_iota(jnp.int32, (slots, slots), 0) == lax.broadcasted_iota(jnp.int32, (slots, slots), 1)
    column = lambda row: jnp.sum(jnp.where(same, row, 0.0), axis=1, keepdims=True)
    spot = lax.broadcasted_iota(jnp.int32, (slots, width), 1).astype(jnp.float32)
    lane = lax.broadcasted_iota(jnp.int32, (1, width), 1)
    chosen = jnp.zeros_like(owner)
    for order in sorted(set(orders)):
        place = jnp.zeros_like(owner)
        for k, bit in enumerate(order):
            place = place | (((owner >> bit) & 1) << (len(order) - 1 - k))
        for i in range(chunks):
            if orders[i] == order:
                chosen = jnp.where(chunk == i, place, chosen)
    place = (chosen << log2(small)) + rest
    keep = place < half
    target = jnp.where(keep, chunk * half + place, place - half)
    group = jnp.where(number < count, jnp.where(keep, chunks, chunk), chunks + 1)
    key = (group * slots + number).astype(jnp.float32)
    word = ((number << SLOT_AT) | (col_block << SOURCE_AT) | target).astype(jnp.float32)
    rank = jnp.sum(jnp.where(key < column(key), 1.0, 0.0), axis=1, keepdims=True)
    words = jnp.sum(jnp.where(rank == spot, column(word), 0.0), axis=0, keepdims=True).astype(jnp.int32)
    for k in range(chunks + 2):
        before = jnp.sum(jnp.where(group < k, 1.0, 0.0), axis=1, keepdims=True).astype(jnp.int32)
        words = jnp.where(lane == width - 8 + k, before, words)
    words_ref[...] = words


def relayout_kernel(orders, per, col_bits, count_ref, codes_hbm, values_hbm, out_ref, words_ref, codes, held, scratch, arrived, codes_arrived):
    codes_copy = pltpu.make_async_copy(codes_hbm, codes, codes_arrived)
    codes_copy.start()
    step = values_hbm.shape[0] // STEPS
    copies = []
    for k in range(STEPS):
        rows = pl.ds(k * step, step)
        copies.append(pltpu.make_async_copy(values_hbm.at[rows], held.at[rows], arrived.at[k]))
        copies[k].start()
    codes_copy.wait()
    make_lists(orders, per, col_bits, count_ref[0, 0], codes[...], words_ref)

    def one(g, carry):
        slots = pl.ds(pl.multiple_of(g * GROUP, GROUP), GROUP)
        base = pl.multiple_of(g * (GROUP * PAIR), GROUP * PAIR)
        for p in range(PAIR):
            scratch[pl.ds(base + p * GROUP, GROUP), :] = held[slots, p * LANES : (p + 1) * LANES].astype(jnp.float32)
        for s in range(GROUP):
            rows = scratch[pl.ds(base + s, PAIR, stride=GROUP), :]
            out_ref[pl.ds(base + s * PAIR, PAIR), :] = rows.astype(out_ref.dtype)
        return carry

    groups = step // GROUP
    for k in range(STEPS):
        copies[k].wait()
        lax.fori_loop(k * groups, (k + 1) * groups, one, 0, unroll=2)


def relayout(orders, per, col_bits, count, codes, values):
    slots = values.shape[0]
    return pl.pallas_call(
        functools.partial(relayout_kernel, orders, per, col_bits),
        in_specs=[SMEM] + [pl.BlockSpec(memory_space=pltpu.HBM)] * 2,
        out_specs=(VMEM, VMEM),
        out_shape=(
            jax.ShapeDtypeStruct((slots * PAIR, LANES), values.dtype),
            jax.ShapeDtypeStruct((1, list_width(slots)), jnp.int32),
        ),
        scratch_shapes=[
            pltpu.VMEM(codes.shape, codes.dtype),
            pltpu.VMEM(values.shape, values.dtype),
            pltpu.VMEM((slots * PAIR, LANES), jnp.float32),
            pltpu.SemaphoreType.DMA((STEPS,)),
            pltpu.SemaphoreType.DMA,
        ],
        cost_estimate=pl.CostEstimate(flops=0, bytes_accessed=4 * slots * BLK * BLK, transcendentals=0),
        compiler_params=pltpu.CompilerParams(vmem_limit_bytes=48 * MIB),
        name="relayout",
    )(count, codes, values)


def table_kernel(*refs):
    parts, table = refs[:-1], refs[-1]

    def build(q, carry):
        at = pl.ds(pl.multiple_of(q * LANES, LANES), LANES)
        x = [part[:, at].astype(jnp.float32) for part in parts]
        table[at, :] = jnp.concatenate(x, axis=0).T.astype(table.dtype)
        return carry

    lax.fori_loop(0, table.shape[0] // LANES, build, 0, unroll=4)


def make_table(parts):
    nodes = parts[0].shape[1]
    return pl.pallas_call(
        table_kernel,
        in_specs=[VMEM] * len(parts),
        out_specs=VMEM,
        out_shape=jax.ShapeDtypeStruct((nodes, LANES), jnp.bfloat16),
        compiler_params=pltpu.CompilerParams(vmem_limit_bytes=4 * MIB),
        cost_estimate=pl.CostEstimate(flops=0, bytes_accessed=nodes * LANES * 3, transcendentals=0),
        name="table",
    )(*parts)


def product_kernel(trash, group, words_ref, blocks_ref, table_ref, *outs):
    pending, acc = outs[-1], outs[-2]
    bounds = words_ref.shape[1] - 8 + group
    start, end = words_ref[0, bounds], words_ref[0, bounds + 1]
    acc[...] = jnp.zeros_like(acc)

    def add(first):
        for u in range(UNROLL):
            i = first + u
            word = words_ref[0, jnp.maximum(i, 0)]
            place = jnp.where((i >= start) & (i < end), word & ((1 << SOURCE_AT) - 1), trash)
            rows = pl.ds(pl.multiple_of(place * PAIR, PAIR), PAIR)
            acc[rows, :] = acc[rows, :] + pending[u * PAIR : (u + 1) * PAIR, :]

    def step(g, carry):
        first = start + g * UNROLL
        products = []
        for u in range(UNROLL):
            word = words_ref[0, first + u]
            block = blocks_ref[pl.ds(pl.multiple_of((word >> SLOT_AT) * PAIR, PAIR), PAIR), :]
            source = (word >> SOURCE_AT) & ((1 << (SLOT_AT - SOURCE_AT)) - 1)
            part = table_ref[pl.ds(pl.multiple_of(source * BLK, BLK), BLK), :]
            zero = jnp.zeros_like(part)
            right = jnp.concatenate([jnp.concatenate([part, zero], axis=1), jnp.concatenate([zero, part], axis=1)], axis=0)
            products.append(jnp.dot(block, right, preferred_element_type=jnp.float32))
        add(first - UNROLL)
        for u in range(UNROLL):
            pending[u * PAIR : (u + 1) * PAIR, :] = products[u]
        return carry

    groups = (end - start + (UNROLL - 1)) // UNROLL
    lax.fori_loop(0, groups, step, 0)
    add(start + (groups - 1) * UNROLL)
    if len(outs) > 2:
        outs[0][...] = acc[: trash * PAIR, :].astype(outs[0].dtype)


def product(group, words, blocks, table, trash, sent):
    full = jax.ShapeDtypeStruct(((trash + 1) * PAIR, 2 * LANES), jnp.float32)
    out = jax.ShapeDtypeStruct((trash * PAIR, 2 * LANES), jnp.bfloat16) if sent else full
    sums = [pltpu.VMEM(full.shape, full.dtype)] if sent else []
    return pl.pallas_call(
        functools.partial(product_kernel, trash, group),
        in_specs=[SMEM, VMEM, VMEM],
        out_specs=VMEM,
        out_shape=out,
        scratch_shapes=sums + [pltpu.VMEM((UNROLL * PAIR, 2 * LANES), jnp.float32)],
        compiler_params=pltpu.CompilerParams(vmem_limit_bytes=8 * MIB),
        cost_estimate=pl.CostEstimate(flops=1, bytes_accessed=1, transcendentals=0),
        name="product_send" if sent else "product_keep",
    )(words, blocks, table)


def add_kernel(keep_ref, got_ref, next_ref, send_ref):
    half = next_ref.shape[0]
    next_ref[...] = keep_ref[:half, :] + got_ref[:half, :].astype(jnp.float32)
    send_ref[...] = (keep_ref[half:, :] + got_ref[half:, :].astype(jnp.float32)).astype(send_ref.dtype)


def add_halves(keep, which, got):
    rows, lanes = got.shape
    block = lambda n, i: pl.BlockSpec((n, lanes), lambda _: (i, 0))
    return pl.pallas_call(
        add_kernel,
        grid=(1,),
        in_specs=[block(rows, which), block(rows, 0)],
        out_specs=(block(rows // 2, 0), block(rows // 2, 0)),
        out_shape=(
            jax.ShapeDtypeStruct((rows // 2, lanes), jnp.float32),
            jax.ShapeDtypeStruct((rows // 2, lanes), jnp.bfloat16),
        ),
        compiler_params=pltpu.CompilerParams(vmem_limit_bytes=4 * MIB),
        cost_estimate=pl.CostEstimate(flops=rows * lanes, bytes_accessed=MIB, transcendentals=0),
        name="add",
    )(keep, got)


def layer_kernel(index, *refs):
    sums, (weight_ref, bias_ref, out_ref, wide, left, right) = refs[:-6], refs[-6:]
    r = lax.axis_index("row")
    wide[...] = weight_ref[...].astype(jnp.float32)
    size = wide.shape[0] // len(index)
    pieces = [wide[pl.ds(pl.multiple_of((r ^ i) * size, size), size), :] for i in index]
    weight = jnp.concatenate(pieces, axis=0).astype(jnp.bfloat16)
    rows = sums[0].shape[0]
    for k in range(len(sums) // 2):
        keep, got = sums[2 * k], sums[2 * k + 1]
        aggregated = (keep[...] + got[...].astype(jnp.float32)).astype(jnp.bfloat16)
        for h in range(2):
            part = aggregated[:, h * LANES : (h + 1) * LANES]
            hidden = jnp.dot(part, weight, preferred_element_type=jnp.float32) + bias_ref[...]
            hidden = jnp.maximum(hidden, 0.0)
            left[pl.ds(2 * rows * k + h, rows, stride=2), :] = hidden[:, :LANES]
            right[pl.ds(2 * rows * k + h, rows, stride=2), :] = hidden[:, LANES:]
    out_ref[:, :LANES] = left[...].astype(out_ref.dtype)
    out_ref[:, LANES:] = right[...].astype(out_ref.dtype)


def layer(index, sums, weight, bias):
    rows = len(sums) * sums[0].shape[0]
    return pl.pallas_call(
        functools.partial(layer_kernel, index),
        out_shape=jax.ShapeDtypeStruct((rows, weight.shape[1]), jnp.bfloat16),
        scratch_shapes=[pltpu.VMEM(weight.shape, jnp.float32)] + [pltpu.VMEM((rows, LANES), jnp.float32)] * 2,
        compiler_params=pltpu.CompilerParams(vmem_limit_bytes=8 * MIB),
        name="layer",
    )(*sums, weight, bias)


def exchange(x, axis, size, bit):
    return lax.ppermute(x, axis, [(i, i ^ (1 << bit)) for i in range(size)])


def shards(n_row, n_col, features, block_codes, block_count, block_values, weight, bias):
    top, col_axis_bits = log2(n_row) - 1, list(range(log2(n_col)))
    col_blocks = features.shape[0] // BLK
    row_total = col_blocks * n_col // n_row
    per = row_total // n_col

    z_first, x_first = tuple(col_axis_bits[1:] + col_axis_bits[:1]), tuple(col_axis_bits)
    orders = (x_first, z_first, x_first, x_first)
    chunks = len(orders)
    half = row_total // (2 * chunks)

    mine = features.T
    other = exchange(mine, "row", n_row, top)
    blocks, words = relayout(orders, per, log2(col_blocks), block_count, block_codes, block_values[0])
    other, blocks = lax.optimization_barrier((other, blocks))
    parts, index = [mine, other], [0, 1 << top]
    for bit in range(top):
        parts = parts + [exchange(p, "row", n_row, bit) for p in parts]
        index = index + [i ^ (1 << bit) for i in index]

    table = make_table(parts)
    sends = [product(k, words, blocks, table, half, True) for k in range(chunks)]
    kept = product(chunks, words, blocks, table, chunks * half, False)
    keeps = [(kept, k) for k in range(chunks)]
    for k in range(len(col_axis_bits)):
        for i in range(chunks):
            got = exchange(sends[i], "col", n_col, orders[i][k])
            if k < len(col_axis_bits) - 1:
                total, sends[i] = add_halves(*keeps[i], got)
                keeps[i] = (total, 0)
            else:
                keeps[i], sends[i] = keeps[i][0], got
    sums = [x for i in range(chunks) for x in (keeps[i], sends[i])]
    return layer(tuple(index), sums, weight, bias[None, :])


def solution(mesh):
    in_specs = (P("col", "row"), P("row", "col"), P("row", "col"), P("row", "col", None), P(), P())
    out_specs = P(("row", "col"), None)
    body = functools.partial(shards, mesh.shape["row"], mesh.shape["col"])
    return jax.shard_map(body, mesh=mesh, in_specs=in_specs, out_specs=out_specs, check_vma=False)
```

time: 49.4 us -> 48.8 us (0.988); the launches traced: 49.7 us -> 48.6 us
  Pallas kernels: 22 us -> 11.3 us
  starting transfers between devices: 17.2 us -> 25.1 us
  waiting for transfers between devices: 8.92 us -> 10.7 us
    pallas_call x6 -> x5, Pallas kernels: 15.3 us -> 5.49 us  [product(): pl.pallas_call(functools.partial(product_kernel, trash, group), in_specs=...]
    ppermute x15, starting transfers between devices: 17.2 us -> 25.1 us  [exchange(): return lax.ppermute(x, axis, [(i, i ^ 1 << bit) for i in range(size)])]
    ppermute x15, waiting for transfers between devices: 8.92 us -> 10.7 us  [exchange(): return lax.ppermute(x, axis, [(i, i ^ 1 << bit) for i in range(size)])]
    pallas_call x2 -> x1, Pallas kernels: 1.85 us -> 0.92 us  [make_table(): pl.pallas_call(table_kernel, in_specs=[VMEM] * len(parts), out_specs=VMEM...]
  transfers between devices with their start and end apart: 15 -> 15, of which waited for: 4 -> 5; matrix products, arithmetic and copies ran while one was open for 0% -> 0% of each run, Pallas kernels for 42% -> 17%
where the time goes in v2:
time: 48.8 us; the launch traced here: 48.6 us
  starting transfers between devices  25.1 us (51%)
  Pallas kernels  11.3 us (23%)
  waiting for transfers between devices  10.7 us (22%)
  between operations  0.77 us (2%)
  local copies, waits for them, and re-layouts  0.69 us (1%)
    ppermute x15, starting transfers between devices, exchange(): return lax.ppermute(x, axis, [(i, i ^ 1 << bit) for i in range(size)])  25.1 us
    ppermute x15, waiting for transfers between devices, exchange(): return lax.ppermute(x, axis, [(i, i ^ 1 << bit) for i in range(size)])  10.7 us
    pallas_call x5, Pallas kernels, product(): pl.pallas_call(functools.partial(product_kernel, trash, group), in_specs=...  5.49 us
    pallas_call x1, Pallas kernels, relayout(): pl.pallas_call(functools.partial(relayout_kernel, orders, per, col_bits),...  3.37 us
    pallas_call x1, Pallas kernels, layer(): pl.pallas_call(functools.partial(layer_kernel, index), out_shape=jax.Shap...  1.17 us
  transfers between devices with their start and end apart: 15, of which 5 were waited for; matrix products, arithmetic and copies ran while one was open for 0% of the time, Pallas kernels for 17%

profile of v2, /device:TPU:0, one launch (start us, length us, event | category | flops | bytes accessed | tf_op | source)
XLA Modules:
  0.0 48.6 jit_solution(7830737382758590547)
XLA Ops:
  0.0 3.0 %collective-permute-start = (bf16[32,4096]{1,0:T(8,128)(2,1)}, bf16[32,4096]{1,0:T(8,128)(2,1)S(1)}, u32[]{:S(2)}, u32[]{:S(2)}) collective-permute-start(bf16[32,4096]{1,0:T(8,128)(2,1)} %bitcast.3), channel_id=1, source_target_pairs={{0,16},{8,24},{16,0},{24,8},{1,17},{9,25},{17,1},{25,9},{2,18},{10... | collective-permute-start | bytes 786440 | tf_op jit(solution)/shard_map/ppermute | solution.py:252
  3.0 0.0 collective-permute-start.1
  3.6 0.7 %copy-done.2 = s32[1,384]{1,0:T(1,128)S(1)} copy-done((s32[1,384]{1,0:T(1,128)S(1)}, s32[1,384]{1,0:T(1,128)}, u32[]{:S(2)}) %copy-start.2) | copy-done | bytes 1560
  4.3 3.4 %relayout.1 = (bf16[12288,128]{1,0:T(8,128)(2,1)S(1)}, s32[1,512]{1,0:T(1,128)S(1)}) custom-call(s32[1,1]{1,0:T(1,128)S(6)} %copy.7.count_ref, s32[1,384]{1,0:T(1,128)S(1)} %copy-done.2, bf16[384,4096]{1,0:T(8,128)(2,1)} %bitcast.7), custom_call_target="tpu_custom_call" | custom-call | bytes 6291456 | tf_op jit(solution)/shard_map/relayout/pallas_call | solution.py:96
  7.7 1.9 %collective-permute-done.refs_1_ = bf16[32,4096]{1,0:T(8,128)(2,1)S(1)} collective-permute-done((bf16[32,4096]{1,0:T(8,128)(2,1)}, bf16[32,4096]{1,0:T(8,128)(2,1)S(1)}, u32[]{:S(2)}, u32[]{:S(2)}) %collective-permute-start) | collective-permute-done | bytes 262176 | tf_op jit(solution)/shard_map/ppermute | solution.py:252
  9.6 1.5 %collective-permute-done.2.refs_3_ = bf16[32,4096]{1,0:T(8,128)(2,1)S(1)} collective-permute-done((bf16[32,4096]{1,0:T(8,128)(2,1)S(1)}, bf16[32,4096]{1,0:T(8,128)(2,1)S(1)}, u32[]{:S(2)}, u32[]{:S(2)}) %collective-permute-start.2) | collective-permute-done | bytes 262176 | tf_op jit(solution)/shard_map/ppermute | solution.py:252
  11.1 0.9 %table.1.table_ref = bf16[4096,128]{1,0:T(8,128)(2,1)S(1)} custom-call(bf16[32,4096]{1,0:T(8,128)(2,1)S(1)} %bitcast.5, bf16[32,4096]{1,0:T(8,128)(2,1)S(1)} %collective-permute-done.refs_1_, bf16[32,4096]{1,0:T(8,128)(2,1)S(1)} %collective-permute-done.1.refs_2_, bf16[32,4096]{1,0:T(8,128)(2,1)S(1)} %collective-permute-done.2.refs_3_), custom_call_target="tpu_custom_call" | custom-call | bytes 1572864 | tf_op jit(solution)/shard_map/table/pallas_call | solution.py:131
  12.0 1.0 %product_send.4 = bf16[512,256]{1,0:T(8,128)(2,1)S(1)} custom-call(s32[1,512]{1,0:T(1,128)S(1)} %get-tuple-element.25.words_ref, bf16[12288,128]{1,0:T(8,128)(2,1)S(1)} %get-tuple-element.27.blocks_ref, bf16[4096,128]{1,0:T(8,128)(2,1)S(1)} %table.1.table_ref), custom_call_target="tpu_custom_call" | custom-call | flops 1 | bytes 1 | tf_op jit(solution)/shard_map/product_send/pallas_call | solution.py:183
  13.1 1.4 %collective-permute-start.3 = (bf16[512,256]{1,0:T(8,128)(2,1)S(1)}, bf16[512,256]{1,0:T(8,128)(2,1)S(1)}, u32[]{:S(2)}, u32[]{:S(2)}) collective-permute-start(bf16[512,256]{1,0:T(8,128)(2,1)S(1)} %product_send.4), channel_id=1, source_target_pairs={{0,1},{1,0},{2,3},{3,2},{4,5},{5,4},{6,7},{7,6},{8,9},{9,8},{10,11... | collective-permute-start | bytes 786440 | tf_op jit(solution)/shard_map/ppermute | solution.py:252
  14.5 1.0 %product_send.5 = bf16[512,256]{1,0:T(8,128)(2,1)S(1)} custom-call(s32[1,512]{1,0:T(1,128)S(1)} %get-tuple-element.25.words_ref, bf16[12288,128]{1,0:T(8,128)(2,1)S(1)} %get-tuple-element.27.blocks_ref, bf16[4096,128]{1,0:T(8,128)(2,1)S(1)} %table.1.table_ref), custom_call_target="tpu_custom_call" | custom-call | flops 1 | bytes 1 | tf_op jit(solution)/shard_map/product_send/pallas_call | solution.py:183
  15.5 1.9 %collective-permute-start.6 = (bf16[512,256]{1,0:T(8,128)(2,1)S(1)}, bf16[512,256]{1,0:T(8,128)(2,1)S(1)}, u32[]{:S(2)}, u32[]{:S(2)}) collective-permute-start(bf16[512,256]{1,0:T(8,128)(2,1)S(1)} %product_send.5), channel_id=1, source_target_pairs={{0,2},{1,3},{2,0},{3,1},{4,6},{5,7},{6,4},{7,5},{8,10},{9,11},{10,... | collective-permute-start | bytes 786440 | tf_op jit(solution)/shard_map/ppermute | solution.py:252
  17.4 1.0 %product_send.6 = bf16[512,256]{1,0:T(8,128)(2,1)S(1)} custom-call(s32[1,512]{1,0:T(1,128)S(1)} %get-tuple-element.25.words_ref, bf16[12288,128]{1,0:T(8,128)(2,1)S(1)} %get-tuple-element.27.blocks_ref, bf16[4096,128]{1,0:T(8,128)(2,1)S(1)} %table.1.table_ref), custom_call_target="tpu_custom_call" | custom-call | flops 1 | bytes 1 | tf_op jit(solution)/shard_map/product_send/pallas_call | solution.py:183
  18.5 0.6 %collective-permute-start.9 = (bf16[512,256]{1,0:T(8,128)(2,1)S(1)}, bf16[512,256]{1,0:T(8,128)(2,1)S(1)}, u32[]{:S(2)}, u32[]{:S(2)}) collective-permute-start(bf16[512,256]{1,0:T(8,128)(2,1)S(1)} %product_send.6), channel_id=1, source_target_pairs={{0,1},{1,0},{2,3},{3,2},{4,5},{5,4},{6,7},{7,6},{8,9},{9,8},{10,11... | collective-permute-start | bytes 786440 | tf_op jit(solution)/shard_map/ppermute | solution.py:252
  19.1 1.0 %product_send.7 = bf16[512,256]{1,0:T(8,128)(2,1)S(1)} custom-call(s32[1,512]{1,0:T(1,128)S(1)} %get-tuple-element.25.words_ref, bf16[12288,128]{1,0:T(8,128)(2,1)S(1)} %get-tuple-element.27.blocks_ref, bf16[4096,128]{1,0:T(8,128)(2,1)S(1)} %table.1.table_ref), custom_call_target="tpu_custom_call" | custom-call | flops 1 | bytes 1 | tf_op jit(solution)/shard_map/product_send/pallas_call | solution.py:183
  20.1 1.3 %collective-permute-start.12 = (bf16[512,256]{1,0:T(8,128)(2,1)S(1)}, bf16[512,256]{1,0:T(8,128)(2,1)S(1)}, u32[]{:S(2)}, u32[]{:S(2)}) collective-permute-start(bf16[512,256]{1,0:T(8,128)(2,1)S(1)} %product_send.7), channel_id=1, source_target_pairs={{0,1},{1,0},{2,3},{3,2},{4,5},{5,4},{6,7},{7,6},{8,9},{9,8},{10,11... | collective-permute-start | bytes 786440 | tf_op jit(solution)/shard_map/ppermute | solution.py:252
  21.4 1.4 %product_keep.1.keep_ref = f32[2080,256]{1,0:T(8,128)S(1)} custom-call(s32[1,512]{1,0:T(1,128)S(1)} %get-tuple-element.25.words_ref, bf16[12288,128]{1,0:T(8,128)(2,1)S(1)} %get-tuple-element.27.blocks_ref, bf16[4096,128]{1,0:T(8,128)(2,1)S(1)} %table.1.table_ref), custom_call_target="tpu_custom_call" | custom-call | flops 1 | bytes 1 | tf_op jit(solution)/shard_map/product_keep/pallas_call | solution.py:183
  22.8 0.1 add.8
  22.8 1.6 %collective-permute-start.4 = (bf16[256,256]{1,0:T(8,128)(2,1)S(1)}, bf16[256,256]{1,0:T(8,128)(2,1)S(1)}, u32[]{:S(2)}, u32[]{:S(2)}) collective-permute-start(bf16[256,256]{1,0:T(8,128)(2,1)S(1)} %get-tuple-element.30), channel_id=1, source_target_pairs={{0,2},{1,3},{2,0},{3,1},{4,6},{5,7},{6,4},{7,5},{8,10},{9,11},{10,... | collective-permute-start | bytes 393224 | tf_op jit(solution)/shard_map/ppermute | solution.py:252
  24.5 0.1 add.10
  24.5 0.0 copy-start.1
  24.5 0.0 copy-start.3
  24.5 3.2 %collective-permute-start.7 = (bf16[256,256]{1,0:T(8,128)(2,1)S(1)}, bf16[256,256]{1,0:T(8,128)(2,1)S(1)}, u32[]{:S(2)}, u32[]{:S(2)}) collective-permute-start(bf16[256,256]{1,0:T(8,128)(2,1)S(1)} %get-tuple-element.34), channel_id=1, source_target_pairs={{0,4},{1,5},{2,6},{3,7},{4,0},{5,1},{6,2},{7,3},{8,12},{9,13},{10,... | collective-permute-start | bytes 393224 | tf_op jit(solution)/shard_map/ppermute | solution.py:252
  27.8 2.2 %collective-permute-start.10 = (bf16[256,256]{1,0:T(8,128)(2,1)S(1)}, bf16[256,256]{1,0:T(8,128)(2,1)S(1)}, u32[]{:S(2)}, u32[]{:S(2)}) collective-permute-start(bf16[256,256]{1,0:T(8,128)(2,1)S(1)} %get-tuple-element.38), channel_id=1, source_target_pairs={{0,2},{1,3},{2,0},{3,1},{4,6},{5,7},{6,4},{7,5},{8,10},{9,11},{10,... | collective-permute-start | bytes 393224 | tf_op jit(solution)/shard_map/ppermute | solution.py:252
  30.1 2.4 %collective-permute-done.12.got_ref = bf16[512,256]{1,0:T(8,128)(2,1)S(1)} collective-permute-done((bf16[512,256]{1,0:T(8,128)(2,1)S(1)}, bf16[512,256]{1,0:T(8,128)(2,1)S(1)}, u32[]{:S(2)}, u32[]{:S(2)}) %collective-permute-start.12) | collective-permute-done | bytes 262176 | tf_op jit(solution)/shard_map/ppermute | solution.py:252
  32.5 2.1 %collective-permute-start.13 = (bf16[256,256]{1,0:T(8,128)(2,1)S(1)}, bf16[256,256]{1,0:T(8,128)(2,1)S(1)}, u32[]{:S(2)}, u32[]{:S(2)}) collective-permute-start(bf16[256,256]{1,0:T(8,128)(2,1)S(1)} %get-tuple-element.42), channel_id=1, source_target_pairs={{0,2},{1,3},{2,0},{3,1},{4,6},{5,7},{6,4},{7,5},{8,10},{9,11},{10,... | collective-permute-start | bytes 393224 | tf_op jit(solution)/shard_map/ppermute | solution.py:252
  34.6 2.7 %collective-permute-start.5 = (bf16[128,256]{1,0:T(8,128)(2,1)S(1)}, bf16[128,256]{1,0:T(8,128)(2,1)S(1)}, u32[]{:S(2)}, u32[]{:S(2)}) collective-permute-start(bf16[128,256]{1,0:T(8,128)(2,1)S(1)} %get-tuple-element.32), channel_id=1, source_target_pairs={{0,4},{1,5},{2,6},{3,7},{4,0},{5,1},{6,2},{7,3},{8,12},{9,13},{10,... | collective-permute-start | bytes 196616 | tf_op jit(solution)/shard_map/ppermute | solution.py:252
  37.3 1.6 %collective-permute-start.8 = (bf16[128,256]{1,0:T(8,128)(2,1)S(1)}, bf16[128,256]{1,0:T(8,128)(2,1)S(1)}, u32[]{:S(2)}, u32[]{:S(2)}) collective-permute-start(bf16[128,256]{1,0:T(8,128)(2,1)S(1)} %get-tuple-element.36), channel_id=1, source_target_pairs={{0,1},{1,0},{2,3},{3,2},{4,5},{5,4},{6,7},{7,6},{8,9},{9,8},{10,11... | collective-permute-start | bytes 196616 | tf_op jit(solution)/shard_map/ppermute | solution.py:252
  38.9 0.4 collective-permute-start.11
  39.3 3.2 %collective-permute-start.14 = (bf16[128,256]{1,0:T(8,128)(2,1)S(1)}, bf16[128,256]{1,0:T(8,128)(2,1)S(1)}, u32[]{:S(2)}, u32[]{:S(2)}) collective-permute-start(bf16[128,256]{1,0:T(8,128)(2,1)S(1)} %get-tuple-element.44), channel_id=1, source_target_pairs={{0,4},{1,5},{2,6},{3,7},{4,0},{5,1},{6,2},{7,3},{8,12},{9,13},{10,... | collective-permute-start | bytes 196616 | tf_op jit(solution)/shard_map/ppermute | solution.py:252
  42.5 4.2 %collective-permute-done.11.refs_5_ = bf16[128,256]{1,0:T(8,128)(2,1)S(1)} collective-permute-done((bf16[128,256]{1,0:T(8,128)(2,1)S(1)}, bf16[128,256]{1,0:T(8,128)(2,1)S(1)}, u32[]{:S(2)}, u32[]{:S(2)}) %collective-permute-start.11) | collective-permute-done | bytes 65568 | tf_op jit(solution)/shard_map/ppermute | solution.py:252
  46.7 0.7 %collective-permute-done.14.refs_7_ = bf16[128,256]{1,0:T(8,128)(2,1)S(1)} collective-permute-done((bf16[128,256]{1,0:T(8,128)(2,1)S(1)}, bf16[128,256]{1,0:T(8,128)(2,1)S(1)}, u32[]{:S(2)}, u32[]{:S(2)}) %collective-permute-start.14) | collective-permute-done | bytes 65568 | tf_op jit(solution)/shard_map/ppermute | solution.py:252
  47.4 1.2 %layer.1 = bf16[1024,256]{1,0:T(8,128)(2,1)} custom-call(f32[128,256]{1,0:T(8,128)S(1)} %get-tuple-element.31.refs_0_, bf16[128,256]{1,0:T(8,128)(2,1)S(1)} %collective-permute-done.5.refs_1_, f32[128,256]{1,0:T(8,128)S(1)} %get-tuple-element.35.refs_2_, bf16[128,256]{1,0:T(8,128)(2,1)S(1)} %collective-permute-done.8.refs_3_, ...), custom_call_target="tpu_custom_call" | custom-call | tf_op jit(solution)/shard_map/layer/pallas_call | solution.py:242
  (22 shorter events, 0.2 us)
Async XLA Ops:
  0.0 11.1 %copy-start = (bf16[4096,32]{0,1:T(8,128)(2,1)S(1)}, bf16[4096,32]{0,1:T(8,128)(2,1)}, u32[]{:S(2)}) copy-start(bf16[4096,32]{0,1:T(8,128)(2,1)} %param.6) | copy-start | bytes 786436
  0.0 9.6 %collective-permute-start = (bf16[32,4096]{1,0:T(8,128)(2,1)}, bf16[32,4096]{1,0:T(8,128)(2,1)S(1)}, u32[]{:S(2)}, u32[]{:S(2)}) collective-permute-start(bf16[32,4096]{1,0:T(8,128)(2,1)} %bitcast.3), channel_id=1, source_target_pairs={{0,16},{8,24},{16,0},{24,8},{1,17},{9,25},{17,1},{25,9},{2,18},{10... | collective-permute-start | bytes 786440 | tf_op jit(solution)/shard_map/ppermute | solution.py:252
  3.0 6.6 %collective-permute-start.1 = (bf16[32,4096]{1,0:T(8,128)(2,1)}, bf16[32,4096]{1,0:T(8,128)(2,1)S(1)}, u32[]{:S(2)}, u32[]{:S(2)}) collective-permute-start(bf16[32,4096]{1,0:T(8,128)(2,1)} %bitcast.4), channel_id=1, source_target_pairs={{0,8},{8,0},{16,24},{24,16},{1,9},{9,1},{17,25},{25,17},{2,10},{10... | collective-permute-start | bytes 786440 | tf_op jit(solution)/shard_map/ppermute | solution.py:252
  3.6 0.7 %copy-start.2 = (s32[1,384]{1,0:T(1,128)S(1)}, s32[1,384]{1,0:T(1,128)}, u32[]{:S(2)}) copy-start(s32[1,384]{1,0:T(1,128)} %codes_hbm.1) | copy-start | bytes 4612
  9.6 1.5 %collective-permute-start.2 = (bf16[32,4096]{1,0:T(8,128)(2,1)S(1)}, bf16[32,4096]{1,0:T(8,128)(2,1)S(1)}, u32[]{:S(2)}, u32[]{:S(2)}) collective-permute-start(bf16[32,4096]{1,0:T(8,128)(2,1)S(1)} %collective-permute-done.refs_1_), channel_id=1, source_target_pairs={{0,8},{8,0},{16,24},{24,16},{1,9},{9,1},{17,25},{25,17},{2,10},{10... | collective-permute-start | bytes 786440 | tf_op jit(solution)/shard_map/ppermute | solution.py:252
  13.1 9.7 %collective-permute-start.3 = (bf16[512,256]{1,0:T(8,128)(2,1)S(1)}, bf16[512,256]{1,0:T(8,128)(2,1)S(1)}, u32[]{:S(2)}, u32[]{:S(2)}) collective-permute-start(bf16[512,256]{1,0:T(8,128)(2,1)S(1)} %product_send.4), channel_id=1, source_target_pairs={{0,1},{1,0},{2,3},{3,2},{4,5},{5,4},{6,7},{7,6},{8,9},{9,8},{10,11... | collective-permute-start | bytes 786440 | tf_op jit(solution)/shard_map/ppermute | solution.py:252
  15.5 8.9 %collective-permute-start.6 = (bf16[512,256]{1,0:T(8,128)(2,1)S(1)}, bf16[512,256]{1,0:T(8,128)(2,1)S(1)}, u32[]{:S(2)}, u32[]{:S(2)}) collective-permute-start(bf16[512,256]{1,0:T(8,128)(2,1)S(1)} %product_send.5), channel_id=1, source_target_pairs={{0,2},{1,3},{2,0},{3,1},{4,6},{5,7},{6,4},{7,5},{8,10},{9,11},{10,... | collective-permute-start | bytes 786440 | tf_op jit(solution)/shard_map/ppermute | solution.py:252
  18.5 9.3 %collective-permute-start.9 = (bf16[512,256]{1,0:T(8,128)(2,1)S(1)}, bf16[512,256]{1,0:T(8,128)(2,1)S(1)}, u32[]{:S(2)}, u32[]{:S(2)}) collective-permute-start(bf16[512,256]{1,0:T(8,128)(2,1)S(1)} %product_send.6), channel_id=1, source_target_pairs={{0,1},{1,0},{2,3},{3,2},{4,5},{5,4},{6,7},{7,6},{8,9},{9,8},{10,11... | collective-permute-start | bytes 786440 | tf_op jit(solution)/shard_map/ppermute | solution.py:252
  20.1 12.3 %collective-permute-start.12 = (bf16[512,256]{1,0:T(8,128)(2,1)S(1)}, bf16[512,256]{1,0:T(8,128)(2,1)S(1)}, u32[]{:S(2)}, u32[]{:S(2)}) collective-permute-start(bf16[512,256]{1,0:T(8,128)(2,1)S(1)} %product_send.7), channel_id=1, source_target_pairs={{0,1},{1,0},{2,3},{3,2},{4,5},{5,4},{6,7},{7,6},{8,9},{9,8},{10,11... | collective-permute-start | bytes 786440 | tf_op jit(solution)/shard_map/ppermute | solution.py:252
  22.8 11.7 %collective-permute-start.4 = (bf16[256,256]{1,0:T(8,128)(2,1)S(1)}, bf16[256,256]{1,0:T(8,128)(2,1)S(1)}, u32[]{:S(2)}, u32[]{:S(2)}) collective-permute-start(bf16[256,256]{1,0:T(8,128)(2,1)S(1)} %get-tuple-element.30), channel_id=1, source_target_pairs={{0,2},{1,3},{2,0},{3,1},{4,6},{5,7},{6,4},{7,5},{8,10},{9,11},{10,... | collective-permute-start | bytes 393224 | tf_op jit(solution)/shard_map/ppermute | solution.py:252
  24.5 22.9 %copy-start.1 = (bf16[128,256]{1,0:T(8,128)(2,1)S(1)}, bf16[128,256]{1,0:T(8,128)(2,1)}, u32[]{:S(2)}) copy-start(bf16[128,256]{1,0:T(8,128)(2,1)} %refs_8_.1) | copy-start | bytes 196612
  24.5 22.9 %copy-start.3 = (f32[256]{0:T(256)S(1)}, f32[256]{0:T(256)}, u32[]{:S(2)}) copy-start(f32[256]{0:T(256)} %param.11) | copy-start | bytes 3076
  24.5 12.7 %collective-permute-start.7 = (bf16[256,256]{1,0:T(8,128)(2,1)S(1)}, bf16[256,256]{1,0:T(8,128)(2,1)S(1)}, u32[]{:S(2)}, u32[]{:S(2)}) collective-permute-start(bf16[256,256]{1,0:T(8,128)(2,1)S(1)} %get-tuple-element.34), channel_id=1, source_target_pairs={{0,4},{1,5},{2,6},{3,7},{4,0},{5,1},{6,2},{7,3},{8,12},{9,13},{10,... | collective-permute-start | bytes 393224 | tf_op jit(solution)/shard_map/ppermute | solution.py:252
  27.8 11.0 %collective-permute-start.10 = (bf16[256,256]{1,0:T(8,128)(2,1)S(1)}, bf16[256,256]{1,0:T(8,128)(2,1)S(1)}, u32[]{:S(2)}, u32[]{:S(2)}) collective-permute-start(bf16[256,256]{1,0:T(8,128)(2,1)S(1)} %get-tuple-element.38), channel_id=1, source_target_pairs={{0,2},{1,3},{2,0},{3,1},{4,6},{5,7},{6,4},{7,5},{8,10},{9,11},{10,... | collective-permute-start | bytes 393224 | tf_op jit(solution)/shard_map/ppermute | solution.py:252
  32.5 6.8 %collective-permute-start.13 = (bf16[256,256]{1,0:T(8,128)(2,1)S(1)}, bf16[256,256]{1,0:T(8,128)(2,1)S(1)}, u32[]{:S(2)}, u32[]{:S(2)}) collective-permute-start(bf16[256,256]{1,0:T(8,128)(2,1)S(1)} %get-tuple-element.42), channel_id=1, source_target_pairs={{0,2},{1,3},{2,0},{3,1},{4,6},{5,7},{6,4},{7,5},{8,10},{9,11},{10,... | collective-permute-start | bytes 393224 | tf_op jit(solution)/shard_map/ppermute | solution.py:252
  34.6 7.9 %collective-permute-start.5 = (bf16[128,256]{1,0:T(8,128)(2,1)S(1)}, bf16[128,256]{1,0:T(8,128)(2,1)S(1)}, u32[]{:S(2)}, u32[]{:S(2)}) collective-permute-start(bf16[128,256]{1,0:T(8,128)(2,1)S(1)} %get-tuple-element.32), channel_id=1, source_target_pairs={{0,4},{1,5},{2,6},{3,7},{4,0},{5,1},{6,2},{7,3},{8,12},{9,13},{10,... | collective-permute-start | bytes 196616 | tf_op jit(solution)/shard_map/ppermute | solution.py:252
  37.3 5.2 %collective-permute-start.8 = (bf16[128,256]{1,0:T(8,128)(2,1)S(1)}, bf16[128,256]{1,0:T(8,128)(2,1)S(1)}, u32[]{:S(2)}, u32[]{:S(2)}) collective-permute-start(bf16[128,256]{1,0:T(8,128)(2,1)S(1)} %get-tuple-element.36), channel_id=1, source_target_pairs={{0,1},{1,0},{2,3},{3,2},{4,5},{5,4},{6,7},{7,6},{8,9},{9,8},{10,11... | collective-permute-start | bytes 196616 | tf_op jit(solution)/shard_map/ppermute | solution.py:252
  38.9 7.8 %collective-permute-start.11 = (bf16[128,256]{1,0:T(8,128)(2,1)S(1)}, bf16[128,256]{1,0:T(8,128)(2,1)S(1)}, u32[]{:S(2)}, u32[]{:S(2)}) collective-permute-start(bf16[128,256]{1,0:T(8,128)(2,1)S(1)} %get-tuple-element.40), channel_id=1, source_target_pairs={{0,4},{1,5},{2,6},{3,7},{4,0},{5,1},{6,2},{7,3},{8,12},{9,13},{10,... | collective-permute-start | bytes 196616 | tf_op jit(solution)/shard_map/ppermute | solution.py:252
  39.3 8.1 %collective-permute-start.14 = (bf16[128,256]{1,0:T(8,128)(2,1)S(1)}, bf16[128,256]{1,0:T(8,128)(2,1)S(1)}, u32[]{:S(2)}, u32[]{:S(2)}) collective-permute-start(bf16[128,256]{1,0:T(8,128)(2,1)S(1)} %get-tuple-element.44), channel_id=1, source_target_pairs={{0,4},{1,5},{2,6},{3,7},{4,0},{5,1},{6,2},{7,3},{8,12},{9,13},{10,... | collective-permute-start | bytes 196616 | tf_op jit(solution)/shard_map/ppermute | solution.py:252

commit v3 on v2

v3 whole, which is shorter than its diff:
```python
import functools

import jax
import jax.numpy as jnp
from jax import lax
from jax.experimental import pallas as pl
from jax.experimental.pallas import tpu as pltpu
from jax.sharding import PartitionSpec as P

BLK = 64
PAIR = BLK // 2
LANES = 2 * BLK
GROUP = 16
STEPS = 4
UNROLL = 16
SLOT_AT, SOURCE_AT = 13, 7
MIB = 1024 * 1024
SMEM = pl.BlockSpec(memory_space=pltpu.SMEM)
VMEM = pl.BlockSpec(memory_space=pltpu.VMEM)


def log2(size):
    return size.bit_length() - 1


def list_width(slots):
    return -(-(slots + 2 * UNROLL + 8) // LANES) * LANES


def make_lists(chunks, col_bits, count, codes, words_ref):
    slots, width = codes.shape[1], words_ref.shape[1]
    per = sum(size for size, _ in chunks)
    row_block, col_block = codes >> col_bits, codes & ((1 << col_bits) - 1)
    owner = (row_block >> log2(per)) ^ lax.axis_index("col")
    sub = row_block & (per - 1)
    number = lax.broadcasted_iota(jnp.int32, (1, slots), 1)
    live = number < count
    group, target = jnp.full_like(codes, len(chunks) + 1), jnp.zeros_like(codes)
    first, base = 0, 0
    for c, (size, order) in enumerate(chunks):
        place = jnp.zeros_like(owner)
        for k, bit in enumerate(order):
            place = place | (((owner >> bit) & 1) << (len(order) - 1 - k))
        place = (place << log2(size)) + (sub - first)
        half = size << (len(order) - 1)
        keep = place < half
        here = live & (sub >= first) & (sub < first + size)
        target = jnp.where(here, jnp.where(keep, place + base, place - half), target)
        group = jnp.where(here, jnp.where(keep, len(chunks), c), group)
        first, base = first + size, base + half
    same = lax.broadcasted_iota(jnp.int32, (slots, slots), 0) == lax.broadcasted_iota(jnp.int32, (slots, slots), 1)
    column = lambda row: jnp.sum(jnp.where(same, row, 0.0), axis=1, keepdims=True)
    spot = lax.broadcasted_iota(jnp.int32, (slots, width), 1).astype(jnp.float32)
    lane = lax.broadcasted_iota(jnp.int32, (1, width), 1)
    key = (group * slots + number).astype(jnp.float32)
    word = ((number << SLOT_AT) | (col_block << SOURCE_AT) | target).astype(jnp.float32)
    rank = jnp.sum(jnp.where(key < column(key), 1.0, 0.0), axis=1, keepdims=True)
    words = jnp.sum(jnp.where(rank == spot, column(word), 0.0), axis=0, keepdims=True).astype(jnp.int32)
    for k in range(len(chunks) + 2):
        before = jnp.sum(jnp.where(group < k, 1.0, 0.0), axis=1, keepdims=True).astype(jnp.int32)
        words = jnp.where(lane == width - 8 + k, before, words)
    words_ref[...] = words


def relayout_kernel(chunks, col_bits, count_ref, codes_hbm, values_hbm, out_ref, words_ref, codes, held, scratch, arrived, codes_arrived):
    codes_copy = pltpu.make_async_copy(codes_hbm, codes, codes_arrived)
    codes_copy.start()
    step = values_hbm.shape[0] // STEPS
    copies = []
    for k in range(STEPS):
        rows = pl.ds(k * step, step)
        copies.append(pltpu.make_async_copy(values_hbm.at[rows], held.at[rows], arrived.at[k]))
        copies[k].start()
    codes_copy.wait()
    make_lists(chunks, col_bits, count_ref[0, 0], codes[...], words_ref)

    def one(g, carry):
        slots = pl.ds(pl.multiple_of(g * GROUP, GROUP), GROUP)
        base = pl.multiple_of(g * (GROUP * PAIR), GROUP * PAIR)
        for p in range(PAIR):
            scratch[pl.ds(base + p * GROUP, GROUP), :] = held[slots, p * LANES : (p + 1) * LANES].astype(jnp.float32)
        for s in range(GROUP):
            rows = scratch[pl.ds(base + s, PAIR, stride=GROUP), :]
            out_ref[pl.ds(base + s * PAIR, PAIR), :] = rows.astype(out_ref.dtype)
        return carry

    groups = step // GROUP
    for k in range(STEPS):
        copies[k].wait()
        lax.fori_loop(k * groups, (k + 1) * groups, one, 0, unroll=2)


def relayout(chunks, col_bits, count, codes, values):
    slots = values.shape[0]
    return pl.pallas_call(
        functools.partial(relayout_kernel, chunks, col_bits),
        in_specs=[SMEM] + [pl.BlockSpec(memory_space=pltpu.HBM)] * 2,
        out_specs=(VMEM, VMEM),
        out_shape=(
            jax.ShapeDtypeStruct((slots * PAIR, LANES), values.dtype),
            jax.ShapeDtypeStruct((1, list_width(slots)), jnp.int32),
        ),
        scratch_shapes=[
            pltpu.VMEM(codes.shape, codes.dtype),
            pltpu.VMEM(values.shape, values.dtype),
            pltpu.VMEM((slots * PAIR, LANES), jnp.float32),
            pltpu.SemaphoreType.DMA((STEPS,)),
            pltpu.SemaphoreType.DMA,
        ],
        cost_estimate=pl.CostEstimate(flops=0, bytes_accessed=4 * slots * BLK * BLK, transcendentals=0),
        compiler_params=pltpu.CompilerParams(vmem_limit_bytes=48 * MIB),
        name="relayout",
    )(count, codes, values)


def table_kernel(*refs):
    parts, table = refs[:-1], refs[-1]

    def build(q, carry):
        at = pl.ds(pl.multiple_of(q * LANES, LANES), LANES)
        x = [part[:, at].astype(jnp.float32) for part in parts]
        table[at, :] = jnp.concatenate(x + x, axis=0).T.astype(table.dtype)
        return carry

    lax.fori_loop(0, table.shape[0] // LANES, build, 0, unroll=4)


def make_table(parts):
    nodes = parts[0].shape[1]
    return pl.pallas_call(
        table_kernel,
        in_specs=[VMEM] * len(parts),
        out_specs=VMEM,
        out_shape=jax.ShapeDtypeStruct((nodes, LANES), jnp.bfloat16),
        compiler_params=pltpu.CompilerParams(vmem_limit_bytes=4 * MIB),
        cost_estimate=pl.CostEstimate(flops=1, bytes_accessed=1, transcendentals=0),
        name="table",
    )(*parts)


def product_kernel(trash, group, n_tables, words_ref, blocks_ref, *refs):
    tables, outs = refs[:n_tables], refs[n_tables:]
    pending, acc = outs[-1], outs[-2]
    bounds = words_ref.shape[1] - 8 + group
    start, end = words_ref[0, bounds], words_ref[0, bounds + 1]
    low = lax.broadcasted_iota(jnp.int32, (BLK, LANES), 1) < BLK
    acc[...] = jnp.zeros_like(acc)

    def add(first):
        for u in range(UNROLL):
            i = first + u
            word = words_ref[0, jnp.maximum(i, 0)]
            place = jnp.where((i >= start) & (i < end), word & ((1 << SOURCE_AT) - 1), trash)
            rows = pl.ds(pl.multiple_of(place * PAIR, PAIR), PAIR)
            acc[rows, :] = acc[rows, :] + pending[u * PAIR : (u + 1) * PAIR, :]

    def step(g, carry):
        first = start + g * UNROLL
        products = []
        for u in range(UNROLL):
            word = words_ref[0, first + u]
            block = blocks_ref[pl.ds(pl.multiple_of((word >> SLOT_AT) * PAIR, PAIR), PAIR), :]
            source = (word >> SOURCE_AT) & ((1 << (SLOT_AT - SOURCE_AT)) - 1)
            right = []
            for table in tables:
                part = table[pl.ds(pl.multiple_of(source * BLK, BLK), BLK), :]
                zero = jnp.zeros_like(part)
                right.append(jnp.concatenate([jnp.where(low, part, zero), jnp.where(low, zero, part)], axis=0))
            products.append(jnp.dot(block, jnp.concatenate(right, axis=1), preferred_element_type=jnp.float32))
        add(first - UNROLL)
        for u in range(UNROLL):
            pending[u * PAIR : (u + 1) * PAIR, :] = products[u]
        return carry

    groups = (end - start + (UNROLL - 1)) // UNROLL
    lax.fori_loop(0, groups, step, 0)
    add(start + (groups - 1) * UNROLL)
    if len(outs) > 2:
        outs[0][...] = acc[: trash * PAIR, :].astype(outs[0].dtype)


def product(group, words, blocks, tables, trash, sent):
    lanes = LANES * len(tables)
    full = jax.ShapeDtypeStruct(((trash + 1) * PAIR, lanes), jnp.float32)
    out = jax.ShapeDtypeStruct((trash * PAIR, lanes), jnp.bfloat16) if sent else full
    sums = [pltpu.VMEM(full.shape, full.dtype)] if sent else []
    return pl.pallas_call(
        functools.partial(product_kernel, trash, group, len(tables)),
        in_specs=[SMEM, VMEM] + [VMEM] * len(tables),
        out_specs=VMEM,
        out_shape=out,
        scratch_shapes=sums + [pltpu.VMEM((UNROLL * PAIR, lanes), jnp.float32)],
        compiler_params=pltpu.CompilerParams(vmem_limit_bytes=8 * MIB),
        cost_estimate=pl.CostEstimate(flops=1, bytes_accessed=1, transcendentals=0),
        name="product_send" if sent else "product_keep",
    )(words, blocks, *tables)


def add_kernel(keep_ref, *refs):
    parts, (next_ref, send_ref) = refs[:-2], refs[-2:]
    half, lanes = next_ref.shape[0], parts[0].shape[1]
    for i, got_ref in enumerate(parts):
        at = slice(i * lanes, (i + 1) * lanes)
        next_ref[:, at] = keep_ref[:half, at] + got_ref[:half, :].astype(jnp.float32)
        send_ref[:, at] = (keep_ref[half:, at] + got_ref[half:, :].astype(jnp.float32)).astype(send_ref.dtype)


def add_halves(keep, which, got):
    rows, lanes = got[0].shape[0], keep.shape[1]
    block = lambda n, lanes, i: pl.BlockSpec((n, lanes), lambda _: (i, 0))
    return pl.pallas_call(
        add_kernel,
        grid=(1,),
        in_specs=[block(rows, lanes, which)] + [block(*g.shape, 0) for g in got],
        out_specs=(block(rows // 2, lanes, 0), block(rows // 2, lanes, 0)),
        out_shape=(
            jax.ShapeDtypeStruct((rows // 2, lanes), jnp.float32),
            jax.ShapeDtypeStruct((rows // 2, lanes), jnp.bfloat16),
        ),
        compiler_params=pltpu.CompilerParams(vmem_limit_bytes=8 * MIB),
        cost_estimate=pl.CostEstimate(flops=rows * lanes, bytes_accessed=MIB, transcendentals=0),
        name="add",
    )(keep, *got)


def layer_kernel(index, *refs):
    sums, (weight_ref, bias_ref, out_ref, wide, left, right) = refs[:-6], refs[-6:]
    r = lax.axis_index("row")
    wide[...] = weight_ref[...].astype(jnp.float32)
    size = wide.shape[0] // (2 * len(index[0]))
    halves = []
    for pieces in index:
        rows = [wide[pl.ds(pl.multiple_of((r ^ i) * size, size), size), :] for i in pieces]
        halves.append(jnp.concatenate(rows, axis=0).astype(jnp.bfloat16))
    zero = jnp.zeros_like(halves[0])
    even = jnp.concatenate([halves[0], zero, halves[1], zero], axis=0)
    odd = jnp.concatenate([zero, halves[0], zero, halves[1]], axis=0)
    base = 0
    for k in range(len(sums) // 2):
        keep, got = sums[2 * k], sums[2 * k + 1]
        aggregated = (keep[...] + got[...].astype(jnp.float32)).astype(jnp.bfloat16)
        rows = got.shape[0]
        for h, w in enumerate((even, odd)):
            hidden = jnp.dot(aggregated, w, preferred_element_type=jnp.float32) + bias_ref[...]
            hidden = jnp.maximum(hidden, 0.0)
            left[pl.ds(base + h, rows, stride=2), :] = hidden[:, :LANES]
            right[pl.ds(base + h, rows, stride=2), :] = hidden[:, LANES:]
        base += 2 * rows
    out_ref[:, :LANES] = left[...].astype(out_ref.dtype)
    out_ref[:, LANES:] = right[...].astype(out_ref.dtype)


def layer(index, sums, weight, bias):
    rows = sum(x.shape[0] for x in sums)
    return pl.pallas_call(
        functools.partial(layer_kernel, index),
        out_shape=jax.ShapeDtypeStruct((rows, weight.shape[1]), jnp.bfloat16),
        scratch_shapes=[pltpu.VMEM(weight.shape, jnp.float32)] + [pltpu.VMEM((rows, LANES), jnp.float32)] * 2,
        compiler_params=pltpu.CompilerParams(vmem_limit_bytes=8 * MIB),
        name="layer",
    )(*sums, weight, bias)


def exchange(x, axis, size, bit):
    return lax.ppermute(x, axis, [(i, i ^ (1 << bit)) for i in range(size)])


def shards(n_row, n_col, features, block_codes, block_count, block_values, weight, bias):
    top, col_axis_bits = log2(n_row) - 1, list(range(log2(n_col)))
    col_blocks = features.shape[0] // BLK
    row_total = col_blocks * n_col // n_row
    per = row_total // n_col

    z_first, x_first = tuple(col_axis_bits[1:] + col_axis_bits[:1]), tuple(col_axis_bits)
    chunks = ((per // 2, x_first), (per // 4, x_first), (per // 4, z_first))
    halves = [size * n_col // 2 for size, _ in chunks]

    def spread(pieces, index):
        for bit in range(top):
            pieces = pieces + [exchange(p, "row", n_row, bit) for p in pieces]
            index = index + [i ^ (1 << bit) for i in index]
        return pieces, index

    mine = features.T
    other = exchange(mine, "row", n_row, top)
    near, near_index = spread([mine], [0])
    blocks, words = relayout(chunks, log2(col_blocks), block_count, block_codes, block_values[0])

    tables = [make_table(near)]
    first = product(0, words, blocks, tables, halves[0], True)
    other, first = lax.optimization_barrier((other, first))
    far, far_index = spread([other], [1 << top])
    tables.append(make_table(far))
    sends = [(first, product(0, words, blocks, tables[1:], halves[0], True))]
    sends += [(product(k, words, blocks, tables, halves[k], True),) for k in (1, 2)]
    gots = [[exchange(s, "col", n_col, order[0]) for s in send] for send, (_, order) in zip(sends, chunks)]
    words, gots[0][0] = lax.optimization_barrier((words, gots[0][0]))
    kept = product(len(chunks), words, blocks, tables, sum(halves), False)
    keeps = [(kept, sum(halves[:k]) // halves[k]) for k in range(len(chunks))]
    for k in range(len(col_axis_bits)):
        for i, (_, order) in enumerate(chunks):
            got = gots[i] if k == 0 else [exchange(sends[i][0], "col", n_col, order[k])]
            if k < len(col_axis_bits) - 1:
                total, send = add_halves(*keeps[i], got)
                keeps[i], sends[i] = (total, 0), (send,)
            else:
                keeps[i], sends[i] = keeps[i][0], got[0]
    sums = [x for pair in zip(keeps, sends) for x in pair]
    return layer((near_index, far_index), sums, weight, bias[None, :])


def solution(mesh):
    in_specs = (P("col", "row"), P("row", "col"), P("row", "col"), P("row", "col", None), P(), P())
    out_specs = P(("row", "col"), None)
    body = functools.partial(shards, mesh.shape["row"], mesh.shape["col"])
    return jax.shard_map(body, mesh=mesh, in_specs=in_specs, out_specs=out_specs, check_vma=False)
```

time: 48.8 us -> 48.7 us (level)
  waiting for transfers between devices: 10.7 us -> 11.5 us
  starting transfers between devices: 25.1 us -> 24.4 us
    pallas_call x1 -> x2, Pallas kernels: 0.92 us -> 1.85 us  [make_table(): pl.pallas_call(table_kernel, in_specs=[VMEM] * len(parts), out_specs=VMEM...]
    ppermute x15 -> x13, waiting for transfers between devices: 10.7 us -> 11.5 us  [exchange(): return lax.ppermute(x, axis, [(i, i ^ 1 << bit) for i in range(size)])]
    ppermute x15 -> x13, starting transfers between devices: 25.1 us -> 24.4 us  [exchange(): return lax.ppermute(x, axis, [(i, i ^ 1 << bit) for i in range(size)])]
    pallas_call x14 -> x12, Pallas kernels: 9.17 us -> 8.6 us  [the longest x5 4.9 us: product(): pl.pallas_call(functools.partial(product_kernel, trash, group, len(tables...]
  transfers between devices with their start and end apart: 15 -> 13, of which waited for: 5 -> 5; matrix products, arithmetic and copies ran while one was open for 0% -> 0% of each run, Pallas kernels for 17% -> 21%
where the time goes in v3:
time: 48.7 us; the launch traced here: 49 us
  starting transfers between devices  24.4 us (50%)
  Pallas kernels  11.6 us (24%)
  waiting for transfers between devices  11.5 us (24%)
  between operations  0.77 us (2%)
  local copies, waits for them, and re-layouts  0.69 us (1%)
    ppermute x13, starting transfers between devices, exchange(): return lax.ppermute(x, axis, [(i, i ^ 1 << bit) for i in range(size)])  24.4 us
    ppermute x13, waiting for transfers between devices, exchange(): return lax.ppermute(x, axis, [(i, i ^ 1 << bit) for i in range(size)])  11.5 us
    pallas_call x5, Pallas kernels, product(): pl.pallas_call(functools.partial(product_kernel, trash, group, len(tables...  4.9 us
    pallas_call x1, Pallas kernels, relayout(): pl.pallas_call(functools.partial(relayout_kernel, chunks, col_bits), in_s...  3.37 us
    pallas_call x2, Pallas kernels, make_table(): pl.pallas_call(table_kernel, in_specs=[VMEM] * len(parts), out_specs=VMEM...  1.85 us
    pallas_call x1, Pallas kernels, layer(): pl.pallas_call(functools.partial(layer_kernel, index), out_shape=jax.Shap...  1.18 us
  transfers between devices with their start and end apart: 13, of which 5 were waited for; matrix products, arithmetic and copies ran while one was open for 0% of the time, Pallas kernels for 21%

profile of v3, /device:TPU:0, one launch (start us, length us, event | category | flops | bytes accessed | tf_op | source)
XLA Modules:
  0.0 49.0 jit_solution(3283980429096064147)
XLA Ops:
  0.0 0.5 collective-permute-start.1
  0.5 2.6 %collective-permute-start = (bf16[32,4096]{1,0:T(8,128)(2,1)}, bf16[32,4096]{1,0:T(8,128)(2,1)S(1)}, u32[]{:S(2)}, u32[]{:S(2)}) collective-permute-start(bf16[32,4096]{1,0:T(8,128)(2,1)} %bitcast.4), channel_id=1, source_target_pairs={{0,16},{8,24},{16,0},{24,8},{1,17},{9,25},{17,1},{25,9},{2,18},{10... | collective-permute-start | bytes 786440 | tf_op jit(solution)/shard_map/ppermute | solution.py:265
  3.7 0.7 %copy-done.2 = s32[1,384]{1,0:T(1,128)S(1)} copy-done((s32[1,384]{1,0:T(1,128)S(1)}, s32[1,384]{1,0:T(1,128)}, u32[]{:S(2)}) %copy-start.2) | copy-done | bytes 1560
  4.4 3.4 %relayout.1 = (bf16[12288,128]{1,0:T(8,128)(2,1)S(1)}, s32[1,512]{1,0:T(1,128)S(1)}) custom-call(s32[1,1]{1,0:T(1,128)S(6)} %copy.7.count_ref, s32[1,384]{1,0:T(1,128)S(1)} %copy-done.2, bf16[384,4096]{1,0:T(8,128)(2,1)} %bitcast.7), custom_call_target="tpu_custom_call" | custom-call | bytes 6291456 | tf_op jit(solution)/shard_map/relayout/pallas_call | solution.py:95
  7.8 0.9 %table.2.refs_0_ = bf16[4096,128]{1,0:T(8,128)(2,1)S(1)} custom-call(bf16[32,4096]{1,0:T(8,128)(2,1)S(1)} %bitcast.5, bf16[32,4096]{1,0:T(8,128)(2,1)S(1)} %collective-permute-done.1.refs_1_), custom_call_target="tpu_custom_call" | custom-call | flops 1 | bytes 1 | tf_op jit(solution)/shard_map/table/pallas_call | solution.py:130
  8.7 1.0 %product_send.4 = bf16[1024,128]{1,0:T(8,128)(2,1)S(1)} custom-call(s32[1,512]{1,0:T(1,128)S(1)} %get-tuple-element.26.words_ref, bf16[12288,128]{1,0:T(8,128)(2,1)S(1)} %get-tuple-element.24.blocks_ref, bf16[4096,128]{1,0:T(8,128)(2,1)S(1)} %table.2.refs_0_), custom_call_target="tpu_custom_call" | custom-call | flops 1 | bytes 1 | tf_op jit(solution)/shard_map/product_send/pallas_call | solution.py:187
  9.7 0.4 collective-permute-done.refs_0_
  10.2 2.2 %collective-permute-start.2 = (bf16[1024,128]{1,0:T(8,128)(2,1)S(1)}, bf16[1024,128]{1,0:T(8,128)(2,1)S(1)}, u32[]{:S(2)}, u32[]{:S(2)}) collective-permute-start(bf16[1024,128]{1,0:T(8,128)(2,1)S(1)} %product_send.4), channel_id=1, source_target_pairs={{0,1},{1,0},{2,3},{3,2},{4,5},{5,4},{6,7},{7,6},{8,9},{9,8},{10,11... | collective-permute-start | bytes 786440 | tf_op jit(solution)/shard_map/ppermute | solution.py:265
  12.4 0.9 %table.3.refs_1_.refs_0_ = bf16[4096,128]{1,0:T(8,128)(2,1)S(1)} custom-call(bf16[32,4096]{1,0:T(8,128)(2,1)S(1)} %collective-permute-done.refs_0_, bf16[32,4096]{1,0:T(8,128)(2,1)S(1)} %collective-permute-done.3.refs_1_), custom_call_target="tpu_custom_call" | custom-call | flops 1 | bytes 1 | tf_op jit(solution)/shard_map/table/pallas_call | solution.py:130
  13.3 1.0 %product_send.5 = bf16[1024,128]{1,0:T(8,128)(2,1)S(1)} custom-call(s32[1,512]{1,0:T(1,128)S(1)} %get-tuple-element.26.words_ref, bf16[12288,128]{1,0:T(8,128)(2,1)S(1)} %get-tuple-element.24.blocks_ref, bf16[4096,128]{1,0:T(8,128)(2,1)S(1)} %table.3.refs_1_.refs_0_), custom_call_target="tpu_custom_call" | custom-call | flops 1 | bytes 1 | tf_op jit(solution)/shard_map/product_send/pallas_call | solution.py:187
  14.3 2.6 %collective-permute-start.4 = (bf16[1024,128]{1,0:T(8,128)(2,1)S(1)}, bf16[1024,128]{1,0:T(8,128)(2,1)S(1)}, u32[]{:S(2)}, u32[]{:S(2)}) collective-permute-start(bf16[1024,128]{1,0:T(8,128)(2,1)S(1)} %product_send.5), channel_id=1, source_target_pairs={{0,1},{1,0},{2,3},{3,2},{4,5},{5,4},{6,7},{7,6},{8,9},{9,8},{10,11... | collective-permute-start | bytes 786440 | tf_op jit(solution)/shard_map/ppermute | solution.py:265
  16.9 0.8 %product_send.7 = bf16[512,256]{1,0:T(8,128)(2,1)S(1)} custom-call(s32[1,512]{1,0:T(1,128)S(1)} %get-tuple-element.26.words_ref, bf16[12288,128]{1,0:T(8,128)(2,1)S(1)} %get-tuple-element.24.blocks_ref, bf16[4096,128]{1,0:T(8,128)(2,1)S(1)} %table.2.refs_0_, bf16[4096,128]{1,0:T(8,128)(2,1)S(1)} %table.3.refs_1_.refs_0_), custom_call_target="tpu_custom_call" | custom-call | flops 1 | bytes 1 | tf_op jit(solution)/shard_map/product_send/pallas_call | solution.py:187
  17.6 2.9 %collective-permute-start.10 = (bf16[512,256]{1,0:T(8,128)(2,1)S(1)}, bf16[512,256]{1,0:T(8,128)(2,1)S(1)}, u32[]{:S(2)}, u32[]{:S(2)}) collective-permute-start(bf16[512,256]{1,0:T(8,128)(2,1)S(1)} %product_send.7), channel_id=1, source_target_pairs={{0,2},{1,3},{2,0},{3,1},{4,6},{5,7},{6,4},{7,5},{8,10},{9,11},{10,... | collective-permute-start | bytes 786440 | tf_op jit(solution)/shard_map/ppermute | solution.py:265
  20.6 1.0 %product_send.6 = bf16[512,256]{1,0:T(8,128)(2,1)S(1)} custom-call(s32[1,512]{1,0:T(1,128)S(1)} %get-tuple-element.26.words_ref, bf16[12288,128]{1,0:T(8,128)(2,1)S(1)} %get-tuple-element.24.blocks_ref, bf16[4096,128]{1,0:T(8,128)(2,1)S(1)} %table.2.refs_0_, bf16[4096,128]{1,0:T(8,128)(2,1)S(1)} %table.3.refs_1_.refs_0_), custom_call_target="tpu_custom_call" | custom-call | flops 1 | bytes 1 | tf_op jit(solution)/shard_map/product_send/pallas_call | solution.py:187
  21.6 1.7 %collective-permute-start.7 = (bf16[512,256]{1,0:T(8,128)(2,1)S(1)}, bf16[512,256]{1,0:T(8,128)(2,1)S(1)}, u32[]{:S(2)}, u32[]{:S(2)}) collective-permute-start(bf16[512,256]{1,0:T(8,128)(2,1)S(1)} %product_send.6), channel_id=1, source_target_pairs={{0,1},{1,0},{2,3},{3,2},{4,5},{5,4},{6,7},{7,6},{8,9},{9,8},{10,11... | collective-permute-start | bytes 786440 | tf_op jit(solution)/shard_map/ppermute | solution.py:265
  23.3 1.1 %product_keep.1.keep_ref = f32[2080,256]{1,0:T(8,128)S(1)} custom-call(s32[1,512]{1,0:T(1,128)S(1)} %get-tuple-element.26.words_ref, bf16[12288,128]{1,0:T(8,128)(2,1)S(1)} %get-tuple-element.24.blocks_ref, bf16[4096,128]{1,0:T(8,128)(2,1)S(1)} %table.2.refs_0_, bf16[4096,128]{1,0:T(8,128)(2,1)S(1)} %table.3.refs_1_.refs_0_), custom_call_target="tpu_custom_call" | custom-call | flops 1 | bytes 1 | tf_op jit(solution)/shard_map/product_keep/pallas_call | solution.py:187
  24.4 0.8 %collective-permute-done.4.refs_1_ = bf16[1024,128]{1,0:T(8,128)(2,1)S(1)} collective-permute-done((bf16[1024,128]{1,0:T(8,128)(2,1)S(1)}, bf16[1024,128]{1,0:T(8,128)(2,1)S(1)}, u32[]{:S(2)}, u32[]{:S(2)}) %collective-permute-start.4) | collective-permute-done | bytes 262176 | tf_op jit(solution)/shard_map/ppermute | solution.py:265
  25.2 0.1 add.6
  25.3 0.0 copy-start.1
  25.3 2.7 %collective-permute-start.5 = (bf16[512,256]{1,0:T(8,128)(2,1)S(1)}, bf16[512,256]{1,0:T(8,128)(2,1)S(1)}, u32[]{:S(2)}, u32[]{:S(2)}) collective-permute-start(bf16[512,256]{1,0:T(8,128)(2,1)S(1)} %get-tuple-element.30), channel_id=1, source_target_pairs={{0,2},{1,3},{2,0},{3,1},{4,6},{5,7},{6,4},{7,5},{8,10},{9,11},{10,... | collective-permute-start | bytes 786440 | tf_op jit(solution)/shard_map/ppermute | solution.py:265
  28.0 1.6 %collective-permute-start.11 = (bf16[256,256]{1,0:T(8,128)(2,1)S(1)}, bf16[256,256]{1,0:T(8,128)(2,1)S(1)}, u32[]{:S(2)}, u32[]{:S(2)}) collective-permute-start(bf16[256,256]{1,0:T(8,128)(2,1)S(1)} %get-tuple-element.38), channel_id=1, source_target_pairs={{0,4},{1,5},{2,6},{3,7},{4,0},{5,1},{6,2},{7,3},{8,12},{9,13},{10,... | collective-permute-start | bytes 393224 | tf_op jit(solution)/shard_map/ppermute | solution.py:265
  29.6 0.9 %collective-permute-done.7.refs_0_ = bf16[512,256]{1,0:T(8,128)(2,1)S(1)} collective-permute-done((bf16[512,256]{1,0:T(8,128)(2,1)S(1)}, bf16[512,256]{1,0:T(8,128)(2,1)S(1)}, u32[]{:S(2)}, u32[]{:S(2)}) %collective-permute-start.7) | collective-permute-done | bytes 262176 | tf_op jit(solution)/shard_map/ppermute | solution.py:265
  30.5 0.1 add.8
  30.6 2.4 %collective-permute-start.8 = (bf16[256,256]{1,0:T(8,128)(2,1)S(1)}, bf16[256,256]{1,0:T(8,128)(2,1)S(1)}, u32[]{:S(2)}, u32[]{:S(2)}) collective-permute-start(bf16[256,256]{1,0:T(8,128)(2,1)S(1)} %get-tuple-element.34), channel_id=1, source_target_pairs={{0,2},{1,3},{2,0},{3,1},{4,6},{5,7},{6,4},{7,5},{8,10},{9,11},{10,... | collective-permute-start | bytes 393224 | tf_op jit(solution)/shard_map/ppermute | solution.py:265
  33.0 4.8 %collective-permute-done.5.refs_0_ = bf16[512,256]{1,0:T(8,128)(2,1)S(1)} collective-permute-done((bf16[512,256]{1,0:T(8,128)(2,1)S(1)}, bf16[512,256]{1,0:T(8,128)(2,1)S(1)}, u32[]{:S(2)}, u32[]{:S(2)}) %collective-permute-start.5) | collective-permute-done | bytes 262176 | tf_op jit(solution)/shard_map/ppermute | solution.py:265
  37.8 0.1 add.7
  37.8 1.0 %collective-permute-start.6 = (bf16[256,256]{1,0:T(8,128)(2,1)S(1)}, bf16[256,256]{1,0:T(8,128)(2,1)S(1)}, u32[]{:S(2)}, u32[]{:S(2)}) collective-permute-start(bf16[256,256]{1,0:T(8,128)(2,1)S(1)} %get-tuple-element.32), channel_id=1, source_target_pairs={{0,4},{1,5},{2,6},{3,7},{4,0},{5,1},{6,2},{7,3},{8,12},{9,13},{10,... | collective-permute-start | bytes 393224 | tf_op jit(solution)/shard_map/ppermute | solution.py:265
  38.9 1.5 %collective-permute-start.12 = (bf16[128,256]{1,0:T(8,128)(2,1)S(1)}, bf16[128,256]{1,0:T(8,128)(2,1)S(1)}, u32[]{:S(2)}, u32[]{:S(2)}) collective-permute-start(bf16[128,256]{1,0:T(8,128)(2,1)S(1)} %get-tuple-element.40), channel_id=1, source_target_pairs={{0,1},{1,0},{2,3},{3,2},{4,5},{5,4},{6,7},{7,6},{8,9},{9,8},{10,11... | collective-permute-start | bytes 196616 | tf_op jit(solution)/shard_map/ppermute | solution.py:265
  40.5 2.8 %collective-permute-start.9 = (bf16[128,256]{1,0:T(8,128)(2,1)S(1)}, bf16[128,256]{1,0:T(8,128)(2,1)S(1)}, u32[]{:S(2)}, u32[]{:S(2)}) collective-permute-start(bf16[128,256]{1,0:T(8,128)(2,1)S(1)} %get-tuple-element.36), channel_id=1, source_target_pairs={{0,4},{1,5},{2,6},{3,7},{4,0},{5,1},{6,2},{7,3},{8,12},{9,13},{10,... | collective-permute-start | bytes 196616 | tf_op jit(solution)/shard_map/ppermute | solution.py:265
  43.2 0.0 collective-permute-done.12.refs_5_
  43.2 4.5 %collective-permute-done.9.refs_3_ = bf16[128,256]{1,0:T(8,128)(2,1)S(1)} collective-permute-done((bf16[128,256]{1,0:T(8,128)(2,1)S(1)}, bf16[128,256]{1,0:T(8,128)(2,1)S(1)}, u32[]{:S(2)}, u32[]{:S(2)}) %collective-permute-start.9) | collective-permute-done | bytes 65568 | tf_op jit(solution)/shard_map/ppermute | solution.py:265
  47.8 1.2 %layer.1 = bf16[1024,256]{1,0:T(8,128)(2,1)} custom-call(f32[256,256]{1,0:T(8,128)S(1)} %get-tuple-element.31.refs_0_, bf16[256,256]{1,0:T(8,128)(2,1)S(1)} %collective-permute-done.6.refs_1_, f32[128,256]{1,0:T(8,128)S(1)} %get-tuple-element.35.refs_2_, bf16[128,256]{1,0:T(8,128)(2,1)S(1)} %collective-permute-done.9.refs_3_, ...), custom_call_target="tpu_custom_call" | custom-call | tf_op jit(solution)/shard_map/layer/pallas_call | solution.py:255
  (17 shorter events, 0.1 us)
Async XLA Ops:
  0.0 7.8 %copy-start = (bf16[4096,32]{0,1:T(8,128)(2,1)S(1)}, bf16[4096,32]{0,1:T(8,128)(2,1)}, u32[]{:S(2)}) copy-start(bf16[4096,32]{0,1:T(8,128)(2,1)} %param.6) | copy-start | bytes 786436
  0.0 7.7 %collective-permute-start.1 = (bf16[32,4096]{1,0:T(8,128)(2,1)}, bf16[32,4096]{1,0:T(8,128)(2,1)S(1)}, u32[]{:S(2)}, u32[]{:S(2)}) collective-permute-start(bf16[32,4096]{1,0:T(8,128)(2,1)} %bitcast.3), channel_id=1, source_target_pairs={{0,8},{8,0},{16,24},{24,16},{1,9},{9,1},{17,25},{25,17},{2,10},{10... | collective-permute-start | bytes 786440 | tf_op jit(solution)/shard_map/ppermute | solution.py:265
  0.5 9.7 %collective-permute-start = (bf16[32,4096]{1,0:T(8,128)(2,1)}, bf16[32,4096]{1,0:T(8,128)(2,1)S(1)}, u32[]{:S(2)}, u32[]{:S(2)}) collective-permute-start(bf16[32,4096]{1,0:T(8,128)(2,1)} %bitcast.4), channel_id=1, source_target_pairs={{0,16},{8,24},{16,0},{24,8},{1,17},{9,25},{17,1},{25,9},{2,18},{10... | collective-permute-start | bytes 786440 | tf_op jit(solution)/shard_map/ppermute | solution.py:265
  3.7 0.7 %copy-start.2 = (s32[1,384]{1,0:T(1,128)S(1)}, s32[1,384]{1,0:T(1,128)}, u32[]{:S(2)}) copy-start(s32[1,384]{1,0:T(1,128)} %codes_hbm.1) | copy-start | bytes 4612
  10.2 2.2 %collective-permute-start.3 = (bf16[32,4096]{1,0:T(8,128)(2,1)S(1)}, bf16[32,4096]{1,0:T(8,128)(2,1)S(1)}, u32[]{:S(2)}, u32[]{:S(2)}) collective-permute-start(bf16[32,4096]{1,0:T(8,128)(2,1)S(1)} %collective-permute-done.refs_0_), channel_id=1, source_target_pairs={{0,8},{8,0},{16,24},{24,16},{1,9},{9,1},{17,25},{25,17},{2,10},{10... | collective-permute-start | bytes 786440 | tf_op jit(solution)/shard_map/ppermute | solution.py:265
  10.2 13.1 %collective-permute-start.2 = (bf16[1024,128]{1,0:T(8,128)(2,1)S(1)}, bf16[1024,128]{1,0:T(8,128)(2,1)S(1)}, u32[]{:S(2)}, u32[]{:S(2)}) collective-permute-start(bf16[1024,128]{1,0:T(8,128)(2,1)S(1)} %product_send.4), channel_id=1, source_target_pairs={{0,1},{1,0},{2,3},{3,2},{4,5},{5,4},{6,7},{7,6},{8,9},{9,8},{10,11... | collective-permute-start | bytes 786440 | tf_op jit(solution)/shard_map/ppermute | solution.py:265
  14.3 10.8 %collective-permute-start.4 = (bf16[1024,128]{1,0:T(8,128)(2,1)S(1)}, bf16[1024,128]{1,0:T(8,128)(2,1)S(1)}, u32[]{:S(2)}, u32[]{:S(2)}) collective-permute-start(bf16[1024,128]{1,0:T(8,128)(2,1)S(1)} %product_send.5), channel_id=1, source_target_pairs={{0,1},{1,0},{2,3},{3,2},{4,5},{5,4},{6,7},{7,6},{8,9},{9,8},{10,11... | collective-permute-start | bytes 786440 | tf_op jit(solution)/shard_map/ppermute | solution.py:265
  17.6 10.3 %collective-permute-start.10 = (bf16[512,256]{1,0:T(8,128)(2,1)S(1)}, bf16[512,256]{1,0:T(8,128)(2,1)S(1)}, u32[]{:S(2)}, u32[]{:S(2)}) collective-permute-start(bf16[512,256]{1,0:T(8,128)(2,1)S(1)} %product_send.7), channel_id=1, source_target_pairs={{0,2},{1,3},{2,0},{3,1},{4,6},{5,7},{6,4},{7,5},{8,10},{9,11},{10,... | collective-permute-start | bytes 786440 | tf_op jit(solution)/shard_map/ppermute | solution.py:265
  21.6 8.9 %collective-permute-start.7 = (bf16[512,256]{1,0:T(8,128)(2,1)S(1)}, bf16[512,256]{1,0:T(8,128)(2,1)S(1)}, u32[]{:S(2)}, u32[]{:S(2)}) collective-permute-start(bf16[512,256]{1,0:T(8,128)(2,1)S(1)} %product_send.6), channel_id=1, source_target_pairs={{0,1},{1,0},{2,3},{3,2},{4,5},{5,4},{6,7},{7,6},{8,9},{9,8},{10,11... | collective-permute-start | bytes 786440 | tf_op jit(solution)/shard_map/ppermute | solution.py:265
  25.3 22.5 %copy-start.1 = (bf16[128,256]{1,0:T(8,128)(2,1)S(1)}, bf16[128,256]{1,0:T(8,128)(2,1)}, u32[]{:S(2)}) copy-start(bf16[128,256]{1,0:T(8,128)(2,1)} %refs_6_.1) | copy-start | bytes 196612
  25.3 22.5 %copy-start.3 = (f32[256]{0:T(256)S(1)}, f32[256]{0:T(256)}, u32[]{:S(2)}) copy-start(f32[256]{0:T(256)} %param.11) | copy-start | bytes 3076
  25.3 12.5 %collective-permute-start.5 = (bf16[512,256]{1,0:T(8,128)(2,1)S(1)}, bf16[512,256]{1,0:T(8,128)(2,1)S(1)}, u32[]{:S(2)}, u32[]{:S(2)}) collective-permute-start(bf16[512,256]{1,0:T(8,128)(2,1)S(1)} %get-tuple-element.30), channel_id=1, source_target_pairs={{0,2},{1,3},{2,0},{3,1},{4,6},{5,7},{6,4},{7,5},{8,10},{9,11},{10,... | collective-permute-start | bytes 786440 | tf_op jit(solution)/shard_map/ppermute | solution.py:265
  28.0 10.9 %collective-permute-start.11 = (bf16[256,256]{1,0:T(8,128)(2,1)S(1)}, bf16[256,256]{1,0:T(8,128)(2,1)S(1)}, u32[]{:S(2)}, u32[]{:S(2)}) collective-permute-start(bf16[256,256]{1,0:T(8,128)(2,1)S(1)} %get-tuple-element.38), channel_id=1, source_target_pairs={{0,4},{1,5},{2,6},{3,7},{4,0},{5,1},{6,2},{7,3},{8,12},{9,13},{10,... | collective-permute-start | bytes 393224 | tf_op jit(solution)/shard_map/ppermute | solution.py:265
  30.6 9.8 %collective-permute-start.8 = (bf16[256,256]{1,0:T(8,128)(2,1)S(1)}, bf16[256,256]{1,0:T(8,128)(2,1)S(1)}, u32[]{:S(2)}, u32[]{:S(2)}) collective-permute-start(bf16[256,256]{1,0:T(8,128)(2,1)S(1)} %get-tuple-element.34), channel_id=1, source_target_pairs={{0,2},{1,3},{2,0},{3,1},{4,6},{5,7},{6,4},{7,5},{8,10},{9,11},{10,... | collective-permute-start | bytes 393224 | tf_op jit(solution)/shard_map/ppermute | solution.py:265
  37.8 9.9 %collective-permute-start.6 = (bf16[256,256]{1,0:T(8,128)(2,1)S(1)}, bf16[256,256]{1,0:T(8,128)(2,1)S(1)}, u32[]{:S(2)}, u32[]{:S(2)}) collective-permute-start(bf16[256,256]{1,0:T(8,128)(2,1)S(1)} %get-tuple-element.32), channel_id=1, source_target_pairs={{0,4},{1,5},{2,6},{3,7},{4,0},{5,1},{6,2},{7,3},{8,12},{9,13},{10,... | collective-permute-start | bytes 393224 | tf_op jit(solution)/shard_map/ppermute | solution.py:265
  38.9 4.3 %collective-permute-start.12 = (bf16[128,256]{1,0:T(8,128)(2,1)S(1)}, bf16[128,256]{1,0:T(8,128)(2,1)S(1)}, u32[]{:S(2)}, u32[]{:S(2)}) collective-permute-start(bf16[128,256]{1,0:T(8,128)(2,1)S(1)} %get-tuple-element.40), channel_id=1, source_target_pairs={{0,1},{1,0},{2,3},{3,2},{4,5},{5,4},{6,7},{7,6},{8,9},{9,8},{10,11... | collective-permute-start | bytes 196616 | tf_op jit(solution)/shard_map/ppermute | solution.py:265
  40.5 7.3 %collective-permute-start.9 = (bf16[128,256]{1,0:T(8,128)(2,1)S(1)}, bf16[128,256]{1,0:T(8,128)(2,1)S(1)}, u32[]{:S(2)}, u32[]{:S(2)}) collective-permute-start(bf16[128,256]{1,0:T(8,128)(2,1)S(1)} %get-tuple-element.36), channel_id=1, source_target_pairs={{0,4},{1,5},{2,6},{3,7},{4,0},{5,1},{6,2},{7,3},{8,12},{9,13},{10,... | collective-permute-start | bytes 196616 | tf_op jit(solution)/shard_map/ppermute | solution.py:265

commit v4 on v3

--- a/solution.py
+++ b/solution.py
@@ -29,15 +29,15 @@
 
 def make_lists(chunks, col_bits, count, codes, words_ref):
     slots, width = codes.shape[1], words_ref.shape[1]
-    per = sum(size for size, _ in chunks)
+    per = sum(size for size, _, _ in chunks)
     row_block, col_block = codes >> col_bits, codes & ((1 << col_bits) - 1)
     owner = (row_block >> log2(per)) ^ lax.axis_index("col")
     sub = row_block & (per - 1)
     number = lax.broadcasted_iota(jnp.int32, (1, slots), 1)
     live = number < count
     group, target = jnp.full_like(codes, len(chunks) + 1), jnp.zeros_like(codes)
-    first, base = 0, 0
-    for c, (size, order) in enumerate(chunks):
+    first = 0
+    for c, (size, base, order) in enumerate(chunks):
         place = jnp.zeros_like(owner)
         for k, bit in enumerate(order):
             place = place | (((owner >> bit) & 1) << (len(order) - 1 - k))
@@ -47,7 +47,7 @@
         here = live & (sub >= first) & (sub < first + size)
         target = jnp.where(here, jnp.where(keep, place + base, place - half), target)
         group = jnp.where(here, jnp.where(keep, len(chunks), c), group)
-        first, base = first + size, base + half
+        first += size
     same = lax.broadcasted_iota(jnp.int32, (slots, slots), 0) == lax.broadcasted_iota(jnp.int32, (slots, slots), 1)
     column = lambda row: jnp.sum(jnp.where(same, row, 0.0), axis=1, keepdims=True)
     spot = lax.broadcasted_iota(jnp.int32, (slots, width), 1).astype(jnp.float32)
@@ -272,8 +272,10 @@
     per = row_total // n_col
 
     z_first, x_first = tuple(col_axis_bits[1:] + col_axis_bits[:1]), tuple(col_axis_bits)
-    chunks = ((per // 2, x_first), (per // 4, x_first), (per // 4, z_first))
-    halves = [size * n_col // 2 for size, _ in chunks]
+    quarter = per // 4
+    part = quarter * n_col // 2
+    chunks = ((quarter, 2 * part, z_first), (2 * quarter, 0, x_first), (quarter, 3 * part, x_first))
+    halves = [size * n_col // 2 for size, _, _ in chunks]
 
     def spread(pieces, index):
         for bit in range(top):
@@ -287,24 +289,27 @@
     blocks, words = relayout(chunks, log2(col_blocks), block_count, block_codes, block_values[0])
 
     tables = [make_table(near)]
-    first = product(0, words, blocks, tables, halves[0], True)
-    other, first = lax.optimization_barrier((other, first))
+    early = product(1, words, blocks, tables, halves[1], True)
+    other, early = lax.optimization_barrier((other, early))
     far, far_index = spread([other], [1 << top])
     tables.append(make_table(far))
-    sends = [(first, product(0, words, blocks, tables[1:], halves[0], True))]
-    sends += [(product(k, words, blocks, tables, halves[k], True),) for k in (1, 2)]
-    gots = [[exchange(s, "col", n_col, order[0]) for s in send] for send, (_, order) in zip(sends, chunks)]
-    words, gots[0][0] = lax.optimization_barrier((words, gots[0][0]))
+    sends = [(product(0, words, blocks, tables, halves[0], True),)]
+    words, _ = lax.optimization_barrier((words, sends[0]))
+    sends.append((early, product(1, words, blocks, tables[1:], halves[1], True)))
+    sends.append((product(2, words, blocks, tables, halves[2], True),))
+    gots = [[exchange(s, "col", n_col, order[0]) for s in send] for send, (_, _, order) in zip(sends, chunks)]
+    words, _, gots[1][0] = lax.optimization_barrier((words, sends, gots[1][0]))
     kept = product(len(chunks), words, blocks, tables, sum(halves), False)
-    keeps = [(kept, sum(halves[:k]) // halves[k]) for k in range(len(chunks))]
-    for k in range(len(col_axis_bits)):
-        for i, (_, order) in enumerate(chunks):
-            got = gots[i] if k == 0 else [exchange(sends[i][0], "col", n_col, order[k])]
-            if k < len(col_axis_bits) - 1:
-                total, send = add_halves(*keeps[i], got)
-                keeps[i], sends[i] = (total, 0), (send,)
-            else:
-                keeps[i], sends[i] = keeps[i][0], got[0]
+    keeps = [(kept, base // size) for (_, base, _), size in zip(chunks, halves)]
+    stages = len(col_axis_bits)
+    turns = sorted((2 * k + (0, 1, 2.5)[i], k, i) for k in range(stages - 1) for i in range(len(chunks)))
+    for _, k, i in turns:
+        got = gots[i]
+        if i == 1:
+            got, _ = lax.optimization_barrier((got, keeps[0][0]))
+        total, send = add_halves(*keeps[i], got)
+        keeps[i], gots[i] = (total, 0), [exchange(send, "col", n_col, chunks[i][2][k + 1])]
+    keeps, sends = [keep for keep, _ in keeps], [got[0] for got in gots]
     sums = [x for pair in zip(keeps, sends) for x in pair]
     return layer((near_index, far_index), sums, weight, bias[None, :])
 

time: 48.7 us -> 50.5 us (1.037); the launches traced: 49 us -> 49.9 us
  waiting for transfers between devices: 11.5 us -> 18.7 us
  starting transfers between devices: 24.4 us -> 17.7 us
    ppermute x13, waiting for transfers between devices: 11.5 us -> 18.7 us  [exchange(): return lax.ppermute(x, axis, [(i, i ^ 1 << bit) for i in range(size)])]
    ppermute x13, starting transfers between devices: 24.4 us -> 17.7 us  [exchange(): return lax.ppermute(x, axis, [(i, i ^ 1 << bit) for i in range(size)])]
  transfers between devices with their start and end apart: 13 -> 13, of which waited for: 5 -> 8; matrix products, arithmetic and copies ran while one was open for 0% -> 0% of each run, Pallas kernels for 21% -> 22%
where the time goes in v4:
time: 50.5 us; the launch traced here: 49.9 us
  waiting for transfers between devices  18.7 us (37%)
  starting transfers between devices  17.7 us (35%)
  Pallas kernels  12.1 us (24%)
  between operations  0.77 us (2%)
  local copies, waits for them, and re-layouts  0.68 us (1%)
    ppermute x13, waiting for transfers between devices, exchange(): return lax.ppermute(x, axis, [(i, i ^ 1 << bit) for i in range(size)])  18.7 us
    ppermute x13, starting transfers between devices, exchange(): return lax.ppermute(x, axis, [(i, i ^ 1 << bit) for i in range(size)])  17.7 us
    pallas_call x5, Pallas kernels, product(): pl.pallas_call(functools.partial(product_kernel, trash, group, len(tables...  5.4 us
    pallas_call x1, Pallas kernels, relayout(): pl.pallas_call(functools.partial(relayout_kernel, chunks, col_bits), in_s...  3.37 us
    pallas_call x2, Pallas kernels, make_table(): pl.pallas_call(table_kernel, in_specs=[VMEM] * len(parts), out_specs=VMEM...  1.85 us
    pallas_call x1, Pallas kernels, layer(): pl.pallas_call(functools.partial(layer_kernel, index), out_shape=jax.Shap...  1.19 us
  transfers between devices with their start and end apart: 13, of which 8 were waited for; matrix products, arithmetic and copies ran while one was open for 0% of the time, Pallas kernels for 22%

profile of v4, /device:TPU:0, one launch (start us, length us, event | category | flops | bytes accessed | tf_op | source)
XLA Modules:
  0.0 49.9 jit_solution(14293266256351731520)
XLA Ops:
  0.0 0.5 collective-permute-start
  0.5 2.6 %collective-permute-start.1 = (bf16[32,4096]{1,0:T(8,128)(2,1)}, bf16[32,4096]{1,0:T(8,128)(2,1)S(1)}, u32[]{:S(2)}, u32[]{:S(2)}) collective-permute-start(bf16[32,4096]{1,0:T(8,128)(2,1)} %bitcast.4), channel_id=1, source_target_pairs={{0,16},{8,24},{16,0},{24,8},{1,17},{9,25},{17,1},{25,9},{2,18},{10... | collective-permute-start | bytes 786440 | tf_op jit(solution)/shard_map/ppermute | solution.py:265
  3.7 0.7 %copy-done.2 = s32[1,384]{1,0:T(1,128)S(1)} copy-done((s32[1,384]{1,0:T(1,128)S(1)}, s32[1,384]{1,0:T(1,128)}, u32[]{:S(2)}) %copy-start.2) | copy-done | bytes 1560
  4.4 3.4 %relayout.1 = (bf16[12288,128]{1,0:T(8,128)(2,1)S(1)}, s32[1,512]{1,0:T(1,128)S(1)}) custom-call(s32[1,1]{1,0:T(1,128)S(6)} %copy.7.count_ref, s32[1,384]{1,0:T(1,128)S(1)} %copy-done.2, bf16[384,4096]{1,0:T(8,128)(2,1)} %bitcast.7), custom_call_target="tpu_custom_call" | custom-call | bytes 6291456 | tf_op jit(solution)/shard_map/relayout/pallas_call | solution.py:95
  7.8 0.9 %table.2.refs_0_ = bf16[4096,128]{1,0:T(8,128)(2,1)S(1)} custom-call(bf16[32,4096]{1,0:T(8,128)(2,1)S(1)} %bitcast.5, bf16[32,4096]{1,0:T(8,128)(2,1)S(1)} %collective-permute-done.refs_1_), custom_call_target="tpu_custom_call" | custom-call | flops 1 | bytes 1 | tf_op jit(solution)/shard_map/table/pallas_call | solution.py:130
  8.7 1.0 %product_send.4 = bf16[1024,128]{1,0:T(8,128)(2,1)S(1)} custom-call(s32[1,512]{1,0:T(1,128)S(1)} %get-tuple-element.32.words_ref, bf16[12288,128]{1,0:T(8,128)(2,1)S(1)} %get-tuple-element.28.blocks_ref, bf16[4096,128]{1,0:T(8,128)(2,1)S(1)} %table.2.refs_0_), custom_call_target="tpu_custom_call" | custom-call | flops 1 | bytes 1 | tf_op jit(solution)/shard_map/product_send/pallas_call | solution.py:187
  9.7 0.5 collective-permute-done.1.refs_0_
  10.2 0.8 %collective-permute-start.2 = (bf16[32,4096]{1,0:T(8,128)(2,1)S(1)}, bf16[32,4096]{1,0:T(8,128)(2,1)S(1)}, u32[]{:S(2)}, u32[]{:S(2)}) collective-permute-start(bf16[32,4096]{1,0:T(8,128)(2,1)S(1)} %collective-permute-done.1.refs_0_), channel_id=1, source_target_pairs={{0,8},{8,0},{16,24},{24,16},{1,9},{9,1},{17,25},{25,17},{2,10},{10... | collective-permute-start | bytes 786440 | tf_op jit(solution)/shard_map/ppermute | solution.py:265
  11.0 2.0 %collective-permute-start.3 = (bf16[1024,128]{1,0:T(8,128)(2,1)S(1)}, bf16[1024,128]{1,0:T(8,128)(2,1)S(1)}, u32[]{:S(2)}, u32[]{:S(2)}) collective-permute-start(bf16[1024,128]{1,0:T(8,128)(2,1)S(1)} %product_send.4), channel_id=1, source_target_pairs={{0,1},{1,0},{2,3},{3,2},{4,5},{5,4},{6,7},{7,6},{8,9},{9,8},{10,11... | collective-permute-start | bytes 786440 | tf_op jit(solution)/shard_map/ppermute | solution.py:265
  13.0 0.9 %table.3.refs_1_.refs_0_ = bf16[4096,128]{1,0:T(8,128)(2,1)S(1)} custom-call(bf16[32,4096]{1,0:T(8,128)(2,1)S(1)} %collective-permute-done.1.refs_0_, bf16[32,4096]{1,0:T(8,128)(2,1)S(1)} %collective-permute-done.2.refs_1_), custom_call_target="tpu_custom_call" | custom-call | flops 1 | bytes 1 | tf_op jit(solution)/shard_map/table/pallas_call | solution.py:130
  13.9 1.0 %product_send.5 = bf16[512,256]{1,0:T(8,128)(2,1)S(1)} custom-call(s32[1,512]{1,0:T(1,128)S(1)} %get-tuple-element.32.words_ref, bf16[12288,128]{1,0:T(8,128)(2,1)S(1)} %get-tuple-element.28.blocks_ref, bf16[4096,128]{1,0:T(8,128)(2,1)S(1)} %table.2.refs_0_, bf16[4096,128]{1,0:T(8,128)(2,1)S(1)} %table.3.refs_1_.refs_0_), custom_call_target="tpu_custom_call" | custom-call | flops 1 | bytes 1 | tf_op jit(solution)/shard_map/product_send/pallas_call | solution.py:187
  14.9 2.4 %collective-permute-start.4 = (bf16[512,256]{1,0:T(8,128)(2,1)S(1)}, bf16[512,256]{1,0:T(8,128)(2,1)S(1)}, u32[]{:S(2)}, u32[]{:S(2)}) collective-permute-start(bf16[512,256]{1,0:T(8,128)(2,1)S(1)} %product_send.5), channel_id=1, source_target_pairs={{0,2},{1,3},{2,0},{3,1},{4,6},{5,7},{6,4},{7,5},{8,10},{9,11},{10,... | collective-permute-start | bytes 786440 | tf_op jit(solution)/shard_map/ppermute | solution.py:265
  17.3 1.0 %product_send.6 = bf16[1024,128]{1,0:T(8,128)(2,1)S(1)} custom-call(s32[1,512]{1,0:T(1,128)S(1)} %get-tuple-element.32.words_ref, bf16[12288,128]{1,0:T(8,128)(2,1)S(1)} %get-tuple-element.28.blocks_ref, bf16[4096,128]{1,0:T(8,128)(2,1)S(1)} %table.3.refs_1_.refs_0_), custom_call_target="tpu_custom_call" | custom-call | flops 1 | bytes 1 | tf_op jit(solution)/shard_map/product_send/pallas_call | solution.py:187
  18.3 1.2 %collective-permute-start.7 = (bf16[1024,128]{1,0:T(8,128)(2,1)S(1)}, bf16[1024,128]{1,0:T(8,128)(2,1)S(1)}, u32[]{:S(2)}, u32[]{:S(2)}) collective-permute-start(bf16[1024,128]{1,0:T(8,128)(2,1)S(1)} %product_send.6), channel_id=1, source_target_pairs={{0,1},{1,0},{2,3},{3,2},{4,5},{5,4},{6,7},{7,6},{8,9},{9,8},{10,11... | collective-permute-start | bytes 786440 | tf_op jit(solution)/shard_map/ppermute | solution.py:265
  19.5 1.0 %product_send.7 = bf16[512,256]{1,0:T(8,128)(2,1)S(1)} custom-call(s32[1,512]{1,0:T(1,128)S(1)} %get-tuple-element.32.words_ref, bf16[12288,128]{1,0:T(8,128)(2,1)S(1)} %get-tuple-element.28.blocks_ref, bf16[4096,128]{1,0:T(8,128)(2,1)S(1)} %table.2.refs_0_, bf16[4096,128]{1,0:T(8,128)(2,1)S(1)} %table.3.refs_1_.refs_0_), custom_call_target="tpu_custom_call" | custom-call | flops 1 | bytes 1 | tf_op jit(solution)/shard_map/product_send/pallas_call | solution.py:187
  20.5 1.5 %collective-permute-start.10 = (bf16[512,256]{1,0:T(8,128)(2,1)S(1)}, bf16[512,256]{1,0:T(8,128)(2,1)S(1)}, u32[]{:S(2)}, u32[]{:S(2)}) collective-permute-start(bf16[512,256]{1,0:T(8,128)(2,1)S(1)} %product_send.7), channel_id=1, source_target_pairs={{0,1},{1,0},{2,3},{3,2},{4,5},{5,4},{6,7},{7,6},{8,9},{9,8},{10,11... | collective-permute-start | bytes 786440 | tf_op jit(solution)/shard_map/ppermute | solution.py:265
  22.0 1.4 %product_keep.1.keep_ref = f32[2080,256]{1,0:T(8,128)S(1)} custom-call(s32[1,512]{1,0:T(1,128)S(1)} %get-tuple-element.32.words_ref, bf16[12288,128]{1,0:T(8,128)(2,1)S(1)} %get-tuple-element.28.blocks_ref, bf16[4096,128]{1,0:T(8,128)(2,1)S(1)} %table.2.refs_0_, bf16[4096,128]{1,0:T(8,128)(2,1)S(1)} %table.3.refs_1_.refs_0_), custom_call_target="tpu_custom_call" | custom-call | flops 1 | bytes 1 | tf_op jit(solution)/shard_map/product_keep/pallas_call | solution.py:187
  23.4 0.3 collective-permute-done.4.refs_0_
  23.7 3.8 %collective-permute-done.7.refs_1_ = bf16[1024,128]{1,0:T(8,128)(2,1)S(1)} collective-permute-done((bf16[1024,128]{1,0:T(8,128)(2,1)S(1)}, bf16[1024,128]{1,0:T(8,128)(2,1)S(1)}, u32[]{:S(2)}, u32[]{:S(2)}) %collective-permute-start.7) | collective-permute-done | bytes 262176 | tf_op jit(solution)/shard_map/ppermute | solution.py:265
  27.5 0.1 add.8
  27.7 1.6 %collective-permute-start.8 = (bf16[512,256]{1,0:T(8,128)(2,1)S(1)}, bf16[512,256]{1,0:T(8,128)(2,1)S(1)}, u32[]{:S(2)}, u32[]{:S(2)}) collective-permute-start(bf16[512,256]{1,0:T(8,128)(2,1)S(1)} %get-tuple-element.41), channel_id=1, source_target_pairs={{0,2},{1,3},{2,0},{3,1},{4,6},{5,7},{6,4},{7,5},{8,10},{9,11},{10,... | collective-permute-start | bytes 786440 | tf_op jit(solution)/shard_map/ppermute | solution.py:265
  29.3 0.1 collective-permute-start.5
  29.4 3.4 %collective-permute-done.10.refs_0_ = bf16[512,256]{1,0:T(8,128)(2,1)S(1)} collective-permute-done((bf16[512,256]{1,0:T(8,128)(2,1)S(1)}, bf16[512,256]{1,0:T(8,128)(2,1)S(1)}, u32[]{:S(2)}, u32[]{:S(2)}) %collective-permute-start.10) | collective-permute-done | bytes 262176 | tf_op jit(solution)/shard_map/ppermute | solution.py:265
  32.9 0.9 %collective-permute-start.11 = (bf16[256,256]{1,0:T(8,128)(2,1)S(1)}, bf16[256,256]{1,0:T(8,128)(2,1)S(1)}, u32[]{:S(2)}, u32[]{:S(2)}) collective-permute-start(bf16[256,256]{1,0:T(8,128)(2,1)S(1)} %get-tuple-element.46), channel_id=1, source_target_pairs={{0,2},{1,3},{2,0},{3,1},{4,6},{5,7},{6,4},{7,5},{8,10},{9,11},{10,... | collective-permute-start | bytes 393224 | tf_op jit(solution)/shard_map/ppermute | solution.py:265
  33.8 3.6 %collective-permute-done.5.refs_0_ = bf16[256,256]{1,0:T(8,128)(2,1)S(1)} collective-permute-done((bf16[256,256]{1,0:T(8,128)(2,1)S(1)}, bf16[256,256]{1,0:T(8,128)(2,1)S(1)}, u32[]{:S(2)}, u32[]{:S(2)}) %collective-permute-start.5) | collective-permute-done | bytes 131104 | tf_op jit(solution)/shard_map/ppermute | solution.py:265
  37.4 1.9 %collective-permute-done.8.refs_0_ = bf16[512,256]{1,0:T(8,128)(2,1)S(1)} collective-permute-done((bf16[512,256]{1,0:T(8,128)(2,1)S(1)}, bf16[512,256]{1,0:T(8,128)(2,1)S(1)}, u32[]{:S(2)}, u32[]{:S(2)}) %collective-permute-start.8) | collective-permute-done | bytes 262176 | tf_op jit(solution)/shard_map/ppermute | solution.py:265
  39.4 1.6 %collective-permute-start.9 = (bf16[256,256]{1,0:T(8,128)(2,1)S(1)}, bf16[256,256]{1,0:T(8,128)(2,1)S(1)}, u32[]{:S(2)}, u32[]{:S(2)}) collective-permute-start(bf16[256,256]{1,0:T(8,128)(2,1)S(1)} %get-tuple-element.44), channel_id=1, source_target_pairs={{0,4},{1,5},{2,6},{3,7},{4,0},{5,1},{6,2},{7,3},{8,12},{9,13},{10,... | collective-permute-start | bytes 393224 | tf_op jit(solution)/shard_map/ppermute | solution.py:265
  41.0 0.2 collective-permute-done.11.refs_0_
  41.2 1.3 %collective-permute-start.12 = (bf16[128,256]{1,0:T(8,128)(2,1)S(1)}, bf16[128,256]{1,0:T(8,128)(2,1)S(1)}, u32[]{:S(2)}, u32[]{:S(2)}) collective-permute-start(bf16[128,256]{1,0:T(8,128)(2,1)S(1)} %get-tuple-element.48), channel_id=1, source_target_pairs={{0,4},{1,5},{2,6},{3,7},{4,0},{5,1},{6,2},{7,3},{8,12},{9,13},{10,... | collective-permute-start | bytes 196616 | tf_op jit(solution)/shard_map/ppermute | solution.py:265
  42.5 1.2 %collective-permute-start.6 = (bf16[128,256]{1,0:T(8,128)(2,1)S(1)}, bf16[128,256]{1,0:T(8,128)(2,1)S(1)}, u32[]{:S(2)}, u32[]{:S(2)}) collective-permute-start(bf16[128,256]{1,0:T(8,128)(2,1)S(1)} %get-tuple-element.36), channel_id=1, source_target_pairs={{0,1},{1,0},{2,3},{3,2},{4,5},{5,4},{6,7},{7,6},{8,9},{9,8},{10,11... | collective-permute-start | bytes 196616 | tf_op jit(solution)/shard_map/ppermute | solution.py:265
  43.7 5.0 %collective-permute-done.12.refs_5_ = bf16[128,256]{1,0:T(8,128)(2,1)S(1)} collective-permute-done((bf16[128,256]{1,0:T(8,128)(2,1)S(1)}, bf16[128,256]{1,0:T(8,128)(2,1)S(1)}, u32[]{:S(2)}, u32[]{:S(2)}) %collective-permute-start.12) | collective-permute-done | bytes 65568 | tf_op jit(solution)/shard_map/ppermute | solution.py:265
  48.7 1.2 %layer.1 = bf16[1024,256]{1,0:T(8,128)(2,1)} custom-call(f32[128,256]{1,0:T(8,128)S(1)} %get-tuple-element.35.refs_0_, bf16[128,256]{1,0:T(8,128)(2,1)S(1)} %collective-permute-done.6.refs_1_, f32[256,256]{1,0:T(8,128)S(1)} %get-tuple-element.43.refs_2_, bf16[256,256]{1,0:T(8,128)(2,1)S(1)} %collective-permute-done.9.refs_3_, ...), custom_call_target="tpu_custom_call" | custom-call | tf_op jit(solution)/shard_map/layer/pallas_call | solution.py:255
  (17 shorter events, 0.2 us)
Async XLA Ops:
  0.0 7.8 %copy-start = (bf16[4096,32]{0,1:T(8,128)(2,1)S(1)}, bf16[4096,32]{0,1:T(8,128)(2,1)}, u32[]{:S(2)}) copy-start(bf16[4096,32]{0,1:T(8,128)(2,1)} %param.6) | copy-start | bytes 786436
  0.0 7.7 %collective-permute-start = (bf16[32,4096]{1,0:T(8,128)(2,1)}, bf16[32,4096]{1,0:T(8,128)(2,1)S(1)}, u32[]{:S(2)}, u32[]{:S(2)}) collective-permute-start(bf16[32,4096]{1,0:T(8,128)(2,1)} %bitcast.3), channel_id=1, source_target_pairs={{0,8},{8,0},{16,24},{24,16},{1,9},{9,1},{17,25},{25,17},{2,10},{10... | collective-permute-start | bytes 786440 | tf_op jit(solution)/shard_map/ppermute | solution.py:265
  0.5 9.7 %collective-permute-start.1 = (bf16[32,4096]{1,0:T(8,128)(2,1)}, bf16[32,4096]{1,0:T(8,128)(2,1)S(1)}, u32[]{:S(2)}, u32[]{:S(2)}) collective-permute-start(bf16[32,4096]{1,0:T(8,128)(2,1)} %bitcast.4), channel_id=1, source_target_pairs={{0,16},{8,24},{16,0},{24,8},{1,17},{9,25},{17,1},{25,9},{2,18},{10... | collective-permute-start | bytes 786440 | tf_op jit(solution)/shard_map/ppermute | solution.py:265
  3.7 0.7 %copy-start.2 = (s32[1,384]{1,0:T(1,128)S(1)}, s32[1,384]{1,0:T(1,128)}, u32[]{:S(2)}) copy-start(s32[1,384]{1,0:T(1,128)} %codes_hbm.1) | copy-start | bytes 4612
  10.2 2.8 %collective-permute-start.2 = (bf16[32,4096]{1,0:T(8,128)(2,1)S(1)}, bf16[32,4096]{1,0:T(8,128)(2,1)S(1)}, u32[]{:S(2)}, u32[]{:S(2)}) collective-permute-start(bf16[32,4096]{1,0:T(8,128)(2,1)S(1)} %collective-permute-done.1.refs_0_), channel_id=1, source_target_pairs={{0,8},{8,0},{16,24},{24,16},{1,9},{9,1},{17,25},{25,17},{2,10},{10... | collective-permute-start | bytes 786440 | tf_op jit(solution)/shard_map/ppermute | solution.py:265
  11.0 11.0 %collective-permute-start.3 = (bf16[1024,128]{1,0:T(8,128)(2,1)S(1)}, bf16[1024,128]{1,0:T(8,128)(2,1)S(1)}, u32[]{:S(2)}, u32[]{:S(2)}) collective-permute-start(bf16[1024,128]{1,0:T(8,128)(2,1)S(1)} %product_send.4), channel_id=1, source_target_pairs={{0,1},{1,0},{2,3},{3,2},{4,5},{5,4},{6,7},{7,6},{8,9},{9,8},{10,11... | collective-permute-start | bytes 786440 | tf_op jit(solution)/shard_map/ppermute | solution.py:265
  14.9 8.7 %collective-permute-start.4 = (bf16[512,256]{1,0:T(8,128)(2,1)S(1)}, bf16[512,256]{1,0:T(8,128)(2,1)S(1)}, u32[]{:S(2)}, u32[]{:S(2)}) collective-permute-start(bf16[512,256]{1,0:T(8,128)(2,1)S(1)} %product_send.5), channel_id=1, source_target_pairs={{0,2},{1,3},{2,0},{3,1},{4,6},{5,7},{6,4},{7,5},{8,10},{9,11},{10,... | collective-permute-start | bytes 786440 | tf_op jit(solution)/shard_map/ppermute | solution.py:265
  18.3 9.2 %collective-permute-start.7 = (bf16[1024,128]{1,0:T(8,128)(2,1)S(1)}, bf16[1024,128]{1,0:T(8,128)(2,1)S(1)}, u32[]{:S(2)}, u32[]{:S(2)}) collective-permute-start(bf16[1024,128]{1,0:T(8,128)(2,1)S(1)} %product_send.6), channel_id=1, source_target_pairs={{0,1},{1,0},{2,3},{3,2},{4,5},{5,4},{6,7},{7,6},{8,9},{9,8},{10,11... | collective-permute-start | bytes 786440 | tf_op jit(solution)/shard_map/ppermute | solution.py:265
  20.5 12.3 %collective-permute-start.10 = (bf16[512,256]{1,0:T(8,128)(2,1)S(1)}, bf16[512,256]{1,0:T(8,128)(2,1)S(1)}, u32[]{:S(2)}, u32[]{:S(2)}) collective-permute-start(bf16[512,256]{1,0:T(8,128)(2,1)S(1)} %product_send.7), channel_id=1, source_target_pairs={{0,1},{1,0},{2,3},{3,2},{4,5},{5,4},{6,7},{7,6},{8,9},{9,8},{10,11... | collective-permute-start | bytes 786440 | tf_op jit(solution)/shard_map/ppermute | solution.py:265
  27.5 21.2 %copy-start.1 = (bf16[128,256]{1,0:T(8,128)(2,1)S(1)}, bf16[128,256]{1,0:T(8,128)(2,1)}, u32[]{:S(2)}) copy-start(bf16[128,256]{1,0:T(8,128)(2,1)} %refs_6_.1) | copy-start | bytes 196612
  27.5 21.2 %copy-start.3 = (f32[256]{0:T(256)S(1)}, f32[256]{0:T(256)}, u32[]{:S(2)}) copy-start(f32[256]{0:T(256)} %param.11) | copy-start | bytes 3076
  27.7 11.7 %collective-permute-start.8 = (bf16[512,256]{1,0:T(8,128)(2,1)S(1)}, bf16[512,256]{1,0:T(8,128)(2,1)S(1)}, u32[]{:S(2)}, u32[]{:S(2)}) collective-permute-start(bf16[512,256]{1,0:T(8,128)(2,1)S(1)} %get-tuple-element.41), channel_id=1, source_target_pairs={{0,2},{1,3},{2,0},{3,1},{4,6},{5,7},{6,4},{7,5},{8,10},{9,11},{10,... | collective-permute-start | bytes 786440 | tf_op jit(solution)/shard_map/ppermute | solution.py:265
  29.3 8.1 %collective-permute-start.5 = (bf16[256,256]{1,0:T(8,128)(2,1)S(1)}, bf16[256,256]{1,0:T(8,128)(2,1)S(1)}, u32[]{:S(2)}, u32[]{:S(2)}) collective-permute-start(bf16[256,256]{1,0:T(8,128)(2,1)S(1)} %get-tuple-element.34), channel_id=1, source_target_pairs={{0,4},{1,5},{2,6},{3,7},{4,0},{5,1},{6,2},{7,3},{8,12},{9,13},{10,... | collective-permute-start | bytes 393224 | tf_op jit(solution)/shard_map/ppermute | solution.py:265
  32.9 8.2 %collective-permute-start.11 = (bf16[256,256]{1,0:T(8,128)(2,1)S(1)}, bf16[256,256]{1,0:T(8,128)(2,1)S(1)}, u32[]{:S(2)}, u32[]{:S(2)}) collective-permute-start(bf16[256,256]{1,0:T(8,128)(2,1)S(1)} %get-tuple-element.46), channel_id=1, source_target_pairs={{0,2},{1,3},{2,0},{3,1},{4,6},{5,7},{6,4},{7,5},{8,10},{9,11},{10,... | collective-permute-start | bytes 393224 | tf_op jit(solution)/shard_map/ppermute | solution.py:265
  39.4 9.3 %collective-permute-start.9 = (bf16[256,256]{1,0:T(8,128)(2,1)S(1)}, bf16[256,256]{1,0:T(8,128)(2,1)S(1)}, u32[]{:S(2)}, u32[]{:S(2)}) collective-permute-start(bf16[256,256]{1,0:T(8,128)(2,1)S(1)} %get-tuple-element.44), channel_id=1, source_target_pairs={{0,4},{1,5},{2,6},{3,7},{4,0},{5,1},{6,2},{7,3},{8,12},{9,13},{10,... | collective-permute-start | bytes 393224 | tf_op jit(solution)/shard_map/ppermute | solution.py:265
  41.2 7.6 %collective-permute-start.12 = (bf16[128,256]{1,0:T(8,128)(2,1)S(1)}, bf16[128,256]{1,0:T(8,128)(2,1)S(1)}, u32[]{:S(2)}, u32[]{:S(2)}) collective-permute-start(bf16[128,256]{1,0:T(8,128)(2,1)S(1)} %get-tuple-element.48), channel_id=1, source_target_pairs={{0,4},{1,5},{2,6},{3,7},{4,0},{5,1},{6,2},{7,3},{8,12},{9,13},{10,... | collective-permute-start | bytes 196616 | tf_op jit(solution)/shard_map/ppermute | solution.py:265
  42.5 6.2 %collective-permute-start.6 = (bf16[128,256]{1,0:T(8,128)(2,1)S(1)}, bf16[128,256]{1,0:T(8,128)(2,1)S(1)}, u32[]{:S(2)}, u32[]{:S(2)}) collective-permute-start(bf16[128,256]{1,0:T(8,128)(2,1)S(1)} %get-tuple-element.36), channel_id=1, source_target_pairs={{0,1},{1,0},{2,3},{3,2},{4,5},{5,4},{6,7},{7,6},{8,9},{9,8},{10,11... | collective-permute-start | bytes 196616 | tf_op jit(solution)/shard_map/ppermute | solution.py:265

commit v5 on v3

--- a/solution.py
+++ b/solution.py
@@ -11,7 +11,7 @@
 PAIR = BLK // 2
 LANES = 2 * BLK
 GROUP = 16
-STEPS = 4
+TOGETHER = 4
 UNROLL = 16
 SLOT_AT, SOURCE_AT = 13, 7
 MIB = 1024 * 1024
@@ -65,29 +65,33 @@
 def relayout_kernel(chunks, col_bits, count_ref, codes_hbm, values_hbm, out_ref, words_ref, codes, held, scratch, arrived, codes_arrived):
     codes_copy = pltpu.make_async_copy(codes_hbm, codes, codes_arrived)
     codes_copy.start()
-    step = values_hbm.shape[0] // STEPS
-    copies = []
-    for k in range(STEPS):
-        rows = pl.ds(k * step, step)
-        copies.append(pltpu.make_async_copy(values_hbm.at[rows], held.at[rows], arrived.at[k]))
-        copies[k].start()
+    step = GROUP * TOGETHER
+
+    def copy(k):
+        rows = pl.ds(pl.multiple_of(k * step, step), step)
+        return pltpu.make_async_copy(values_hbm.at[rows], held.at[rows], arrived.at[k])
+
+    steps = values_hbm.shape[0] // step
+    for k in range(steps):
+        copy(k).start()
     codes_copy.wait()
     make_lists(chunks, col_bits, count_ref[0, 0], codes[...], words_ref)
 
-    def one(g, carry):
-        slots = pl.ds(pl.multiple_of(g * GROUP, GROUP), GROUP)
-        base = pl.multiple_of(g * (GROUP * PAIR), GROUP * PAIR)
-        for p in range(PAIR):
-            scratch[pl.ds(base + p * GROUP, GROUP), :] = held[slots, p * LANES : (p + 1) * LANES].astype(jnp.float32)
-        for s in range(GROUP):
-            rows = scratch[pl.ds(base + s, PAIR, stride=GROUP), :]
-            out_ref[pl.ds(base + s * PAIR, PAIR), :] = rows.astype(out_ref.dtype)
+    def one(k, carry):
+        copy(k).wait()
+        for g in range(TOGETHER):
+            slots = pl.ds(pl.multiple_of(k * step + g * GROUP, GROUP), GROUP)
+            for p in range(PAIR):
+                wide = held[slots, p * LANES : (p + 1) * LANES].astype(jnp.float32)
+                scratch[(g * PAIR + p) * GROUP : (g * PAIR + p + 1) * GROUP, :] = wide
+        for g in range(TOGETHER):
+            for s in range(GROUP):
+                rows = scratch[pl.ds(g * PAIR * GROUP + s, PAIR, stride=GROUP), :]
+                at = pl.multiple_of((k * step + g * GROUP + s) * PAIR, PAIR)
+                out_ref[pl.ds(at, PAIR), :] = rows.astype(out_ref.dtype)
         return carry
 
-    groups = step // GROUP
-    for k in range(STEPS):
-        copies[k].wait()
-        lax.fori_loop(k * groups, (k + 1) * groups, one, 0, unroll=2)
+    lax.fori_loop(0, steps, one, 0)
 
 
 def relayout(chunks, col_bits, count, codes, values):
@@ -103,8 +107,8 @@
         scratch_shapes=[
             pltpu.VMEM(codes.shape, codes.dtype),
             pltpu.VMEM(values.shape, values.dtype),
-            pltpu.VMEM((slots * PAIR, LANES), jnp.float32),
-            pltpu.SemaphoreType.DMA((STEPS,)),
+            pltpu.VMEM((TOGETHER * GROUP * PAIR, LANES), jnp.float32),
+            pltpu.SemaphoreType.DMA((slots // (GROUP * TOGETHER),)),
             pltpu.SemaphoreType.DMA,
         ],
         cost_estimate=pl.CostEstimate(flops=0, bytes_accessed=4 * slots * BLK * BLK, transcendentals=0),
@@ -115,10 +119,11 @@
 
 def table_kernel(*refs):
     parts, table = refs[:-1], refs[-1]
+    kind = table.dtype if parts[0].shape[0] % 16 == 0 else jnp.float32
 
     def build(q, carry):
         at = pl.ds(pl.multiple_of(q * LANES, LANES), LANES)
-        x = [part[:, at].astype(jnp.float32) for part in parts]
+        x = [part[:, at].astype(kind) for part in parts]
         table[at, :] = jnp.concatenate(x + x, axis=0).T.astype(table.dtype)
         return carry
 

time: 48.7 us -> 47.8 us (0.982)
  starting transfers between devices: 24.4 us -> 22.6 us
  waiting for transfers between devices: 11.5 us -> 12.3 us
    ppermute x13, starting transfers between devices: 24.4 us -> 22.6 us  [exchange(): return lax.ppermute(x, axis, [(i, i ^ 1 << bit) for i in range(size)])]
    ppermute x13, waiting for transfers between devices: 11.5 us -> 12.3 us  [exchange(): return lax.ppermute(x, axis, [(i, i ^ 1 << bit) for i in range(size)])]
  transfers between devices with their start and end apart: 13 -> 13, of which waited for: 5 -> 6; matrix products, arithmetic and copies ran while one was open for 0% -> 0% of each run, Pallas kernels for 21% -> 21%
where the time goes in v5:
time: 47.8 us
  starting transfers between devices  22.6 us (47%)
  waiting for transfers between devices  12.3 us (26%)
  Pallas kernels  11.4 us (24%)
  between operations  0.77 us (2%)
  local copies, waits for them, and re-layouts  0.69 us (1%)
    ppermute x13, starting transfers between devices, exchange(): return lax.ppermute(x, axis, [(i, i ^ 1 << bit) for i in range(size)])  22.6 us
    ppermute x13, waiting for transfers between devices, exchange(): return lax.ppermute(x, axis, [(i, i ^ 1 << bit) for i in range(size)])  12.3 us
    pallas_call x5, Pallas kernels, product(): pl.pallas_call(functools.partial(product_kernel, trash, group, len(tables...  5.2 us
    pallas_call x1, Pallas kernels, relayout(): pl.pallas_call(functools.partial(relayout_kernel, chunks, col_bits), in_s...  3.24 us
    pallas_call x2, Pallas kernels, make_table(): pl.pallas_call(table_kernel, in_specs=[VMEM] * len(parts), out_specs=VMEM...  1.49 us
    pallas_call x1, Pallas kernels, layer(): pl.pallas_call(functools.partial(layer_kernel, index), out_shape=jax.Shap...  1.19 us
  transfers between devices with their start and end apart: 13, of which 6 were waited for; matrix products, arithmetic and copies ran while one was open for 0% of the time, Pallas kernels for 21%

profile of v5, /device:TPU:0, one launch (start us, length us, event | category | flops | bytes accessed | tf_op | source)
XLA Modules:
  0.0 47.8 jit_solution(10326415384277381670)
XLA Ops:
  0.0 0.5 collective-permute-start.1
  0.5 2.6 %collective-permute-start = (bf16[32,4096]{1,0:T(8,128)(2,1)}, bf16[32,4096]{1,0:T(8,128)(2,1)S(1)}, u32[]{:S(2)}, u32[]{:S(2)}) collective-permute-start(bf16[32,4096]{1,0:T(8,128)(2,1)} %bitcast.4), channel_id=1, source_target_pairs={{0,16},{8,24},{16,0},{24,8},{1,17},{9,25},{17,1},{25,9},{2,18},{10... | collective-permute-start | bytes 786440 | tf_op jit(solution)/shard_map/ppermute | solution.py:270
  3.7 0.7 %copy-done.2 = s32[1,384]{1,0:T(1,128)S(1)} copy-done((s32[1,384]{1,0:T(1,128)S(1)}, s32[1,384]{1,0:T(1,128)}, u32[]{:S(2)}) %copy-start.2) | copy-done | bytes 1560
  4.4 3.2 %relayout.1 = (bf16[12288,128]{1,0:T(8,128)(2,1)S(1)}, s32[1,512]{1,0:T(1,128)S(1)}) custom-call(s32[1,1]{1,0:T(1,128)S(6)} %copy.7.count_ref, s32[1,384]{1,0:T(1,128)S(1)} %copy-done.2, bf16[384,4096]{1,0:T(8,128)(2,1)} %bitcast.7), custom_call_target="tpu_custom_call" | custom-call | bytes 6291456 | tf_op jit(solution)/shard_map/relayout/pallas_call | solution.py:99
  7.6 0.7 %table.2.refs_0_ = bf16[4096,128]{1,0:T(8,128)(2,1)S(1)} custom-call(bf16[32,4096]{1,0:T(8,128)(2,1)S(1)} %bitcast.5, bf16[32,4096]{1,0:T(8,128)(2,1)S(1)} %collective-permute-done.1.refs_1_), custom_call_target="tpu_custom_call" | custom-call | flops 1 | bytes 1 | tf_op jit(solution)/shard_map/table/pallas_call | solution.py:135
  8.4 1.0 %product_send.4 = bf16[1024,128]{1,0:T(8,128)(2,1)S(1)} custom-call(s32[1,512]{1,0:T(1,128)S(1)} %get-tuple-element.26.words_ref, bf16[12288,128]{1,0:T(8,128)(2,1)S(1)} %get-tuple-element.24.blocks_ref, bf16[4096,128]{1,0:T(8,128)(2,1)S(1)} %table.2.refs_0_), custom_call_target="tpu_custom_call" | custom-call | flops 1 | bytes 1 | tf_op jit(solution)/shard_map/product_send/pallas_call | solution.py:192
  9.4 0.7 %collective-permute-done.refs_0_ = bf16[32,4096]{1,0:T(8,128)(2,1)S(1)} collective-permute-done((bf16[32,4096]{1,0:T(8,128)(2,1)}, bf16[32,4096]{1,0:T(8,128)(2,1)S(1)}, u32[]{:S(2)}, u32[]{:S(2)}) %collective-permute-start) | collective-permute-done | bytes 262176 | tf_op jit(solution)/shard_map/ppermute | solution.py:270
  10.2 0.2 collective-permute-start.3
  10.4 1.7 %collective-permute-start.2 = (bf16[1024,128]{1,0:T(8,128)(2,1)S(1)}, bf16[1024,128]{1,0:T(8,128)(2,1)S(1)}, u32[]{:S(2)}, u32[]{:S(2)}) collective-permute-start(bf16[1024,128]{1,0:T(8,128)(2,1)S(1)} %product_send.4), channel_id=1, source_target_pairs={{0,1},{1,0},{2,3},{3,2},{4,5},{5,4},{6,7},{7,6},{8,9},{9,8},{10,11... | collective-permute-start | bytes 786440 | tf_op jit(solution)/shard_map/ppermute | solution.py:270
  12.1 0.7 %table.3.refs_1_.refs_0_ = bf16[4096,128]{1,0:T(8,128)(2,1)S(1)} custom-call(bf16[32,4096]{1,0:T(8,128)(2,1)S(1)} %collective-permute-done.refs_0_, bf16[32,4096]{1,0:T(8,128)(2,1)S(1)} %collective-permute-done.3.refs_1_), custom_call_target="tpu_custom_call" | custom-call | flops 1 | bytes 1 | tf_op jit(solution)/shard_map/table/pallas_call | solution.py:135
  12.8 1.0 %product_send.5 = bf16[1024,128]{1,0:T(8,128)(2,1)S(1)} custom-call(s32[1,512]{1,0:T(1,128)S(1)} %get-tuple-element.26.words_ref, bf16[12288,128]{1,0:T(8,128)(2,1)S(1)} %get-tuple-element.24.blocks_ref, bf16[4096,128]{1,0:T(8,128)(2,1)S(1)} %table.3.refs_1_.refs_0_), custom_call_target="tpu_custom_call" | custom-call | flops 1 | bytes 1 | tf_op jit(solution)/shard_map/product_send/pallas_call | solution.py:192
  13.8 2.5 %collective-permute-start.4 = (bf16[1024,128]{1,0:T(8,128)(2,1)S(1)}, bf16[1024,128]{1,0:T(8,128)(2,1)S(1)}, u32[]{:S(2)}, u32[]{:S(2)}) collective-permute-start(bf16[1024,128]{1,0:T(8,128)(2,1)S(1)} %product_send.5), channel_id=1, source_target_pairs={{0,1},{1,0},{2,3},{3,2},{4,5},{5,4},{6,7},{7,6},{8,9},{9,8},{10,11... | collective-permute-start | bytes 786440 | tf_op jit(solution)/shard_map/ppermute | solution.py:270
  16.3 1.0 %product_send.7 = bf16[512,256]{1,0:T(8,128)(2,1)S(1)} custom-call(s32[1,512]{1,0:T(1,128)S(1)} %get-tuple-element.26.words_ref, bf16[12288,128]{1,0:T(8,128)(2,1)S(1)} %get-tuple-element.24.blocks_ref, bf16[4096,128]{1,0:T(8,128)(2,1)S(1)} %table.2.refs_0_, bf16[4096,128]{1,0:T(8,128)(2,1)S(1)} %table.3.refs_1_.refs_0_), custom_call_target="tpu_custom_call" | custom-call | flops 1 | bytes 1 | tf_op jit(solution)/shard_map/product_send/pallas_call | solution.py:192
  17.4 2.2 %collective-permute-start.10 = (bf16[512,256]{1,0:T(8,128)(2,1)S(1)}, bf16[512,256]{1,0:T(8,128)(2,1)S(1)}, u32[]{:S(2)}, u32[]{:S(2)}) collective-permute-start(bf16[512,256]{1,0:T(8,128)(2,1)S(1)} %product_send.7), channel_id=1, source_target_pairs={{0,2},{1,3},{2,0},{3,1},{4,6},{5,7},{6,4},{7,5},{8,10},{9,11},{10,... | collective-permute-start | bytes 786440 | tf_op jit(solution)/shard_map/ppermute | solution.py:270
  19.6 1.0 %product_send.6 = bf16[512,256]{1,0:T(8,128)(2,1)S(1)} custom-call(s32[1,512]{1,0:T(1,128)S(1)} %get-tuple-element.26.words_ref, bf16[12288,128]{1,0:T(8,128)(2,1)S(1)} %get-tuple-element.24.blocks_ref, bf16[4096,128]{1,0:T(8,128)(2,1)S(1)} %table.2.refs_0_, bf16[4096,128]{1,0:T(8,128)(2,1)S(1)} %table.3.refs_1_.refs_0_), custom_call_target="tpu_custom_call" | custom-call | flops 1 | bytes 1 | tf_op jit(solution)/shard_map/product_send/pallas_call | solution.py:192
  20.6 1.2 %collective-permute-start.7 = (bf16[512,256]{1,0:T(8,128)(2,1)S(1)}, bf16[512,256]{1,0:T(8,128)(2,1)S(1)}, u32[]{:S(2)}, u32[]{:S(2)}) collective-permute-start(bf16[512,256]{1,0:T(8,128)(2,1)S(1)} %product_send.6), channel_id=1, source_target_pairs={{0,1},{1,0},{2,3},{3,2},{4,5},{5,4},{6,7},{7,6},{8,9},{9,8},{10,11... | collective-permute-start | bytes 786440 | tf_op jit(solution)/shard_map/ppermute | solution.py:270
  21.8 1.1 %product_keep.1.keep_ref = f32[2080,256]{1,0:T(8,128)S(1)} custom-call(s32[1,512]{1,0:T(1,128)S(1)} %get-tuple-element.26.words_ref, bf16[12288,128]{1,0:T(8,128)(2,1)S(1)} %get-tuple-element.24.blocks_ref, bf16[4096,128]{1,0:T(8,128)(2,1)S(1)} %table.2.refs_0_, bf16[4096,128]{1,0:T(8,128)(2,1)S(1)} %table.3.refs_1_.refs_0_), custom_call_target="tpu_custom_call" | custom-call | flops 1 | bytes 1 | tf_op jit(solution)/shard_map/product_keep/pallas_call | solution.py:192
  22.9 2.2 %collective-permute-done.4.refs_1_ = bf16[1024,128]{1,0:T(8,128)(2,1)S(1)} collective-permute-done((bf16[1024,128]{1,0:T(8,128)(2,1)S(1)}, bf16[1024,128]{1,0:T(8,128)(2,1)S(1)}, u32[]{:S(2)}, u32[]{:S(2)}) %collective-permute-start.4) | collective-permute-done | bytes 262176 | tf_op jit(solution)/shard_map/ppermute | solution.py:270
  25.1 0.1 add.6
  25.3 1.6 %collective-permute-start.5 = (bf16[512,256]{1,0:T(8,128)(2,1)S(1)}, bf16[512,256]{1,0:T(8,128)(2,1)S(1)}, u32[]{:S(2)}, u32[]{:S(2)}) collective-permute-start(bf16[512,256]{1,0:T(8,128)(2,1)S(1)} %get-tuple-element.30), channel_id=1, source_target_pairs={{0,2},{1,3},{2,0},{3,1},{4,6},{5,7},{6,4},{7,5},{8,10},{9,11},{10,... | collective-permute-start | bytes 786440 | tf_op jit(solution)/shard_map/ppermute | solution.py:270
  26.9 3.1 %collective-permute-start.11 = (bf16[256,256]{1,0:T(8,128)(2,1)S(1)}, bf16[256,256]{1,0:T(8,128)(2,1)S(1)}, u32[]{:S(2)}, u32[]{:S(2)}) collective-permute-start(bf16[256,256]{1,0:T(8,128)(2,1)S(1)} %get-tuple-element.38), channel_id=1, source_target_pairs={{0,4},{1,5},{2,6},{3,7},{4,0},{5,1},{6,2},{7,3},{8,12},{9,13},{10,... | collective-permute-start | bytes 393224 | tf_op jit(solution)/shard_map/ppermute | solution.py:270
  30.1 0.1 collective-permute-done.7.refs_0_
  30.2 0.1 add.8
  30.2 1.9 %collective-permute-start.8 = (bf16[256,256]{1,0:T(8,128)(2,1)S(1)}, bf16[256,256]{1,0:T(8,128)(2,1)S(1)}, u32[]{:S(2)}, u32[]{:S(2)}) collective-permute-start(bf16[256,256]{1,0:T(8,128)(2,1)S(1)} %get-tuple-element.34), channel_id=1, source_target_pairs={{0,2},{1,3},{2,0},{3,1},{4,6},{5,7},{6,4},{7,5},{8,10},{9,11},{10,... | collective-permute-start | bytes 393224 | tf_op jit(solution)/shard_map/ppermute | solution.py:270
  32.2 5.0 %collective-permute-done.5.refs_0_ = bf16[512,256]{1,0:T(8,128)(2,1)S(1)} collective-permute-done((bf16[512,256]{1,0:T(8,128)(2,1)S(1)}, bf16[512,256]{1,0:T(8,128)(2,1)S(1)}, u32[]{:S(2)}, u32[]{:S(2)}) %collective-permute-start.5) | collective-permute-done | bytes 262176 | tf_op jit(solution)/shard_map/ppermute | solution.py:270
  37.2 0.1 add.7
  37.2 1.8 %collective-permute-start.6 = (bf16[256,256]{1,0:T(8,128)(2,1)S(1)}, bf16[256,256]{1,0:T(8,128)(2,1)S(1)}, u32[]{:S(2)}, u32[]{:S(2)}) collective-permute-start(bf16[256,256]{1,0:T(8,128)(2,1)S(1)} %get-tuple-element.32), channel_id=1, source_target_pairs={{0,4},{1,5},{2,6},{3,7},{4,0},{5,1},{6,2},{7,3},{8,12},{9,13},{10,... | collective-permute-start | bytes 393224 | tf_op jit(solution)/shard_map/ppermute | solution.py:270
  39.0 1.4 %collective-permute-start.12 = (bf16[128,256]{1,0:T(8,128)(2,1)S(1)}, bf16[128,256]{1,0:T(8,128)(2,1)S(1)}, u32[]{:S(2)}, u32[]{:S(2)}) collective-permute-start(bf16[128,256]{1,0:T(8,128)(2,1)S(1)} %get-tuple-element.40), channel_id=1, source_target_pairs={{0,1},{1,0},{2,3},{3,2},{4,5},{5,4},{6,7},{7,6},{8,9},{9,8},{10,11... | collective-permute-start | bytes 196616 | tf_op jit(solution)/shard_map/ppermute | solution.py:270
  40.4 2.0 %collective-permute-start.9 = (bf16[128,256]{1,0:T(8,128)(2,1)S(1)}, bf16[128,256]{1,0:T(8,128)(2,1)S(1)}, u32[]{:S(2)}, u32[]{:S(2)}) collective-permute-start(bf16[128,256]{1,0:T(8,128)(2,1)S(1)} %get-tuple-element.36), channel_id=1, source_target_pairs={{0,4},{1,5},{2,6},{3,7},{4,0},{5,1},{6,2},{7,3},{8,12},{9,13},{10,... | collective-permute-start | bytes 196616 | tf_op jit(solution)/shard_map/ppermute | solution.py:270
  42.5 0.9 %collective-permute-done.12.refs_5_ = bf16[128,256]{1,0:T(8,128)(2,1)S(1)} collective-permute-done((bf16[128,256]{1,0:T(8,128)(2,1)S(1)}, bf16[128,256]{1,0:T(8,128)(2,1)S(1)}, u32[]{:S(2)}, u32[]{:S(2)}) %collective-permute-start.12) | collective-permute-done | bytes 65568 | tf_op jit(solution)/shard_map/ppermute | solution.py:270
  43.4 3.2 %collective-permute-done.9.refs_3_ = bf16[128,256]{1,0:T(8,128)(2,1)S(1)} collective-permute-done((bf16[128,256]{1,0:T(8,128)(2,1)S(1)}, bf16[128,256]{1,0:T(8,128)(2,1)S(1)}, u32[]{:S(2)}, u32[]{:S(2)}) %collective-permute-start.9) | collective-permute-done | bytes 65568 | tf_op jit(solution)/shard_map/ppermute | solution.py:270
  46.6 1.2 %layer.1 = bf16[1024,256]{1,0:T(8,128)(2,1)} custom-call(f32[256,256]{1,0:T(8,128)S(1)} %get-tuple-element.31.refs_0_, bf16[256,256]{1,0:T(8,128)(2,1)S(1)} %collective-permute-done.6.refs_1_, f32[128,256]{1,0:T(8,128)S(1)} %get-tuple-element.35.refs_2_, bf16[128,256]{1,0:T(8,128)(2,1)S(1)} %collective-permute-done.9.refs_3_, ...), custom_call_target="tpu_custom_call" | custom-call | tf_op jit(solution)/shard_map/layer/pallas_call | solution.py:260
  (17 shorter events, 0.1 us)
Async XLA Ops:
  0.0 7.6 %copy-start = (bf16[4096,32]{0,1:T(8,128)(2,1)S(1)}, bf16[4096,32]{0,1:T(8,128)(2,1)}, u32[]{:S(2)}) copy-start(bf16[4096,32]{0,1:T(8,128)(2,1)} %param.6) | copy-start | bytes 786436
  0.0 7.6 %collective-permute-start.1 = (bf16[32,4096]{1,0:T(8,128)(2,1)}, bf16[32,4096]{1,0:T(8,128)(2,1)S(1)}, u32[]{:S(2)}, u32[]{:S(2)}) collective-permute-start(bf16[32,4096]{1,0:T(8,128)(2,1)} %bitcast.3), channel_id=1, source_target_pairs={{0,8},{8,0},{16,24},{24,16},{1,9},{9,1},{17,25},{25,17},{2,10},{10... | collective-permute-start | bytes 786440 | tf_op jit(solution)/shard_map/ppermute | solution.py:270
  0.5 9.7 %collective-permute-start = (bf16[32,4096]{1,0:T(8,128)(2,1)}, bf16[32,4096]{1,0:T(8,128)(2,1)S(1)}, u32[]{:S(2)}, u32[]{:S(2)}) collective-permute-start(bf16[32,4096]{1,0:T(8,128)(2,1)} %bitcast.4), channel_id=1, source_target_pairs={{0,16},{8,24},{16,0},{24,8},{1,17},{9,25},{17,1},{25,9},{2,18},{10... | collective-permute-start | bytes 786440 | tf_op jit(solution)/shard_map/ppermute | solution.py:270
  3.7 0.7 %copy-start.2 = (s32[1,384]{1,0:T(1,128)S(1)}, s32[1,384]{1,0:T(1,128)}, u32[]{:S(2)}) copy-start(s32[1,384]{1,0:T(1,128)} %codes_hbm.1) | copy-start | bytes 4612
  10.2 1.9 %collective-permute-start.3 = (bf16[32,4096]{1,0:T(8,128)(2,1)S(1)}, bf16[32,4096]{1,0:T(8,128)(2,1)S(1)}, u32[]{:S(2)}, u32[]{:S(2)}) collective-permute-start(bf16[32,4096]{1,0:T(8,128)(2,1)S(1)} %collective-permute-done.refs_0_), channel_id=1, source_target_pairs={{0,8},{8,0},{16,24},{24,16},{1,9},{9,1},{17,25},{25,17},{2,10},{10... | collective-permute-start | bytes 786440 | tf_op jit(solution)/shard_map/ppermute | solution.py:270
  10.4 11.4 %collective-permute-start.2 = (bf16[1024,128]{1,0:T(8,128)(2,1)S(1)}, bf16[1024,128]{1,0:T(8,128)(2,1)S(1)}, u32[]{:S(2)}, u32[]{:S(2)}) collective-permute-start(bf16[1024,128]{1,0:T(8,128)(2,1)S(1)} %product_send.4), channel_id=1, source_target_pairs={{0,1},{1,0},{2,3},{3,2},{4,5},{5,4},{6,7},{7,6},{8,9},{9,8},{10,11... | collective-permute-start | bytes 786440 | tf_op jit(solution)/shard_map/ppermute | solution.py:270
  13.8 11.3 %collective-permute-start.4 = (bf16[1024,128]{1,0:T(8,128)(2,1)S(1)}, bf16[1024,128]{1,0:T(8,128)(2,1)S(1)}, u32[]{:S(2)}, u32[]{:S(2)}) collective-permute-start(bf16[1024,128]{1,0:T(8,128)(2,1)S(1)} %product_send.5), channel_id=1, source_target_pairs={{0,1},{1,0},{2,3},{3,2},{4,5},{5,4},{6,7},{7,6},{8,9},{9,8},{10,11... | collective-permute-start | bytes 786440 | tf_op jit(solution)/shard_map/ppermute | solution.py:270
  17.4 9.5 %collective-permute-start.10 = (bf16[512,256]{1,0:T(8,128)(2,1)S(1)}, bf16[512,256]{1,0:T(8,128)(2,1)S(1)}, u32[]{:S(2)}, u32[]{:S(2)}) collective-permute-start(bf16[512,256]{1,0:T(8,128)(2,1)S(1)} %product_send.7), channel_id=1, source_target_pairs={{0,2},{1,3},{2,0},{3,1},{4,6},{5,7},{6,4},{7,5},{8,10},{9,11},{10,... | collective-permute-start | bytes 786440 | tf_op jit(solution)/shard_map/ppermute | solution.py:270
  20.6 9.6 %collective-permute-start.7 = (bf16[512,256]{1,0:T(8,128)(2,1)S(1)}, bf16[512,256]{1,0:T(8,128)(2,1)S(1)}, u32[]{:S(2)}, u32[]{:S(2)}) collective-permute-start(bf16[512,256]{1,0:T(8,128)(2,1)S(1)} %product_send.6), channel_id=1, source_target_pairs={{0,1},{1,0},{2,3},{3,2},{4,5},{5,4},{6,7},{7,6},{8,9},{9,8},{10,11... | collective-permute-start | bytes 786440 | tf_op jit(solution)/shard_map/ppermute | solution.py:270
  25.2 21.4 %copy-start.1 = (bf16[128,256]{1,0:T(8,128)(2,1)S(1)}, bf16[128,256]{1,0:T(8,128)(2,1)}, u32[]{:S(2)}) copy-start(bf16[128,256]{1,0:T(8,128)(2,1)} %refs_6_.1) | copy-start | bytes 196612
  25.2 21.4 %copy-start.3 = (f32[256]{0:T(256)S(1)}, f32[256]{0:T(256)}, u32[]{:S(2)}) copy-start(f32[256]{0:T(256)} %param.11) | copy-start | bytes 3076
  25.3 11.9 %collective-permute-start.5 = (bf16[512,256]{1,0:T(8,128)(2,1)S(1)}, bf16[512,256]{1,0:T(8,128)(2,1)S(1)}, u32[]{:S(2)}, u32[]{:S(2)}) collective-permute-start(bf16[512,256]{1,0:T(8,128)(2,1)S(1)} %get-tuple-element.30), channel_id=1, source_target_pairs={{0,2},{1,3},{2,0},{3,1},{4,6},{5,7},{6,4},{7,5},{8,10},{9,11},{10,... | collective-permute-start | bytes 786440 | tf_op jit(solution)/shard_map/ppermute | solution.py:270
  26.9 12.1 %collective-permute-start.11 = (bf16[256,256]{1,0:T(8,128)(2,1)S(1)}, bf16[256,256]{1,0:T(8,128)(2,1)S(1)}, u32[]{:S(2)}, u32[]{:S(2)}) collective-permute-start(bf16[256,256]{1,0:T(8,128)(2,1)S(1)} %get-tuple-element.38), channel_id=1, source_target_pairs={{0,4},{1,5},{2,6},{3,7},{4,0},{5,1},{6,2},{7,3},{8,12},{9,13},{10,... | collective-permute-start | bytes 393224 | tf_op jit(solution)/shard_map/ppermute | solution.py:270
  30.2 10.2 %collective-permute-start.8 = (bf16[256,256]{1,0:T(8,128)(2,1)S(1)}, bf16[256,256]{1,0:T(8,128)(2,1)S(1)}, u32[]{:S(2)}, u32[]{:S(2)}) collective-permute-start(bf16[256,256]{1,0:T(8,128)(2,1)S(1)} %get-tuple-element.34), channel_id=1, source_target_pairs={{0,2},{1,3},{2,0},{3,1},{4,6},{5,7},{6,4},{7,5},{8,10},{9,11},{10,... | collective-permute-start | bytes 393224 | tf_op jit(solution)/shard_map/ppermute | solution.py:270
  37.2 9.4 %collective-permute-start.6 = (bf16[256,256]{1,0:T(8,128)(2,1)S(1)}, bf16[256,256]{1,0:T(8,128)(2,1)S(1)}, u32[]{:S(2)}, u32[]{:S(2)}) collective-permute-start(bf16[256,256]{1,0:T(8,128)(2,1)S(1)} %get-tuple-element.32), channel_id=1, source_target_pairs={{0,4},{1,5},{2,6},{3,7},{4,0},{5,1},{6,2},{7,3},{8,12},{9,13},{10,... | collective-permute-start | bytes 393224 | tf_op jit(solution)/shard_map/ppermute | solution.py:270
  39.0 4.3 %collective-permute-start.12 = (bf16[128,256]{1,0:T(8,128)(2,1)S(1)}, bf16[128,256]{1,0:T(8,128)(2,1)S(1)}, u32[]{:S(2)}, u32[]{:S(2)}) collective-permute-start(bf16[128,256]{1,0:T(8,128)(2,1)S(1)} %get-tuple-element.40), channel_id=1, source_target_pairs={{0,1},{1,0},{2,3},{3,2},{4,5},{5,4},{6,7},{7,6},{8,9},{9,8},{10,11... | collective-permute-start | bytes 196616 | tf_op jit(solution)/shard_map/ppermute | solution.py:270
  40.4 6.1 %collective-permute-start.9 = (bf16[128,256]{1,0:T(8,128)(2,1)S(1)}, bf16[128,256]{1,0:T(8,128)(2,1)S(1)}, u32[]{:S(2)}, u32[]{:S(2)}) collective-permute-start(bf16[128,256]{1,0:T(8,128)(2,1)S(1)} %get-tuple-element.36), channel_id=1, source_target_pairs={{0,4},{1,5},{2,6},{3,7},{4,0},{5,1},{6,2},{7,3},{8,12},{9,13},{10,... | collective-permute-start | bytes 196616 | tf_op jit(solution)/shard_map/ppermute | solution.py:270

commit v6 on v5

--- a/solution.py
+++ b/solution.py
@@ -276,7 +276,7 @@
     row_total = col_blocks * n_col // n_row
     per = row_total // n_col
 
-    z_first, x_first = tuple(col_axis_bits[1:] + col_axis_bits[:1]), tuple(col_axis_bits)
+    z_first, x_first = tuple(col_axis_bits[-1:] + col_axis_bits[:-1]), tuple(col_axis_bits)
     chunks = ((per // 2, x_first), (per // 4, x_first), (per // 4, z_first))
     halves = [size * n_col // 2 for size, _ in chunks]
 

time: 47.8 us -> 50.6 us (1.059); the launches traced: 47.8 us -> 51.2 us
  waiting for transfers between devices: 12.3 us -> 22.8 us
  starting transfers between devices: 22.6 us -> 15.3 us
    ppermute x13, waiting for transfers between devices: 12.3 us -> 22.8 us  [exchange(): return lax.ppermute(x, axis, [(i, i ^ 1 << bit) for i in range(size)])]
    ppermute x13, starting transfers between devices: 22.6 us -> 15.3 us  [exchange(): return lax.ppermute(x, axis, [(i, i ^ 1 << bit) for i in range(size)])]
  transfers between devices with their start and end apart: 13 -> 13, of which waited for: 6 -> 6; matrix products, arithmetic and copies ran while one was open for 0% -> 0% of each run, Pallas kernels for 21% -> 20%
where the time goes in v6:
time: 50.6 us; the launch traced here: 51.2 us
  waiting for transfers between devices  22.8 us (45%)
  starting transfers between devices  15.3 us (30%)
  Pallas kernels  11.6 us (23%)
  between operations  0.78 us (2%)
  local copies, waits for them, and re-layouts  0.69 us (1%)
    ppermute x13, waiting for transfers between devices, exchange(): return lax.ppermute(x, axis, [(i, i ^ 1 << bit) for i in range(size)])  22.8 us
    ppermute x13, starting transfers between devices, exchange(): return lax.ppermute(x, axis, [(i, i ^ 1 << bit) for i in range(size)])  15.3 us
    pallas_call x5, Pallas kernels, product(): pl.pallas_call(functools.partial(product_kernel, trash, group, len(tables...  5.36 us
    pallas_call x1, Pallas kernels, relayout(): pl.pallas_call(functools.partial(relayout_kernel, chunks, col_bits), in_s...  3.24 us
    pallas_call x2, Pallas kernels, make_table(): pl.pallas_call(table_kernel, in_specs=[VMEM] * len(parts), out_specs=VMEM...  1.49 us
    pallas_call x1, Pallas kernels, layer(): pl.pallas_call(functools.partial(layer_kernel, index), out_shape=jax.Shap...  1.18 us
  transfers between devices with their start and end apart: 13, of which 6 were waited for; matrix products, arithmetic and copies ran while one was open for 0% of the time, Pallas kernels for 20%

profile of v6, /device:TPU:0, one launch (start us, length us, event | category | flops | bytes accessed | tf_op | source)
XLA Modules:
  0.0 51.2 jit_solution(15503920167341073921)
XLA Ops:
  0.0 0.5 collective-permute-start.1
  0.5 2.6 %collective-permute-start = (bf16[32,4096]{1,0:T(8,128)(2,1)}, bf16[32,4096]{1,0:T(8,128)(2,1)S(1)}, u32[]{:S(2)}, u32[]{:S(2)}) collective-permute-start(bf16[32,4096]{1,0:T(8,128)(2,1)} %bitcast.4), channel_id=1, source_target_pairs={{0,16},{8,24},{16,0},{24,8},{1,17},{9,25},{17,1},{25,9},{2,18},{10... | collective-permute-start | bytes 786440 | tf_op jit(solution)/shard_map/ppermute | solution.py:270
  3.7 0.7 %copy-done.2 = s32[1,384]{1,0:T(1,128)S(1)} copy-done((s32[1,384]{1,0:T(1,128)S(1)}, s32[1,384]{1,0:T(1,128)}, u32[]{:S(2)}) %copy-start.2) | copy-done | bytes 1560
  4.4 3.2 %relayout.1 = (bf16[12288,128]{1,0:T(8,128)(2,1)S(1)}, s32[1,512]{1,0:T(1,128)S(1)}) custom-call(s32[1,1]{1,0:T(1,128)S(6)} %copy.7.count_ref, s32[1,384]{1,0:T(1,128)S(1)} %copy-done.2, bf16[384,4096]{1,0:T(8,128)(2,1)} %bitcast.7), custom_call_target="tpu_custom_call" | custom-call | bytes 6291456 | tf_op jit(solution)/shard_map/relayout/pallas_call | solution.py:99
  7.6 0.7 %table.2.refs_0_ = bf16[4096,128]{1,0:T(8,128)(2,1)S(1)} custom-call(bf16[32,4096]{1,0:T(8,128)(2,1)S(1)} %bitcast.5, bf16[32,4096]{1,0:T(8,128)(2,1)S(1)} %collective-permute-done.1.refs_1_), custom_call_target="tpu_custom_call" | custom-call | flops 1 | bytes 1 | tf_op jit(solution)/shard_map/table/pallas_call | solution.py:135
  8.4 1.0 %product_send.4 = bf16[1024,128]{1,0:T(8,128)(2,1)S(1)} custom-call(s32[1,512]{1,0:T(1,128)S(1)} %get-tuple-element.26.words_ref, bf16[12288,128]{1,0:T(8,128)(2,1)S(1)} %get-tuple-element.24.blocks_ref, bf16[4096,128]{1,0:T(8,128)(2,1)S(1)} %table.2.refs_0_), custom_call_target="tpu_custom_call" | custom-call | flops 1 | bytes 1 | tf_op jit(solution)/shard_map/product_send/pallas_call | solution.py:192
  9.4 0.8 %collective-permute-done.refs_0_ = bf16[32,4096]{1,0:T(8,128)(2,1)S(1)} collective-permute-done((bf16[32,4096]{1,0:T(8,128)(2,1)}, bf16[32,4096]{1,0:T(8,128)(2,1)S(1)}, u32[]{:S(2)}, u32[]{:S(2)}) %collective-permute-start) | collective-permute-done | bytes 262176 | tf_op jit(solution)/shard_map/ppermute | solution.py:270
  10.2 0.8 %collective-permute-start.3 = (bf16[32,4096]{1,0:T(8,128)(2,1)S(1)}, bf16[32,4096]{1,0:T(8,128)(2,1)S(1)}, u32[]{:S(2)}, u32[]{:S(2)}) collective-permute-start(bf16[32,4096]{1,0:T(8,128)(2,1)S(1)} %collective-permute-done.refs_0_), channel_id=1, source_target_pairs={{0,8},{8,0},{16,24},{24,16},{1,9},{9,1},{17,25},{25,17},{2,10},{10... | collective-permute-start | bytes 786440 | tf_op jit(solution)/shard_map/ppermute | solution.py:270
  10.9 1.5 %collective-permute-start.2 = (bf16[1024,128]{1,0:T(8,128)(2,1)S(1)}, bf16[1024,128]{1,0:T(8,128)(2,1)S(1)}, u32[]{:S(2)}, u32[]{:S(2)}) collective-permute-start(bf16[1024,128]{1,0:T(8,128)(2,1)S(1)} %product_send.4), channel_id=1, source_target_pairs={{0,1},{1,0},{2,3},{3,2},{4,5},{5,4},{6,7},{7,6},{8,9},{9,8},{10,11... | collective-permute-start | bytes 786440 | tf_op jit(solution)/shard_map/ppermute | solution.py:270
  12.4 0.7 %table.3.refs_1_.refs_0_ = bf16[4096,128]{1,0:T(8,128)(2,1)S(1)} custom-call(bf16[32,4096]{1,0:T(8,128)(2,1)S(1)} %collective-permute-done.refs_0_, bf16[32,4096]{1,0:T(8,128)(2,1)S(1)} %collective-permute-done.3.refs_1_), custom_call_target="tpu_custom_call" | custom-call | flops 1 | bytes 1 | tf_op jit(solution)/shard_map/table/pallas_call | solution.py:135
  13.2 1.0 %product_send.5 = bf16[1024,128]{1,0:T(8,128)(2,1)S(1)} custom-call(s32[1,512]{1,0:T(1,128)S(1)} %get-tuple-element.26.words_ref, bf16[12288,128]{1,0:T(8,128)(2,1)S(1)} %get-tuple-element.24.blocks_ref, bf16[4096,128]{1,0:T(8,128)(2,1)S(1)} %table.3.refs_1_.refs_0_), custom_call_target="tpu_custom_call" | custom-call | flops 1 | bytes 1 | tf_op jit(solution)/shard_map/product_send/pallas_call | solution.py:192
  14.1 2.3 %collective-permute-start.4 = (bf16[1024,128]{1,0:T(8,128)(2,1)S(1)}, bf16[1024,128]{1,0:T(8,128)(2,1)S(1)}, u32[]{:S(2)}, u32[]{:S(2)}) collective-permute-start(bf16[1024,128]{1,0:T(8,128)(2,1)S(1)} %product_send.5), channel_id=1, source_target_pairs={{0,1},{1,0},{2,3},{3,2},{4,5},{5,4},{6,7},{7,6},{8,9},{9,8},{10,11... | collective-permute-start | bytes 786440 | tf_op jit(solution)/shard_map/ppermute | solution.py:270
  16.4 1.0 %product_send.7 = bf16[512,256]{1,0:T(8,128)(2,1)S(1)} custom-call(s32[1,512]{1,0:T(1,128)S(1)} %get-tuple-element.26.words_ref, bf16[12288,128]{1,0:T(8,128)(2,1)S(1)} %get-tuple-element.24.blocks_ref, bf16[4096,128]{1,0:T(8,128)(2,1)S(1)} %table.2.refs_0_, bf16[4096,128]{1,0:T(8,128)(2,1)S(1)} %table.3.refs_1_.refs_0_), custom_call_target="tpu_custom_call" | custom-call | flops 1 | bytes 1 | tf_op jit(solution)/shard_map/product_send/pallas_call | solution.py:192
  17.5 1.9 %collective-permute-start.10 = (bf16[512,256]{1,0:T(8,128)(2,1)S(1)}, bf16[512,256]{1,0:T(8,128)(2,1)S(1)}, u32[]{:S(2)}, u32[]{:S(2)}) collective-permute-start(bf16[512,256]{1,0:T(8,128)(2,1)S(1)} %product_send.7), channel_id=1, source_target_pairs={{0,4},{1,5},{2,6},{3,7},{4,0},{5,1},{6,2},{7,3},{8,12},{9,13},{10,... | collective-permute-start | bytes 786440 | tf_op jit(solution)/shard_map/ppermute | solution.py:270
  19.4 1.0 %product_send.6 = bf16[512,256]{1,0:T(8,128)(2,1)S(1)} custom-call(s32[1,512]{1,0:T(1,128)S(1)} %get-tuple-element.26.words_ref, bf16[12288,128]{1,0:T(8,128)(2,1)S(1)} %get-tuple-element.24.blocks_ref, bf16[4096,128]{1,0:T(8,128)(2,1)S(1)} %table.2.refs_0_, bf16[4096,128]{1,0:T(8,128)(2,1)S(1)} %table.3.refs_1_.refs_0_), custom_call_target="tpu_custom_call" | custom-call | flops 1 | bytes 1 | tf_op jit(solution)/shard_map/product_send/pallas_call | solution.py:192
  20.4 0.9 %collective-permute-start.7 = (bf16[512,256]{1,0:T(8,128)(2,1)S(1)}, bf16[512,256]{1,0:T(8,128)(2,1)S(1)}, u32[]{:S(2)}, u32[]{:S(2)}) collective-permute-start(bf16[512,256]{1,0:T(8,128)(2,1)S(1)} %product_send.6), channel_id=1, source_target_pairs={{0,1},{1,0},{2,3},{3,2},{4,5},{5,4},{6,7},{7,6},{8,9},{9,8},{10,11... | collective-permute-start | bytes 786440 | tf_op jit(solution)/shard_map/ppermute | solution.py:270
  21.3 1.4 %product_keep.1.keep_ref = f32[2080,256]{1,0:T(8,128)S(1)} custom-call(s32[1,512]{1,0:T(1,128)S(1)} %get-tuple-element.26.words_ref, bf16[12288,128]{1,0:T(8,128)(2,1)S(1)} %get-tuple-element.24.blocks_ref, bf16[4096,128]{1,0:T(8,128)(2,1)S(1)} %table.2.refs_0_, bf16[4096,128]{1,0:T(8,128)(2,1)S(1)} %table.3.refs_1_.refs_0_), custom_call_target="tpu_custom_call" | custom-call | flops 1 | bytes 1 | tf_op jit(solution)/shard_map/product_keep/pallas_call | solution.py:192
  22.7 3.0 %collective-permute-done.4.refs_1_ = bf16[1024,128]{1,0:T(8,128)(2,1)S(1)} collective-permute-done((bf16[1024,128]{1,0:T(8,128)(2,1)S(1)}, bf16[1024,128]{1,0:T(8,128)(2,1)S(1)}, u32[]{:S(2)}, u32[]{:S(2)}) %collective-permute-start.4) | collective-permute-done | bytes 262176 | tf_op jit(solution)/shard_map/ppermute | solution.py:270
  25.7 0.1 add.6
  25.8 1.1 %collective-permute-start.5 = (bf16[512,256]{1,0:T(8,128)(2,1)S(1)}, bf16[512,256]{1,0:T(8,128)(2,1)S(1)}, u32[]{:S(2)}, u32[]{:S(2)}) collective-permute-start(bf16[512,256]{1,0:T(8,128)(2,1)S(1)} %get-tuple-element.30), channel_id=1, source_target_pairs={{0,2},{1,3},{2,0},{3,1},{4,6},{5,7},{6,4},{7,5},{8,10},{9,11},{10,... | collective-permute-start | bytes 786440 | tf_op jit(solution)/shard_map/ppermute | solution.py:270
  26.9 6.0 %collective-permute-done.10.refs_0_ = bf16[512,256]{1,0:T(8,128)(2,1)S(1)} collective-permute-done((bf16[512,256]{1,0:T(8,128)(2,1)S(1)}, bf16[512,256]{1,0:T(8,128)(2,1)S(1)}, u32[]{:S(2)}, u32[]{:S(2)}) %collective-permute-start.10) | collective-permute-done | bytes 262176 | tf_op jit(solution)/shard_map/ppermute | solution.py:270
  32.9 0.6 %collective-permute-start.11 = (bf16[256,256]{1,0:T(8,128)(2,1)S(1)}, bf16[256,256]{1,0:T(8,128)(2,1)S(1)}, u32[]{:S(2)}, u32[]{:S(2)}) collective-permute-start(bf16[256,256]{1,0:T(8,128)(2,1)S(1)} %get-tuple-element.38), channel_id=1, source_target_pairs={{0,1},{1,0},{2,3},{3,2},{4,5},{5,4},{6,7},{7,6},{8,9},{9,8},{10,11... | collective-permute-start | bytes 393224 | tf_op jit(solution)/shard_map/ppermute | solution.py:270
  33.5 0.1 add.8
  33.6 0.1 collective-permute-start.8
  33.7 4.8 %collective-permute-done.5.refs_0_ = bf16[512,256]{1,0:T(8,128)(2,1)S(1)} collective-permute-done((bf16[512,256]{1,0:T(8,128)(2,1)S(1)}, bf16[512,256]{1,0:T(8,128)(2,1)S(1)}, u32[]{:S(2)}, u32[]{:S(2)}) %collective-permute-start.5) | collective-permute-done | bytes 262176 | tf_op jit(solution)/shard_map/ppermute | solution.py:270
  38.5 0.1 add.7
  38.5 0.3 collective-permute-start.6
  38.9 2.5 %collective-permute-start.12 = (bf16[128,256]{1,0:T(8,128)(2,1)S(1)}, bf16[128,256]{1,0:T(8,128)(2,1)S(1)}, u32[]{:S(2)}, u32[]{:S(2)}) collective-permute-start(bf16[128,256]{1,0:T(8,128)(2,1)S(1)} %get-tuple-element.40), channel_id=1, source_target_pairs={{0,2},{1,3},{2,0},{3,1},{4,6},{5,7},{6,4},{7,5},{8,10},{9,11},{10,... | collective-permute-start | bytes 196616 | tf_op jit(solution)/shard_map/ppermute | solution.py:270
  41.5 0.3 collective-permute-start.9
  41.7 2.1 %collective-permute-done.12.refs_5_ = bf16[128,256]{1,0:T(8,128)(2,1)S(1)} collective-permute-done((bf16[128,256]{1,0:T(8,128)(2,1)S(1)}, bf16[128,256]{1,0:T(8,128)(2,1)S(1)}, u32[]{:S(2)}, u32[]{:S(2)}) %collective-permute-start.12) | collective-permute-done | bytes 65568 | tf_op jit(solution)/shard_map/ppermute | solution.py:270
  43.8 6.2 %collective-permute-done.9.refs_3_ = bf16[128,256]{1,0:T(8,128)(2,1)S(1)} collective-permute-done((bf16[128,256]{1,0:T(8,128)(2,1)S(1)}, bf16[128,256]{1,0:T(8,128)(2,1)S(1)}, u32[]{:S(2)}, u32[]{:S(2)}) %collective-permute-start.9) | collective-permute-done | bytes 65568 | tf_op jit(solution)/shard_map/ppermute | solution.py:270
  50.0 1.2 %layer.1 = bf16[1024,256]{1,0:T(8,128)(2,1)} custom-call(f32[256,256]{1,0:T(8,128)S(1)} %get-tuple-element.31.refs_0_, bf16[256,256]{1,0:T(8,128)(2,1)S(1)} %collective-permute-done.6.refs_1_, f32[128,256]{1,0:T(8,128)S(1)} %get-tuple-element.35.refs_2_, bf16[128,256]{1,0:T(8,128)(2,1)S(1)} %collective-permute-done.9.refs_3_, ...), custom_call_target="tpu_custom_call" | custom-call | tf_op jit(solution)/shard_map/layer/pallas_call | solution.py:260
  (17 shorter events, 0.1 us)
Async XLA Ops:
  0.0 7.6 %copy-start = (bf16[4096,32]{0,1:T(8,128)(2,1)S(1)}, bf16[4096,32]{0,1:T(8,128)(2,1)}, u32[]{:S(2)}) copy-start(bf16[4096,32]{0,1:T(8,128)(2,1)} %param.6) | copy-start | bytes 786436
  0.0 7.6 %collective-permute-start.1 = (bf16[32,4096]{1,0:T(8,128)(2,1)}, bf16[32,4096]{1,0:T(8,128)(2,1)S(1)}, u32[]{:S(2)}, u32[]{:S(2)}) collective-permute-start(bf16[32,4096]{1,0:T(8,128)(2,1)} %bitcast.3), channel_id=1, source_target_pairs={{0,8},{8,0},{16,24},{24,16},{1,9},{9,1},{17,25},{25,17},{2,10},{10... | collective-permute-start | bytes 786440 | tf_op jit(solution)/shard_map/ppermute | solution.py:270
  0.5 9.7 %collective-permute-start = (bf16[32,4096]{1,0:T(8,128)(2,1)}, bf16[32,4096]{1,0:T(8,128)(2,1)S(1)}, u32[]{:S(2)}, u32[]{:S(2)}) collective-permute-start(bf16[32,4096]{1,0:T(8,128)(2,1)} %bitcast.4), channel_id=1, source_target_pairs={{0,16},{8,24},{16,0},{24,8},{1,17},{9,25},{17,1},{25,9},{2,18},{10... | collective-permute-start | bytes 786440 | tf_op jit(solution)/shard_map/ppermute | solution.py:270
  3.7 0.7 %copy-start.2 = (s32[1,384]{1,0:T(1,128)S(1)}, s32[1,384]{1,0:T(1,128)}, u32[]{:S(2)}) copy-start(s32[1,384]{1,0:T(1,128)} %codes_hbm.1) | copy-start | bytes 4612
  10.2 2.2 %collective-permute-start.3 = (bf16[32,4096]{1,0:T(8,128)(2,1)S(1)}, bf16[32,4096]{1,0:T(8,128)(2,1)S(1)}, u32[]{:S(2)}, u32[]{:S(2)}) collective-permute-start(bf16[32,4096]{1,0:T(8,128)(2,1)S(1)} %collective-permute-done.refs_0_), channel_id=1, source_target_pairs={{0,8},{8,0},{16,24},{24,16},{1,9},{9,1},{17,25},{25,17},{2,10},{10... | collective-permute-start | bytes 786440 | tf_op jit(solution)/shard_map/ppermute | solution.py:270
  10.9 10.4 %collective-permute-start.2 = (bf16[1024,128]{1,0:T(8,128)(2,1)S(1)}, bf16[1024,128]{1,0:T(8,128)(2,1)S(1)}, u32[]{:S(2)}, u32[]{:S(2)}) collective-permute-start(bf16[1024,128]{1,0:T(8,128)(2,1)S(1)} %product_send.4), channel_id=1, source_target_pairs={{0,1},{1,0},{2,3},{3,2},{4,5},{5,4},{6,7},{7,6},{8,9},{9,8},{10,11... | collective-permute-start | bytes 786440 | tf_op jit(solution)/shard_map/ppermute | solution.py:270
  14.1 11.6 %collective-permute-start.4 = (bf16[1024,128]{1,0:T(8,128)(2,1)S(1)}, bf16[1024,128]{1,0:T(8,128)(2,1)S(1)}, u32[]{:S(2)}, u32[]{:S(2)}) collective-permute-start(bf16[1024,128]{1,0:T(8,128)(2,1)S(1)} %product_send.5), channel_id=1, source_target_pairs={{0,1},{1,0},{2,3},{3,2},{4,5},{5,4},{6,7},{7,6},{8,9},{9,8},{10,11... | collective-permute-start | bytes 786440 | tf_op jit(solution)/shard_map/ppermute | solution.py:270
  17.5 15.4 %collective-permute-start.10 = (bf16[512,256]{1,0:T(8,128)(2,1)S(1)}, bf16[512,256]{1,0:T(8,128)(2,1)S(1)}, u32[]{:S(2)}, u32[]{:S(2)}) collective-permute-start(bf16[512,256]{1,0:T(8,128)(2,1)S(1)} %product_send.7), channel_id=1, source_target_pairs={{0,4},{1,5},{2,6},{3,7},{4,0},{5,1},{6,2},{7,3},{8,12},{9,13},{10,... | collective-permute-start | bytes 786440 | tf_op jit(solution)/shard_map/ppermute | solution.py:270
  20.4 13.1 %collective-permute-start.7 = (bf16[512,256]{1,0:T(8,128)(2,1)S(1)}, bf16[512,256]{1,0:T(8,128)(2,1)S(1)}, u32[]{:S(2)}, u32[]{:S(2)}) collective-permute-start(bf16[512,256]{1,0:T(8,128)(2,1)S(1)} %product_send.6), channel_id=1, source_target_pairs={{0,1},{1,0},{2,3},{3,2},{4,5},{5,4},{6,7},{7,6},{8,9},{9,8},{10,11... | collective-permute-start | bytes 786440 | tf_op jit(solution)/shard_map/ppermute | solution.py:270
  25.8 24.2 %copy-start.1 = (bf16[128,256]{1,0:T(8,128)(2,1)S(1)}, bf16[128,256]{1,0:T(8,128)(2,1)}, u32[]{:S(2)}) copy-start(bf16[128,256]{1,0:T(8,128)(2,1)} %refs_6_.1) | copy-start | bytes 196612
  25.8 24.2 %copy-start.3 = (f32[256]{0:T(256)S(1)}, f32[256]{0:T(256)}, u32[]{:S(2)}) copy-start(f32[256]{0:T(256)} %param.11) | copy-start | bytes 3076
  25.8 12.6 %collective-permute-start.5 = (bf16[512,256]{1,0:T(8,128)(2,1)S(1)}, bf16[512,256]{1,0:T(8,128)(2,1)S(1)}, u32[]{:S(2)}, u32[]{:S(2)}) collective-permute-start(bf16[512,256]{1,0:T(8,128)(2,1)S(1)} %get-tuple-element.30), channel_id=1, source_target_pairs={{0,2},{1,3},{2,0},{3,1},{4,6},{5,7},{6,4},{7,5},{8,10},{9,11},{10,... | collective-permute-start | bytes 786440 | tf_op jit(solution)/shard_map/ppermute | solution.py:270
  32.9 6.0 %collective-permute-start.11 = (bf16[256,256]{1,0:T(8,128)(2,1)S(1)}, bf16[256,256]{1,0:T(8,128)(2,1)S(1)}, u32[]{:S(2)}, u32[]{:S(2)}) collective-permute-start(bf16[256,256]{1,0:T(8,128)(2,1)S(1)} %get-tuple-element.38), channel_id=1, source_target_pairs={{0,1},{1,0},{2,3},{3,2},{4,5},{5,4},{6,7},{7,6},{8,9},{9,8},{10,11... | collective-permute-start | bytes 393224 | tf_op jit(solution)/shard_map/ppermute | solution.py:270
  33.6 7.9 %collective-permute-start.8 = (bf16[256,256]{1,0:T(8,128)(2,1)S(1)}, bf16[256,256]{1,0:T(8,128)(2,1)S(1)}, u32[]{:S(2)}, u32[]{:S(2)}) collective-permute-start(bf16[256,256]{1,0:T(8,128)(2,1)S(1)} %get-tuple-element.34), channel_id=1, source_target_pairs={{0,2},{1,3},{2,0},{3,1},{4,6},{5,7},{6,4},{7,5},{8,10},{9,11},{10,... | collective-permute-start | bytes 393224 | tf_op jit(solution)/shard_map/ppermute | solution.py:270
  38.5 11.5 %collective-permute-start.6 = (bf16[256,256]{1,0:T(8,128)(2,1)S(1)}, bf16[256,256]{1,0:T(8,128)(2,1)S(1)}, u32[]{:S(2)}, u32[]{:S(2)}) collective-permute-start(bf16[256,256]{1,0:T(8,128)(2,1)S(1)} %get-tuple-element.32), channel_id=1, source_target_pairs={{0,4},{1,5},{2,6},{3,7},{4,0},{5,1},{6,2},{7,3},{8,12},{9,13},{10,... | collective-permute-start | bytes 393224 | tf_op jit(solution)/shard_map/ppermute | solution.py:270
  38.9 4.9 %collective-permute-start.12 = (bf16[128,256]{1,0:T(8,128)(2,1)S(1)}, bf16[128,256]{1,0:T(8,128)(2,1)S(1)}, u32[]{:S(2)}, u32[]{:S(2)}) collective-permute-start(bf16[128,256]{1,0:T(8,128)(2,1)S(1)} %get-tuple-element.40), channel_id=1, source_target_pairs={{0,2},{1,3},{2,0},{3,1},{4,6},{5,7},{6,4},{7,5},{8,10},{9,11},{10,... | collective-permute-start | bytes 196616 | tf_op jit(solution)/shard_map/ppermute | solution.py:270
  41.5 8.5 %collective-permute-start.9 = (bf16[128,256]{1,0:T(8,128)(2,1)S(1)}, bf16[128,256]{1,0:T(8,128)(2,1)S(1)}, u32[]{:S(2)}, u32[]{:S(2)}) collective-permute-start(bf16[128,256]{1,0:T(8,128)(2,1)S(1)} %get-tuple-element.36), channel_id=1, source_target_pairs={{0,4},{1,5},{2,6},{3,7},{4,0},{5,1},{6,2},{7,3},{8,12},{9,13},{10,... | collective-permute-start | bytes 196616 | tf_op jit(solution)/shard_map/ppermute | solution.py:270
